TPU v7x, 32 devices: a whole 2x2x4 slice. The times are simulated.
32 devices in a mesh: outer: 4 (over y, x), inner: 8 (over z, core).
Axes of the slice: x: 2, y: 2, z: 4, core: 2. Of those that a mesh axis runs over, the one named last changes fastest.
Arguments:
- vectors: bfloat16 [65536, 256], P(('outer', 'inner')), may hold values from -6 to 6
- leaf_basis: bfloat16 [65536, 256], P(('outer', 'inner')), may hold values from -0.375 to 0.375
- transfer: bfloat16 [4, 4, 8, 8, 512, 256], P(None, 'outer', 'inner'), may hold values from -0.25 to 0.25
- core_mats: bfloat16 [4, 8, 8, 256, 256], P('outer', 'inner'), may hold values from -0.375 to 0.375
- row_basis: bfloat16 [65536, 256], P(('outer', 'inner')), may hold values from -0.375 to 0.375
- box_order: int32 [4, 8, 8], P('outer', 'inner'), may hold values from 0 to 7, each once within a row
Outputs:
- applied: bfloat16 [65536, 256], P(('outer', 'inner'))
Inputs may be any that keep to these rules, and one draw needn't show every extreme that they name: `box_order`: for every device the 8 entries are a permutation of 0 to 7.
All inputs are finite; a program needn't handle non-finite values.
Results may differ from a plain program's by a relative error of at most 0.011.
Values may be sent and summed in bfloat16 or wider, within the bound.
No kernel may reach another device: no remote copies, remote signals or barrier semaphores. Data moves between devices by JAX's collectives and lax.ppermute only.
A program may use at most 64 MiB of HBM per device.

v0:
```python
import jax
import jax.numpy as jnp
from jax import lax
from jax.sharding import PartitionSpec as P

LEVELS = 4


def swapped(array, axis, apart):
    return lax.ppermute(array, axis, [(i, i ^ 1 << apart) for i in range(lax.axis_size(axis))])


def split_half(box_state, half_flag):
    half_count = box_state.shape[0] // 2
    kept_half = lax.dynamic_slice_in_dim(box_state, half_flag * half_count, half_count, 0)
    sent_half = lax.dynamic_slice_in_dim(box_state, (1 - half_flag) * half_count, half_count, 0)
    return (kept_half, sent_half)


def merge_level(kept_half, received, half_flag, level_w):
    half_count = kept_half.shape[0]
    columns = kept_half.shape[1]
    rank_dim = kept_half.shape[2]
    paired_w = level_w.reshape(half_count, 2, 2 * rank_dim, rank_dim)
    low_part = jnp.where(half_flag == 0, kept_half, received)
    high_part = jnp.where(half_flag == 0, received, kept_half)
    stacked = jnp.concatenate([low_part, high_part], axis=2)
    merged = jnp.einsum("kcs,kosr->kocr", stacked, paired_w, preferred_element_type=jnp.float32)
    return merged.reshape(2 * half_count, columns, rank_dim).astype(jnp.bfloat16)


def on_device(vectors, leaf_basis, transfer, core_mats, row_basis, box_order):
    box_count = transfer.shape[3]
    rank_dim = leaf_basis.shape[1]
    columns = vectors.shape[1]
    leaf_rows = vectors.shape[0] // box_count
    local_x = vectors.reshape(box_count, leaf_rows, columns)
    local_v = leaf_basis.reshape(box_count, leaf_rows, rank_dim)
    box_state = jnp.einsum(
        "klc,klr->kcr", local_x, local_v, preferred_element_type=jnp.float32
    ).astype(jnp.bfloat16)
    weights = transfer.reshape(transfer.shape[0], box_count, 2 * rank_dim, rank_dim)
    for level_idx in range(LEVELS):
        if level_idx < 2:
            bit_pos = level_idx
            half_flag = jnp.bitwise_and(jnp.right_shift(lax.axis_index("inner"), bit_pos), 1)
            kept_half, sent_half = split_half(box_state, half_flag)
            received = swapped(sent_half, "inner", bit_pos)
        else:
            bit_pos = level_idx - 2
            half_flag = jnp.bitwise_and(jnp.right_shift(lax.axis_index("outer"), bit_pos), 1)
            kept_half, sent_half = split_half(box_state, half_flag)
            received = swapped(sent_half, "outer", bit_pos)
        box_state = merge_level(kept_half, received, half_flag, weights[level_idx])
    slot_order = box_order.reshape(box_count)
    chosen = jnp.take(box_state, slot_order, axis=0)
    cores = core_mats.reshape(box_count, rank_dim, rank_dim)
    core_out = jnp.einsum("kcs,ksr->kcr", chosen, cores, preferred_element_type=jnp.float32).astype(
        jnp.bfloat16
    )
    inner_count = lax.axis_size("inner")
    local_u = row_basis.reshape(box_count, leaf_rows, rank_dim)
    row_out = jnp.einsum(
        "klr,kcr->klc", local_u, core_out, preferred_element_type=jnp.float32
    ).astype(jnp.bfloat16)
    pieces = row_out.reshape(inner_count, -1, columns)
    arrived = lax.all_to_all(pieces, "inner", split_axis=0, concat_axis=0, tiled=True)
    return arrived.reshape(box_count * leaf_rows, columns)


def solution(mesh):
    in_specs = (
        P(("outer", "inner"), None),
        P(("outer", "inner"), None),
        P(None, "outer", "inner", None, None, None),
        P("outer", "inner", None, None, None),
        P(("outer", "inner"), None),
        P("outer", "inner", None),
    )
    out_specs = P(("outer", "inner"), None)
    return jax.shard_map(
        on_device, mesh=mesh, in_specs=in_specs, out_specs=out_specs, check_vma=False
    )
```

profile of v0, /device:TPU:0, one launch (start us, length us, event | category | flops | bytes accessed | tf_op | source)
XLA Modules:
  0.0 92.3 jit_solution(15666571901531021347)
XLA Ops:
  0.0 0.0 copy-start
  0.0 1.2 %copy-done = bf16[2048,256]{1,0:T(8,128)(2,1)S(1)} copy-done((bf16[2048,256]{1,0:T(8,128)(2,1)S(1)}, bf16[2048,256]{1,0:T(8,128)(2,1)}, u32[]{:S(2)}) %copy-start) | copy-done | bytes 1048600
  1.2 1.7 %convolution_convert_fusion.6 = bf16[8,256,256]{1,2,0:T(8,128)(2,1)S(1)} fusion(bf16[8,256,256]{2,1,0:T(8,128)(2,1)S(1)} %bitcast.62, bf16[8,256,256]{2,1,0:T(8,128)(2,1)} %bitcast.67), kind=kOutput, calls=%fused_computation.7 | convolution fusion | flops 268959744 | bytes 3145728 | tf_op jit(solution)/shard_map/klc,klr->kcr/dot_general | solution.py:39
  3.0 0.5 collective-permute-start
  3.5 5.7 %fusion.24 = (bf16[1,1,1,8,512,256]{5,4,3,2,1,0:T(8,128)(2,1)S(1)}, bf16[1,1,1,8,512,256]{5,4,3,2,1,0:T(8,128)(2,1)}, bf16[1,1,1,8,512,256]{5,4,3,2,1,0:T(8,128)(2,1)}, bf16[1,1,1,8,512,256]{5,4,3,2,1,0:T(8,128)(2,1)}) fusion(bf16[4,1,1,8,512,256]{5,4,3,2,1,0:T(8,128)(2,1)} %param.8), kind=kLoop, calls=%fused_computation.50 | loop fusion | bytes 16777216 | tf_op jit(solution)/shard_map/slice | solution.py:54
  9.2 0.0 collective-permute-done
  9.2 0.1 broadcast_select_fusion.1
  9.3 0.9 convolution_convert_fusion.5
  10.2 0.1 constant_dynamic-slice_fusion.5
  10.3 0.2 copy.38
  10.5 2.7 %collective-permute-start.1 = (bf16[4,256,256]{2,1,0:T(8,128)(2,1)S(1)}, bf16[4,256,256]{2,1,0:T(8,128)(2,1)S(1)}, u32[]{:S(2)}, u32[]{:S(2)}) collective-permute-start(bf16[4,256,256]{2,1,0:T(8,128)(2,1)S(1)} %copy.38), channel_id=1, source_target_pairs={{0,2},{1,3},{2,0},{3,1},{4,6},{5,7},{6,4},{7,5},{8,10},{9,11},{10,... | collective-permute-start | bytes 1572872 | tf_op jit(solution)/shard_map/ppermute | solution.py:10
  13.1 0.2 copy.37
  13.4 0.0 copy-start.3
  13.4 12.3 %collective-permute-done.1 = bf16[4,256,256]{2,1,0:T(8,128)(2,1)S(1)} collective-permute-done((bf16[4,256,256]{2,1,0:T(8,128)(2,1)S(1)}, bf16[4,256,256]{2,1,0:T(8,128)(2,1)S(1)}, u32[]{:S(2)}, u32[]{:S(2)}) %collective-permute-start.1) | collective-permute-done | bytes 524320 | tf_op jit(solution)/shard_map/ppermute | solution.py:10
  25.7 0.1 broadcast_select_fusion.3
  25.8 0.0 copy-done.3
  25.8 0.9 %convolution_convert_fusion.4 = bf16[4,256,2,256]{1,3,2,0:T(8,128)(2,1)S(1)} fusion(bf16[4,2,512,256]{3,2,1,0:T(8,128)(2,1)S(1)} %bitcast.65, bf16[4,256,256]{2,1,0:T(8,128)(2,1)S(1)} %get-tuple-element.20, bf16[4,256,256]{2,1,0:T(8,128)(2,1)S(1)} %get-tuple-element.19), kind=kOutput, calls=%fused_computation.5 | convolution fusion | flops 539492352 | bytes 4194304 | tf_op jit(solution)/shard_map/kcs,kosr->kocr/dot_general | solution.py:28
  26.7 0.1 constant_dynamic-slice_fusion.3
  26.8 0.2 copy.40
  27.0 1.7 %collective-permute-start.2 = (bf16[4,256,256]{2,1,0:T(8,128)(2,1)S(1)}, bf16[4,256,256]{2,1,0:T(8,128)(2,1)S(1)}, u32[]{:S(2)}, u32[]{:S(2)}) collective-permute-start(bf16[4,256,256]{2,1,0:T(8,128)(2,1)S(1)} %copy.40), channel_id=1, source_target_pairs={{0,8},{8,0},{16,24},{24,16},{1,9},{9,1},{17,25},{25,17},{2,10},{10... | collective-permute-start | bytes 1572872 | tf_op jit(solution)/shard_map/ppermute | solution.py:10
  28.7 0.2 copy.39
  28.9 0.0 copy-start.2
  29.0 11.9 %collective-permute-done.2 = bf16[4,256,256]{2,1,0:T(8,128)(2,1)S(1)} collective-permute-done((bf16[4,256,256]{2,1,0:T(8,128)(2,1)S(1)}, bf16[4,256,256]{2,1,0:T(8,128)(2,1)S(1)}, u32[]{:S(2)}, u32[]{:S(2)}) %collective-permute-start.2) | collective-permute-done | bytes 524320 | tf_op jit(solution)/shard_map/ppermute | solution.py:10
  40.8 0.1 broadcast_select_fusion.5
  40.9 0.0 copy-done.2
  40.9 0.9 %convolution_convert_fusion.3 = bf16[4,256,2,256]{1,3,2,0:T(8,128)(2,1)S(1)} fusion(bf16[4,2,512,256]{3,2,1,0:T(8,128)(2,1)S(1)} %bitcast.64, bf16[4,256,256]{2,1,0:T(8,128)(2,1)S(1)} %get-tuple-element.16, bf16[4,256,256]{2,1,0:T(8,128)(2,1)S(1)} %get-tuple-element.15), kind=kOutput, calls=%fused_computation.4 | convolution fusion | flops 539492352 | bytes 4194304 | tf_op jit(solution)/shard_map/kcs,kosr->kocr/dot_general | solution.py:28
  41.8 0.0 copy-start.4
  41.8 0.1 constant_dynamic-slice_fusion.1
  41.9 0.2 copy.42
  42.1 1.5 %collective-permute-start.3 = (bf16[4,256,256]{2,1,0:T(8,128)(2,1)S(1)}, bf16[4,256,256]{2,1,0:T(8,128)(2,1)S(1)}, u32[]{:S(2)}, u32[]{:S(2)}) collective-permute-start(bf16[4,256,256]{2,1,0:T(8,128)(2,1)S(1)} %copy.42), channel_id=1, source_target_pairs={{0,16},{8,24},{16,0},{24,8},{1,17},{9,25},{17,1},{25,9},{2,18},{10... | collective-permute-start | bytes 1572872 | tf_op jit(solution)/shard_map/ppermute | solution.py:10
  43.7 0.0 copy-done.4
  43.7 0.2 copy.41
  43.9 0.0 copy-start.1
  43.9 11.1 %collective-permute-done.3 = bf16[4,256,256]{2,1,0:T(8,128)(2,1)S(1)} collective-permute-done((bf16[4,256,256]{2,1,0:T(8,128)(2,1)S(1)}, bf16[4,256,256]{2,1,0:T(8,128)(2,1)S(1)}, u32[]{:S(2)}, u32[]{:S(2)}) %collective-permute-start.3) | collective-permute-done | bytes 524320 | tf_op jit(solution)/shard_map/ppermute | solution.py:10
  55.1 0.1 broadcast_select_fusion.7
  55.1 0.0 copy-done.1
  55.1 0.7 convolution_convert_fusion.2
  55.9 0.6 gather_fusion
  56.5 3.3 %fusion = bf16[8,256,256]{1,2,0:T(8,128)(2,1)} fusion(bf16[8,256,256]{2,1,0:T(8,128)(2,1)} %bitcast.72, bf16[1,1,8,256,256]{4,3,2,1,0:T(8,128)(2,1)} %param.9, bf16[8,256,256]{2,1,0:T(8,128)(2,1)S(1)} %gather_fusion, pred[8]{0:T(512)(128)(4,1)S(1)} %compare_and_fusion), kind=kOutput, calls=%fused_computation.8 | convolution fusion | flops 538443776 | bytes 4194312 | tf_op jit(solution)/shard_map/klr,kcr->klc/dot_general | solution.py:63
  59.8 31.2 %all_to_all.5 = bf16[8,256,256]{1,2,0:T(8,128)(2,1)S(1)} all-to-all(bf16[8,256,256]{1,2,0:T(8,128)(2,1)} %fusion), channel_id=1, replica_groups=mesh['outer'=4,'inner'=8] {'inner'}, dimensions={0} | all-to-all | bytes 2097152 | tf_op jit(solution)/shard_map/all_to_all | solution.py:67
  91.0 1.3 %copy.29 = bf16[8,256,256]{2,1,0:T(8,128)(2,1)} copy(bf16[8,256,256]{1,2,0:T(8,128)(2,1)S(1)} %all_to_all.5) | data formatting | bytes 2097152 | tf_op jit(solution)/shard_map/all_to_all | solution.py:67
  (4 shorter events, 0.1 us)
Async XLA Ops:
  0.0 1.2 %copy-start = (bf16[2048,256]{1,0:T(8,128)(2,1)S(1)}, bf16[2048,256]{1,0:T(8,128)(2,1)}, u32[]{:S(2)}) copy-start(bf16[2048,256]{1,0:T(8,128)(2,1)} %param.6) | copy-start | bytes 3145732
  3.0 6.2 %collective-permute-start = (bf16[4,256,256]{1,2,0:T(8,128)(2,1)S(1)}, bf16[4,256,256]{1,2,0:T(8,128)(2,1)S(1)}, u32[]{:S(2)}, u32[]{:S(2)}) collective-permute-start(bf16[4,256,256]{1,2,0:T(8,128)(2,1)S(1)} %constant_dynamic-slice_fusion.6), channel_id=1, source_target_pairs={{0,1},{1,0},{2,3},{3,2},{4,5},{5,4},{6,7},{7,6},{8,9},{9,8},{10,11... | collective-permute-start | bytes 1572872 | tf_op jit(solution)/shard_map/ppermute | solution.py:10
  10.5 15.2 %collective-permute-start.1 = (bf16[4,256,256]{2,1,0:T(8,128)(2,1)S(1)}, bf16[4,256,256]{2,1,0:T(8,128)(2,1)S(1)}, u32[]{:S(2)}, u32[]{:S(2)}) collective-permute-start(bf16[4,256,256]{2,1,0:T(8,128)(2,1)S(1)} %copy.38), channel_id=1, source_target_pairs={{0,2},{1,3},{2,0},{3,1},{4,6},{5,7},{6,4},{7,5},{8,10},{9,11},{10,... | collective-permute-start | bytes 1572872 | tf_op jit(solution)/shard_map/ppermute | solution.py:10
  13.4 12.4 %copy-start.3 = (bf16[1,1,1,8,512,256]{5,4,3,2,1,0:T(8,128)(2,1)S(1)}, bf16[1,1,1,8,512,256]{5,4,3,2,1,0:T(8,128)(2,1)}, u32[]{:S(2)}) copy-start(bf16[1,1,1,8,512,256]{5,4,3,2,1,0:T(8,128)(2,1)} %get-tuple-element.6) | copy-start | bytes 6291460
  27.0 13.8 %collective-permute-start.2 = (bf16[4,256,256]{2,1,0:T(8,128)(2,1)S(1)}, bf16[4,256,256]{2,1,0:T(8,128)(2,1)S(1)}, u32[]{:S(2)}, u32[]{:S(2)}) collective-permute-start(bf16[4,256,256]{2,1,0:T(8,128)(2,1)S(1)} %copy.40), channel_id=1, source_target_pairs={{0,8},{8,0},{16,24},{24,16},{1,9},{9,1},{17,25},{25,17},{2,10},{10... | collective-permute-start | bytes 1572872 | tf_op jit(solution)/shard_map/ppermute | solution.py:10
  28.9 11.9 %copy-start.2 = (bf16[1,1,1,8,512,256]{5,4,3,2,1,0:T(8,128)(2,1)S(1)}, bf16[1,1,1,8,512,256]{5,4,3,2,1,0:T(8,128)(2,1)}, u32[]{:S(2)}) copy-start(bf16[1,1,1,8,512,256]{5,4,3,2,1,0:T(8,128)(2,1)} %get-tuple-element.8) | copy-start | bytes 6291460
  41.8 1.8 %copy-start.4 = (s32[1,1,8]{2,1,0:T(1,128)S(1)}, s32[1,1,8]{2,1,0:T(1,128)}, u32[]{:S(2)}) copy-start(s32[1,1,8]{2,1,0:T(1,128)} %param.11) | copy-start | bytes 100
  42.1 12.9 %collective-permute-start.3 = (bf16[4,256,256]{2,1,0:T(8,128)(2,1)S(1)}, bf16[4,256,256]{2,1,0:T(8,128)(2,1)S(1)}, u32[]{:S(2)}, u32[]{:S(2)}) collective-permute-start(bf16[4,256,256]{2,1,0:T(8,128)(2,1)S(1)} %copy.42), channel_id=1, source_target_pairs={{0,16},{8,24},{16,0},{24,8},{1,17},{9,25},{17,1},{25,9},{2,18},{10... | collective-permute-start | bytes 1572872 | tf_op jit(solution)/shard_map/ppermute | solution.py:10
  43.9 11.2 %copy-start.1 = (bf16[1,1,1,8,512,256]{5,4,3,2,1,0:T(8,128)(2,1)S(1)}, bf16[1,1,1,8,512,256]{5,4,3,2,1,0:T(8,128)(2,1)}, u32[]{:S(2)}) copy-start(bf16[1,1,1,8,512,256]{5,4,3,2,1,0:T(8,128)(2,1)} %get-tuple-element.7) | copy-start | bytes 6291460
where the time goes:
time: 92.5 us; the launch traced here: 92.3 us
  waiting for transfers between devices  35.3 us (38%)
  blocking collectives  31.2 us (34%)
  local copies, waits for them, and re-layouts  10.3 us (11%)
  matrix products  8.48 us (9%)
  starting transfers between devices  6.45 us (7%)
    ppermute x4, waiting for transfers between devices, swapped(): lax.ppermute(array, axis, [(i, i ^ 1 << apart) for i in range(lax.axis_si...  35.3 us
    all_to_all x1, blocking collectives, on_device(): lax.all_to_all(pieces, 'inner', split_axis=0, concat_axis=0, tiled=True)  31.2 us
    ppermute x4, starting transfers between devices, swapped(): lax.ppermute(array, axis, [(i, i ^ 1 << apart) for i in range(lax.axis_si...  6.45 us
    slice x1, local copies, waits for them, and re-layouts, on_device(): box_state = merge_level(kept_half, received, half_flag, weights[level_idx])  5.66 us
    dot_general x4, matrix products, merge_level(): jnp.einsum('kcs,kosr->kocr', stacked, paired_w, preferred_element_type=jn...  3.47 us
    dot_general x1, matrix products, on_device(): jnp.einsum('klr,kcr->klc', local_u, core_out, preferred_element_type=jnp....  3.29 us
    unnamed x16, local copies, waits for them, and re-layouts  2.46 us
  transfers between devices with their start and end apart: 4, of which 3 were waited for; matrix products, arithmetic and copies ran while one was open for 7% of the time, Pallas kernels for 0%

commit v1 on v0

v1 whole, which is shorter than its diff:
```python
import functools

import jax
import jax.numpy as jnp
from jax import lax
from jax.experimental import pallas as pl
from jax.experimental.pallas import tpu as pltpu
from jax.sharding import PartitionSpec as P

INNER_LEVELS = 2
PARTS = (4, 5, 7)
VMEM = pl.BlockSpec(memory_space=pltpu.VMEM)
ANY = pl.BlockSpec(memory_space=pl.ANY)
SMEM = pl.BlockSpec(memory_space=pltpu.SMEM)


def swapped(array, axis, step):
    return lax.ppermute(array, axis, [(i, i ^ step) for i in range(lax.axis_size(axis))])


def level_axis(level):
    return ("inner", level) if level < INNER_LEVELS else ("outer", level - INNER_LEVELS)


def bit_of(level):
    axis, bit = level_axis(level)
    return jnp.bitwise_and(jnp.right_shift(lax.axis_index(axis), bit), 1)


def dot(a, b, dims):
    return lax.dot_general(a, b, (dims, ((), ())), preferred_element_type=jnp.float32).astype(
        jnp.bfloat16
    )


def call(kernel, outs, ins, specs, flops, scratch=()):
    moved = sum(x.size * x.dtype.itemsize for x in list(ins) + list(outs))
    return pl.pallas_call(
        kernel,
        out_shape=outs,
        in_specs=specs,
        out_specs=[VMEM] * len(outs),
        scratch_shapes=list(scratch),
        compiler_params=pltpu.CompilerParams(vmem_limit_bytes=32 * 1024 * 1024),
        cost_estimate=pl.CostEstimate(flops=flops, bytes_accessed=moved, transcendentals=0),
    )(*ins)


def leaf_kernel(cuts, x_ref, v_ref, *outs):
    half = outs[0].shape[0]
    flag = bit_of(0)
    rows = x_ref.shape[0] // (2 * half)
    for slot in range(2 * half):
        side = 1 - flag if slot < half else flag
        box = side * half + slot % half
        window = pl.ds(pl.multiple_of(box * rows, rows), rows)
        state = dot(x_ref[window, :].T, v_ref[window, :], ((1,), (0,)))
        for n, (begin, size) in enumerate(cuts):
            outs[2 * n + (slot >= half)][slot % half] = state[begin : begin + size]


def merge_box(level, kept_ref, got_ref, w_ref, begin, size, k, o):
    rank = kept_ref.shape[2]
    flag = bit_of(level)
    mine = w_ref[level, 0, 0, 2 * k + o, pl.ds(pl.multiple_of(flag * rank, rank), rank), :]
    other = w_ref[level, 0, 0, 2 * k + o, pl.ds(pl.multiple_of((1 - flag) * rank, rank), rank), :]
    dims = (((1,), (0,)), ((), ()))
    total = lax.dot_general(
        kept_ref[k, begin : begin + size], mine, dims, preferred_element_type=jnp.float32
    )
    total += lax.dot_general(
        got_ref[k, begin : begin + size], other, dims, preferred_element_type=jnp.float32
    )
    return total.astype(jnp.bfloat16)


def merge_kernel(level, begin, size, kept_ref, got_ref, w_ref, after_ref, sent_out, kept_out):
    half = kept_ref.shape[0]
    flag = bit_of(level + 1)
    for slot in range(2 * half):
        side = 1 - flag if slot < half else flag
        box = side * half + slot % half
        out = sent_out if slot < half else kept_out
        k = box // 2
        out[slot % half] = merge_box(level, kept_ref, got_ref, w_ref, begin, size, k, slot % 2)


def last_kernel(
    level, begin, size, order_ref, kept_ref, got_ref, w_ref, core_ref, u_ref, after_ref,
    cross_out, mine_out, state, cored,
):
    half = kept_ref.shape[0]
    pieces = 2 * cross_out.shape[0]
    leaf_rows = u_ref.shape[0] // (2 * half)
    rows = u_ref.shape[0] // pieces
    me = lax.axis_index("inner")
    for box in range(2 * half):
        state[box] = merge_box(level, kept_ref, got_ref, w_ref, begin, size, box // 2, box % 2)
    for box in range(2 * half):
        cored[box] = dot(state[order_ref[0, 0, box]], core_ref[0, 0, box], ((1,), (0,)))
    width = min(rows, leaf_rows)
    for t in range(pieces // 2):
        for out, step in ((cross_out, 2 * t + 1), (mine_out, 2 * t)):
            first = jnp.bitwise_xor(me, step) * rows
            for at in range(0, rows, width):
                row = pl.multiple_of(first + at, width)
                out[t, :, at : at + width] = dot(
                    cored[row // leaf_rows], u_ref[pl.ds(row, width), :], ((1,), (1,))
                )


def pack_kernel(got_ref, mine_ref, *outs):
    for t, out in enumerate(outs, 1):
        out[0] = mine_ref[t]
        out[1] = got_ref[t]


def place_kernel(cuts, *refs):
    out, ins = refs[-1], refs[:-1]
    me = lax.axis_index("inner")
    per = len(ins) // len(cuts)
    for n, (begin, size) in enumerate(cuts):
        got_ref, mine_ref, *others = ins[n * per : (n + 1) * per]
        rows = mine_ref.shape[2]
        for t in range(per - 1):
            for odd in range(2):
                if t == 0:
                    block = (got_ref if odd else mine_ref)[0]
                else:
                    block = others[t - 1][odd]
                owner = jnp.bitwise_xor(me, 2 * t + odd)
                window = pl.ds(pl.multiple_of(owner * rows, rows), rows)
                out[window, begin : begin + size] = block.T


def on_device(vectors, leaf_basis, transfer, core_mats, row_basis, box_order):
    boxes = transfer.shape[3]
    half = boxes // 2
    rank = leaf_basis.shape[1]
    columns = vectors.shape[1]
    levels = transfer.shape[0]
    inner = lax.axis_size("inner")
    piece = vectors.shape[0] // inner
    edges = [columns * sum(PARTS[:n]) // sum(PARTS) for n in range(len(PARTS) + 1)]
    cuts = [(a, b - a) for a, b in zip(edges, edges[1:])]

    def arr(*shape):
        return jax.ShapeDtypeStruct(shape, jnp.bfloat16)

    firsts = [cuts[0], (cuts[1][0], columns - cuts[1][0])]
    outs = call(
        functools.partial(leaf_kernel, firsts),
        [arr(half, size, rank) for _, size in firsts for _ in range(2)],
        [vectors, leaf_basis],
        [VMEM, VMEM],
        2 * columns * rank * vectors.shape[0],
    )
    sent_a, kept_a, sent_b, kept_b = outs
    got_a, got_b = swapped(sent_a, "inner", 1), swapped(sent_b, "inner", 1)
    held = [(kept_a, got_a, 0)]
    held += [(kept_b, got_b, begin - cuts[1][0]) for begin, _ in cuts[1:]]

    after = kept_b
    done = [None] * len(cuts)
    steps = sorted((n + 2 * l, -n, n, l) for n in range(len(cuts)) for l in range(levels))
    for _, _, n, level in steps:
        size = cuts[n][1]
        kept, got, begin = held[n]
        flops = 2 * boxes * size * 2 * rank * rank
        if level < levels - 1:
            sent, kept = call(
                functools.partial(merge_kernel, level, begin, size),
                [arr(half, size, rank)] * 2,
                [kept, got, transfer, after],
                [VMEM, VMEM, VMEM, ANY],
                flops,
            )
            after = kept
            axis, bit = level_axis(level + 1)
            held[n] = (kept, swapped(sent, axis, 1 << bit), 0)
        else:
            cross, mine = call(
                functools.partial(last_kernel, level, begin, size),
                [arr(inner // 2, size, piece)] * 2,
                [box_order, kept, got, transfer, core_mats, row_basis, after],
                [SMEM, VMEM, VMEM, VMEM, VMEM, VMEM, ANY],
                2 * flops,
                [pltpu.VMEM((boxes, size, rank), jnp.bfloat16)] * 2,
            )
            after = mine
            got = swapped(cross, "inner", 1)
            packed = call(
                pack_kernel,
                [arr(2, size, piece)] * (inner // 2 - 1),
                [got, mine],
                [VMEM, VMEM],
                0,
            )
            others = [swapped(p, "inner", 2 * t) for t, p in enumerate(packed, 1)]
            done[n] = [got, mine, *others]
    flat = [x for part in done for x in part]
    return call(
        functools.partial(place_kernel, cuts), [arr(*vectors.shape)], flat, [VMEM] * len(flat), 0
    )[0]


def solution(mesh):
    in_specs = (
        P(("outer", "inner"), None),
        P(("outer", "inner"), None),
        P(None, "outer", "inner", None, None, None),
        P("outer", "inner", None, None, None),
        P(("outer", "inner"), None),
        P("outer", "inner", None),
    )
    out_specs = P(("outer", "inner"), None)
    return jax.shard_map(
        on_device, mesh=mesh, in_specs=in_specs, out_specs=out_specs, check_vma=False
    )
```

time: 92.5 us -> 93 us (level)
  blocking collectives: 31.2 us -> 0 us
  starting transfers between devices: 6.45 us -> 27.7 us
  Pallas kernels: 0 us -> 12 us
  waiting for transfers between devices: 35.3 us -> 44.1 us
  matrix products: 8.48 us -> 0 us
  local copies, waits for them, and re-layouts: 10.3 us -> 8.74 us
    all_to_all x1 -> x0, blocking collectives: 31.2 us -> none  [on_device(): lax.all_to_all(pieces, 'inner', split_axis=0, concat_axis=0, tiled=True)]
    ppermute x4 -> x23, starting transfers between devices: 6.45 us -> 27.7 us  [swapped(): lax.ppermute(array, axis, [(i, i ^ step) for i in range(lax.axis_size(axi...]
    pallas_call x0 -> x17, Pallas kernels: none -> 12 us  [call(): pl.pallas_call(kernel, out_shape=outs, in_specs=specs, out_specs=[VMEM] *...]
    ppermute x4 -> x23, waiting for transfers between devices: 35.3 us -> 44.1 us  [swapped(): lax.ppermute(array, axis, [(i, i ^ step) for i in range(lax.axis_size(axi...]
    dot_general x6 -> x0, matrix products: 8.48 us -> none  [the longest x4 3.47 us: merge_level(): jnp.einsum('kcs,kosr->kocr', stacked, paired_w, preferred_element_type=jn...]
    unnamed x16 -> x14, local copies, waits for them, and re-layouts: 2.46 us -> 8.74 us
    slice x1 -> x0, local copies, waits for them, and re-layouts: 5.66 us -> none  [on_device(): box_state = merge_level(kept_half, received, half_flag, weights[level_idx])]
    all_to_all x1 -> x0, local copies, waits for them, and re-layouts: 1.3 us -> none  [on_device(): lax.all_to_all(pieces, 'inner', split_axis=0, concat_axis=0, tiled=True)]
  transfers between devices with their start and end apart: 4 -> 23, of which waited for: 3 -> 6; matrix products, arithmetic and copies ran while one was open for 7% -> 0% of each run, Pallas kernels for 0% -> 6%
where the time goes in v1:
time: 93 us; the launch traced here: 92.7 us
  waiting for transfers between devices  44.1 us (47%)
  starting transfers between devices  27.7 us (30%)
  Pallas kernels  12 us (13%)
  local copies, waits for them, and re-layouts  8.74 us (9%)
    ppermute x23, waiting for transfers between devices, swapped(): lax.ppermute(array, axis, [(i, i ^ step) for i in range(lax.axis_size(axi...  44.1 us
    ppermute x23, starting transfers between devices, swapped(): lax.ppermute(array, axis, [(i, i ^ step) for i in range(lax.axis_size(axi...  27.7 us
    pallas_call x17, Pallas kernels, call(): pl.pallas_call(kernel, out_shape=outs, in_specs=specs, out_specs=[VMEM] *...  12 us
    unnamed x14, local copies, waits for them, and re-layouts  8.74 us
  transfers between devices with their start and end apart: 23, of which 6 were waited for; matrix products, arithmetic and copies ran while one was open for 0% of the time, Pallas kernels for 6%

profile of v1, /device:TPU:0, one launch (start us, length us, event | category | flops | bytes accessed | tf_op | source)
XLA Modules:
  0.0 92.7 jit_solution(14873069461378081956)
XLA Ops:
  0.0 1.2 %copy-done.4 = bf16[2048,256]{1,0:T(8,128)(2,1)S(1)} copy-done((bf16[2048,256]{1,0:T(8,128)(2,1)S(1)}, bf16[2048,256]{1,0:T(8,128)(2,1)}, u32[]{:S(2)}) %copy-start.4) | copy-done | bytes 1048600
  1.2 1.2 %copy-done.5 = bf16[2048,256]{1,0:T(8,128)(2,1)S(1)} copy-done((bf16[2048,256]{1,0:T(8,128)(2,1)S(1)}, bf16[2048,256]{1,0:T(8,128)(2,1)}, u32[]{:S(2)}) %copy-start.5) | copy-done | bytes 1048600
  2.5 0.5 shard_map.64
  2.9 0.5 collective-permute-start.2
  3.5 0.1 collective-permute-start
  3.5 1.5 %collective-permute-done.got_ref = bf16[4,64,256]{2,1,0:T(8,128)(2,1)S(1)} collective-permute-done((bf16[4,64,256]{2,1,0:T(8,128)(2,1)S(1)}, bf16[4,64,256]{2,1,0:T(8,128)(2,1)S(1)}, u32[]{:S(2)}, u32[]{:S(2)}) %collective-permute-start) | collective-permute-done | bytes 131104 | tf_op jit(solution)/shard_map/ppermute | solution.py:18
  5.0 3.4 %copy-done = bf16[4,1,1,8,512,256]{5,4,3,2,1,0:T(8,128)(2,1)S(1)} copy-done((bf16[4,1,1,8,512,256]{5,4,3,2,1,0:T(8,128)(2,1)S(1)}, bf16[4,1,1,8,512,256]{5,4,3,2,1,0:T(8,128)(2,1)}, u32[]{:S(2)}) %copy-start) | copy-done | bytes 8388632
  8.4 0.5 shard_map.65
  8.9 2.9 %copy-done.1 = bf16[4,1,1,8,512,256]{5,4,3,2,1,0:T(8,128)(2,1)S(1)} copy-done((bf16[4,1,1,8,512,256]{5,4,3,2,1,0:T(8,128)(2,1)S(1)}, bf16[4,1,1,8,512,256]{5,4,3,2,1,0:T(8,128)(2,1)}, u32[]{:S(2)}) %copy-start.1) | copy-done | bytes 8388632
  11.8 0.5 shard_map.66
  12.3 0.5 shard_map.67
  12.8 3.0 %collective-permute-start.4 = (bf16[4,112,256]{2,1,0:T(8,128)(2,1)S(1)}, bf16[4,112,256]{2,1,0:T(8,128)(2,1)S(1)}, u32[]{:S(2)}, u32[]{:S(2)}) collective-permute-start(bf16[4,112,256]{2,1,0:T(8,128)(2,1)S(1)} %get-tuple-element.52), channel_id=1, source_target_pairs={{0,2},{1,3},{2,0},{3,1},{4,6},{5,7},{6,4},{7,5},{8,10},{9,11},{10,... | collective-permute-start | bytes 688136 | tf_op jit(solution)/shard_map/ppermute | solution.py:18
  15.8 0.1 collective-permute-start.5
  15.8 1.9 %collective-permute-start.1 = (bf16[4,64,256]{2,1,0:T(8,128)(2,1)S(1)}, bf16[4,64,256]{2,1,0:T(8,128)(2,1)S(1)}, u32[]{:S(2)}, u32[]{:S(2)}) collective-permute-start(bf16[4,64,256]{2,1,0:T(8,128)(2,1)S(1)} %get-tuple-element.46), channel_id=1, source_target_pairs={{0,2},{1,3},{2,0},{3,1},{4,6},{5,7},{6,4},{7,5},{8,10},{9,11},{10,... | collective-permute-start | bytes 393224 | tf_op jit(solution)/shard_map/ppermute | solution.py:18
  17.8 10.2 %collective-permute-done.1.got_ref = bf16[4,64,256]{2,1,0:T(8,128)(2,1)S(1)} collective-permute-done((bf16[4,64,256]{2,1,0:T(8,128)(2,1)S(1)}, bf16[4,64,256]{2,1,0:T(8,128)(2,1)S(1)}, u32[]{:S(2)}, u32[]{:S(2)}) %collective-permute-start.1) | collective-permute-done | bytes 131104 | tf_op jit(solution)/shard_map/ppermute | solution.py:18
  28.0 0.5 shard_map.68
  28.5 0.5 shard_map.69
  29.0 0.5 shard_map.70
  29.5 1.7 %collective-permute-start.7 = (bf16[4,112,256]{2,1,0:T(8,128)(2,1)S(1)}, bf16[4,112,256]{2,1,0:T(8,128)(2,1)S(1)}, u32[]{:S(2)}, u32[]{:S(2)}) collective-permute-start(bf16[4,112,256]{2,1,0:T(8,128)(2,1)S(1)} %get-tuple-element.58), channel_id=1, source_target_pairs={{0,8},{8,0},{16,24},{24,16},{1,9},{9,1},{17,25},{25,17},{2,10},{10... | collective-permute-start | bytes 688136 | tf_op jit(solution)/shard_map/ppermute | solution.py:18
  31.2 0.4 collective-permute-start.8
  31.6 1.7 %collective-permute-start.3 = (bf16[4,64,256]{2,1,0:T(8,128)(2,1)S(1)}, bf16[4,64,256]{2,1,0:T(8,128)(2,1)S(1)}, u32[]{:S(2)}, u32[]{:S(2)}) collective-permute-start(bf16[4,64,256]{2,1,0:T(8,128)(2,1)S(1)} %get-tuple-element.51), channel_id=1, source_target_pairs={{0,8},{8,0},{16,24},{24,16},{1,9},{9,1},{17,25},{25,17},{2,10},{10... | collective-permute-start | bytes 393224 | tf_op jit(solution)/shard_map/ppermute | solution.py:18
  33.2 9.8 %collective-permute-done.3.got_ref = bf16[4,64,256]{2,1,0:T(8,128)(2,1)S(1)} collective-permute-done((bf16[4,64,256]{2,1,0:T(8,128)(2,1)S(1)}, bf16[4,64,256]{2,1,0:T(8,128)(2,1)S(1)}, u32[]{:S(2)}, u32[]{:S(2)}) %collective-permute-start.3) | collective-permute-done | bytes 131104 | tf_op jit(solution)/shard_map/ppermute | solution.py:18
  43.0 0.5 shard_map.71
  43.5 0.0 copy-start.2
  43.5 0.5 shard_map.72
  44.1 0.5 shard_map.73
  44.6 1.4 %collective-permute-start.18 = (bf16[4,112,256]{2,1,0:T(8,128)(2,1)S(1)}, bf16[4,112,256]{2,1,0:T(8,128)(2,1)S(1)}, u32[]{:S(2)}, u32[]{:S(2)}) collective-permute-start(bf16[4,112,256]{2,1,0:T(8,128)(2,1)S(1)} %get-tuple-element.73), channel_id=1, source_target_pairs={{0,16},{8,24},{16,0},{24,8},{1,17},{9,25},{17,1},{25,9},{2,18},{10... | collective-permute-start | bytes 688136 | tf_op jit(solution)/shard_map/ppermute | solution.py:18
  46.0 0.7 collective-permute-start.13
  46.6 1.4 %collective-permute-start.6 = (bf16[4,64,256]{2,1,0:T(8,128)(2,1)S(1)}, bf16[4,64,256]{2,1,0:T(8,128)(2,1)S(1)}, u32[]{:S(2)}, u32[]{:S(2)}) collective-permute-start(bf16[4,64,256]{2,1,0:T(8,128)(2,1)S(1)} %get-tuple-element.57), channel_id=1, source_target_pairs={{0,16},{8,24},{16,0},{24,8},{1,17},{9,25},{17,1},{25,9},{2,18},{10... | collective-permute-start | bytes 393224 | tf_op jit(solution)/shard_map/ppermute | solution.py:18
  48.0 9.1 %collective-permute-done.6.got_ref = bf16[4,64,256]{2,1,0:T(8,128)(2,1)S(1)} collective-permute-done((bf16[4,64,256]{2,1,0:T(8,128)(2,1)S(1)}, bf16[4,64,256]{2,1,0:T(8,128)(2,1)S(1)}, u32[]{:S(2)}, u32[]{:S(2)}) %collective-permute-start.6) | collective-permute-done | bytes 131104 | tf_op jit(solution)/shard_map/ppermute | solution.py:18
  57.2 1.7 %shard_map.74 = (bf16[4,64,256]{2,1,0:T(8,128)(2,1)S(1)}, bf16[4,64,256]{2,1,0:T(8,128)(2,1)S(1)}) custom-call(s32[1,1,8]{2,1,0:T(1,128)S(1)} %copy-done.6, bf16[4,64,256]{2,1,0:T(8,128)(2,1)S(1)} %get-tuple-element.56.after_ref.kept_ref, bf16[4,64,256]{2,1,0:T(8,128)(2,1)S(1)} %collective-permute-done.6.got_ref, ...), custom_call_target="tpu_custom_call" | custom-call | flops 268435456 | bytes 11239456 | tf_op jit(solution)/shard_map/pallas_call | solution.py:38
  58.9 1.7 %shard_map.76 = (bf16[4,80,256]{2,1,0:T(8,128)(2,1)S(1)}, bf16[4,80,256]{2,1,0:T(8,128)(2,1)S(1)}) custom-call(s32[1,1,8]{2,1,0:T(1,128)S(1)} %copy-done.6, bf16[4,80,256]{2,1,0:T(8,128)(2,1)S(1)} %get-tuple-element.60.after_ref.kept_ref, bf16[4,80,256]{2,1,0:T(8,128)(2,1)S(1)} %collective-permute-done.13.got_ref, ...), custom_call_target="tpu_custom_call" | custom-call | flops 335544320 | bytes 11272224 | tf_op jit(solution)/shard_map/pallas_call | solution.py:38
  60.6 1.7 %shard_map.78 = (bf16[4,112,256]{2,1,0:T(8,128)(2,1)S(1)}, bf16[4,112,256]{2,1,0:T(8,128)(2,1)S(1)}) custom-call(s32[1,1,8]{2,1,0:T(1,128)S(1)} %copy-done.6, bf16[4,112,256]{2,1,0:T(8,128)(2,1)S(1)} %get-tuple-element.61.after_ref.kept_ref, bf16[4,112,256]{2,1,0:T(8,128)(2,1)S(1)} %collective-permute-done.18.got_ref, ...), custom_call_target="tpu_custom_call" | custom-call | flops 469762048 | bytes 11567136 | tf_op jit(solution)/shard_map/pallas_call | solution.py:38
  62.3 0.1 collective-permute-start.19
  62.3 0.5 collective-permute-start.14
  62.8 0.1 collective-permute-start.9
  62.9 1.3 %collective-permute-done.9.got_ref.refs_0_ = bf16[4,64,256]{2,1,0:T(8,128)(2,1)S(1)} collective-permute-done((bf16[4,64,256]{2,1,0:T(8,128)(2,1)S(1)}, bf16[4,64,256]{2,1,0:T(8,128)(2,1)S(1)}, u32[]{:S(2)}, u32[]{:S(2)}) %collective-permute-start.9) | collective-permute-done | bytes 131104 | tf_op jit(solution)/shard_map/ppermute | solution.py:18
  64.3 1.2 %collective-permute-start.10 = (bf16[2,64,256]{2,1,0:T(8,128)(2,1)S(1)}, bf16[2,64,256]{2,1,0:T(8,128)(2,1)S(1)}, u32[]{:S(2)}, u32[]{:S(2)}) collective-permute-start(bf16[2,64,256]{2,1,0:T(8,128)(2,1)S(1)} %get-tuple-element.64), channel_id=1, source_target_pairs={{0,2},{1,3},{2,0},{3,1},{4,6},{5,7},{6,4},{7,5},{8,10},{9,11},{10,... | collective-permute-start | bytes 196616 | tf_op jit(solution)/shard_map/ppermute | solution.py:18
  65.4 2.6 %collective-permute-start.11 = (bf16[2,64,256]{2,1,0:T(8,128)(2,1)S(1)}, bf16[2,64,256]{2,1,0:T(8,128)(2,1)S(1)}, u32[]{:S(2)}, u32[]{:S(2)}) collective-permute-start(bf16[2,64,256]{2,1,0:T(8,128)(2,1)S(1)} %get-tuple-element.65), channel_id=1, source_target_pairs={{0,4},{1,5},{2,6},{3,7},{4,0},{5,1},{6,2},{7,3},{8,12},{9,13},{10,... | collective-permute-start | bytes 196616 | tf_op jit(solution)/shard_map/ppermute | solution.py:18
  68.1 0.5 collective-permute-start.15
  68.6 1.3 %collective-permute-start.12 = (bf16[2,64,256]{2,1,0:T(8,128)(2,1)S(1)}, bf16[2,64,256]{2,1,0:T(8,128)(2,1)S(1)}, u32[]{:S(2)}, u32[]{:S(2)}) collective-permute-start(bf16[2,64,256]{2,1,0:T(8,128)(2,1)S(1)} %get-tuple-element.66), channel_id=1, source_target_pairs={{0,6},{1,7},{2,4},{3,5},{4,2},{5,3},{6,0},{7,1},{8,14},{9,15},{10,... | collective-permute-start | bytes 196616 | tf_op jit(solution)/shard_map/ppermute | solution.py:18
  69.9 0.3 collective-permute-start.20
  70.3 2.8 %collective-permute-start.21 = (bf16[2,112,256]{2,1,0:T(8,128)(2,1)S(1)}, bf16[2,112,256]{2,1,0:T(8,128)(2,1)S(1)}, u32[]{:S(2)}, u32[]{:S(2)}) collective-permute-start(bf16[2,112,256]{2,1,0:T(8,128)(2,1)S(1)} %get-tuple-element.77), channel_id=1, source_target_pairs={{0,4},{1,5},{2,6},{3,7},{4,0},{5,1},{6,2},{7,3},{8,12},{9,13},{10,... | collective-permute-start | bytes 344072 | tf_op jit(solution)/shard_map/ppermute | solution.py:18
  73.1 2.7 %collective-permute-start.22 = (bf16[2,112,256]{2,1,0:T(8,128)(2,1)S(1)}, bf16[2,112,256]{2,1,0:T(8,128)(2,1)S(1)}, u32[]{:S(2)}, u32[]{:S(2)}) collective-permute-start(bf16[2,112,256]{2,1,0:T(8,128)(2,1)S(1)} %get-tuple-element.78), channel_id=1, source_target_pairs={{0,6},{1,7},{2,4},{3,5},{4,2},{5,3},{6,0},{7,1},{8,14},{9,15},{10,... | collective-permute-start | bytes 344072 | tf_op jit(solution)/shard_map/ppermute | solution.py:18
  75.8 1.2 %collective-permute-start.16 = (bf16[2,80,256]{2,1,0:T(8,128)(2,1)S(1)}, bf16[2,80,256]{2,1,0:T(8,128)(2,1)S(1)}, u32[]{:S(2)}, u32[]{:S(2)}) collective-permute-start(bf16[2,80,256]{2,1,0:T(8,128)(2,1)S(1)} %get-tuple-element.71), channel_id=1, source_target_pairs={{0,4},{1,5},{2,6},{3,7},{4,0},{5,1},{6,2},{7,3},{8,12},{9,13},{10,... | collective-permute-start | bytes 245768 | tf_op jit(solution)/shard_map/ppermute | solution.py:18
  77.0 1.6 %collective-permute-start.17 = (bf16[2,80,256]{2,1,0:T(8,128)(2,1)S(1)}, bf16[2,80,256]{2,1,0:T(8,128)(2,1)S(1)}, u32[]{:S(2)}, u32[]{:S(2)}) collective-permute-start(bf16[2,80,256]{2,1,0:T(8,128)(2,1)S(1)} %get-tuple-element.72), channel_id=1, source_target_pairs={{0,6},{1,7},{2,4},{3,5},{4,2},{5,3},{6,0},{7,1},{8,14},{9,15},{10,... | collective-permute-start | bytes 245768 | tf_op jit(solution)/shard_map/ppermute | solution.py:18
  78.5 12.2 %collective-permute-done.16.refs_8_ = bf16[2,80,256]{2,1,0:T(8,128)(2,1)S(1)} collective-permute-done((bf16[2,80,256]{2,1,0:T(8,128)(2,1)S(1)}, bf16[2,80,256]{2,1,0:T(8,128)(2,1)S(1)}, u32[]{:S(2)}, u32[]{:S(2)}) %collective-permute-start.16) | collective-permute-done | bytes 81952 | tf_op jit(solution)/shard_map/ppermute | solution.py:18
  90.7 2.0 %shard_map.80 = bf16[2048,256]{1,0:T(8,128)(2,1)} custom-call(bf16[4,64,256]{2,1,0:T(8,128)(2,1)S(1)} %collective-permute-done.9.got_ref.refs_0_, bf16[4,64,256]{2,1,0:T(8,128)(2,1)S(1)} %get-tuple-element.63.mine_ref.after_ref.refs_1_, bf16[2,64,256]{2,1,0:T(8,128)(2,1)S(1)} %collective-permute-done.10.refs_2_, ...), custom_call_target="tpu_custom_call" | custom-call | bytes 2883584 | tf_op jit(solution)/shard_map/pallas_call | solution.py:38
  (29 shorter events, 0.1 us)
Async XLA Ops:
  0.0 1.2 %copy-start.4 = (bf16[2048,256]{1,0:T(8,128)(2,1)S(1)}, bf16[2048,256]{1,0:T(8,128)(2,1)}, u32[]{:S(2)}) copy-start(bf16[2048,256]{1,0:T(8,128)(2,1)} %x_ref.1) | copy-start | bytes 3145732
  1.2 1.2 %copy-start.5 = (bf16[2048,256]{1,0:T(8,128)(2,1)S(1)}, bf16[2048,256]{1,0:T(8,128)(2,1)}, u32[]{:S(2)}) copy-start(bf16[2048,256]{1,0:T(8,128)(2,1)} %v_ref.1) | copy-start | bytes 3145732
  2.9 5.9 %collective-permute-start.2 = (bf16[4,192,256]{2,1,0:T(8,128)(2,1)S(1)}, bf16[4,192,256]{2,1,0:T(8,128)(2,1)S(1)}, u32[]{:S(2)}, u32[]{:S(2)}) collective-permute-start(bf16[4,192,256]{2,1,0:T(8,128)(2,1)S(1)} %get-tuple-element.47), channel_id=1, source_target_pairs={{0,1},{1,0},{2,3},{3,2},{4,5},{5,4},{6,7},{7,6},{8,9},{9,8},{10,11... | collective-permute-start | bytes 1179656 | tf_op jit(solution)/shard_map/ppermute | solution.py:18
  3.5 1.5 %collective-permute-start = (bf16[4,64,256]{2,1,0:T(8,128)(2,1)S(1)}, bf16[4,64,256]{2,1,0:T(8,128)(2,1)S(1)}, u32[]{:S(2)}, u32[]{:S(2)}) collective-permute-start(bf16[4,64,256]{2,1,0:T(8,128)(2,1)S(1)} %get-tuple-element.43), channel_id=1, source_target_pairs={{0,1},{1,0},{2,3},{3,2},{4,5},{5,4},{6,7},{7,6},{8,9},{9,8},{10,11... | collective-permute-start | bytes 393224 | tf_op jit(solution)/shard_map/ppermute | solution.py:18
  5.0 3.4 %copy-start = (bf16[4,1,1,8,512,256]{5,4,3,2,1,0:T(8,128)(2,1)S(1)}, bf16[4,1,1,8,512,256]{5,4,3,2,1,0:T(8,128)(2,1)}, u32[]{:S(2)}) copy-start(bf16[4,1,1,8,512,256]{5,4,3,2,1,0:T(8,128)(2,1)} %w_ref.23) | copy-start | bytes 25165828
  8.4 3.4 %copy-start.1 = (bf16[4,1,1,8,512,256]{5,4,3,2,1,0:T(8,128)(2,1)S(1)}, bf16[4,1,1,8,512,256]{5,4,3,2,1,0:T(8,128)(2,1)}, u32[]{:S(2)}) copy-start(bf16[4,1,1,8,512,256]{5,4,3,2,1,0:T(8,128)(2,1)} %w_ref.23) | copy-start | bytes 25165828
  12.8 16.2 %collective-permute-start.4 = (bf16[4,112,256]{2,1,0:T(8,128)(2,1)S(1)}, bf16[4,112,256]{2,1,0:T(8,128)(2,1)S(1)}, u32[]{:S(2)}, u32[]{:S(2)}) collective-permute-start(bf16[4,112,256]{2,1,0:T(8,128)(2,1)S(1)} %get-tuple-element.52), channel_id=1, source_target_pairs={{0,2},{1,3},{2,0},{3,1},{4,6},{5,7},{6,4},{7,5},{8,10},{9,11},{10,... | collective-permute-start | bytes 688136 | tf_op jit(solution)/shard_map/ppermute | solution.py:18
  15.8 12.7 %collective-permute-start.5 = (bf16[4,80,256]{2,1,0:T(8,128)(2,1)S(1)}, bf16[4,80,256]{2,1,0:T(8,128)(2,1)S(1)}, u32[]{:S(2)}, u32[]{:S(2)}) collective-permute-start(bf16[4,80,256]{2,1,0:T(8,128)(2,1)S(1)} %get-tuple-element.53), channel_id=1, source_target_pairs={{0,2},{1,3},{2,0},{3,1},{4,6},{5,7},{6,4},{7,5},{8,10},{9,11},{10,... | collective-permute-start | bytes 491528 | tf_op jit(solution)/shard_map/ppermute | solution.py:18
  15.8 12.1 %collective-permute-start.1 = (bf16[4,64,256]{2,1,0:T(8,128)(2,1)S(1)}, bf16[4,64,256]{2,1,0:T(8,128)(2,1)S(1)}, u32[]{:S(2)}, u32[]{:S(2)}) collective-permute-start(bf16[4,64,256]{2,1,0:T(8,128)(2,1)S(1)} %get-tuple-element.46), channel_id=1, source_target_pairs={{0,2},{1,3},{2,0},{3,1},{4,6},{5,7},{6,4},{7,5},{8,10},{9,11},{10,... | collective-permute-start | bytes 393224 | tf_op jit(solution)/shard_map/ppermute | solution.py:18
  29.5 14.6 %collective-permute-start.7 = (bf16[4,112,256]{2,1,0:T(8,128)(2,1)S(1)}, bf16[4,112,256]{2,1,0:T(8,128)(2,1)S(1)}, u32[]{:S(2)}, u32[]{:S(2)}) collective-permute-start(bf16[4,112,256]{2,1,0:T(8,128)(2,1)S(1)} %get-tuple-element.58), channel_id=1, source_target_pairs={{0,8},{8,0},{16,24},{24,16},{1,9},{9,1},{17,25},{25,17},{2,10},{10... | collective-permute-start | bytes 688136 | tf_op jit(solution)/shard_map/ppermute | solution.py:18
  31.2 12.3 %collective-permute-start.8 = (bf16[4,80,256]{2,1,0:T(8,128)(2,1)S(1)}, bf16[4,80,256]{2,1,0:T(8,128)(2,1)S(1)}, u32[]{:S(2)}, u32[]{:S(2)}) collective-permute-start(bf16[4,80,256]{2,1,0:T(8,128)(2,1)S(1)} %get-tuple-element.59), channel_id=1, source_target_pairs={{0,8},{8,0},{16,24},{24,16},{1,9},{9,1},{17,25},{25,17},{2,10},{10... | collective-permute-start | bytes 491528 | tf_op jit(solution)/shard_map/ppermute | solution.py:18
  31.6 11.4 %collective-permute-start.3 = (bf16[4,64,256]{2,1,0:T(8,128)(2,1)S(1)}, bf16[4,64,256]{2,1,0:T(8,128)(2,1)S(1)}, u32[]{:S(2)}, u32[]{:S(2)}) collective-permute-start(bf16[4,64,256]{2,1,0:T(8,128)(2,1)S(1)} %get-tuple-element.51), channel_id=1, source_target_pairs={{0,8},{8,0},{16,24},{24,16},{1,9},{9,1},{17,25},{25,17},{2,10},{10... | collective-permute-start | bytes 393224 | tf_op jit(solution)/shard_map/ppermute | solution.py:18
  43.5 13.7 %copy-start.2 = (bf16[1,1,8,256,256]{4,3,2,1,0:T(8,128)(2,1)S(1)}, bf16[1,1,8,256,256]{4,3,2,1,0:T(8,128)(2,1)}, u32[]{:S(2)}) copy-start(bf16[1,1,8,256,256]{4,3,2,1,0:T(8,128)(2,1)} %core_ref.5) | copy-start | bytes 3145732
  43.5 13.7 %copy-start.3 = (bf16[2048,256]{1,0:T(8,128)(2,1)S(1)}, bf16[2048,256]{1,0:T(8,128)(2,1)}, u32[]{:S(2)}) copy-start(bf16[2048,256]{1,0:T(8,128)(2,1)} %u_ref.5) | copy-start | bytes 3145732
  43.5 13.6 %copy-start.6 = (s32[1,1,8]{2,1,0:T(1,128)S(1)}, s32[1,1,8]{2,1,0:T(1,128)}, u32[]{:S(2)}) copy-start(s32[1,1,8]{2,1,0:T(1,128)} %order_ref.5) | copy-start | bytes 100
  44.6 16.0 %collective-permute-start.18 = (bf16[4,112,256]{2,1,0:T(8,128)(2,1)S(1)}, bf16[4,112,256]{2,1,0:T(8,128)(2,1)S(1)}, u32[]{:S(2)}, u32[]{:S(2)}) collective-permute-start(bf16[4,112,256]{2,1,0:T(8,128)(2,1)S(1)} %get-tuple-element.73), channel_id=1, source_target_pairs={{0,16},{8,24},{16,0},{24,8},{1,17},{9,25},{17,1},{25,9},{2,18},{10... | collective-permute-start | bytes 688136 | tf_op jit(solution)/shard_map/ppermute | solution.py:18
  46.0 12.8 %collective-permute-start.13 = (bf16[4,80,256]{2,1,0:T(8,128)(2,1)S(1)}, bf16[4,80,256]{2,1,0:T(8,128)(2,1)S(1)}, u32[]{:S(2)}, u32[]{:S(2)}) collective-permute-start(bf16[4,80,256]{2,1,0:T(8,128)(2,1)S(1)} %get-tuple-element.67), channel_id=1, source_target_pairs={{0,16},{8,24},{16,0},{24,8},{1,17},{9,25},{17,1},{25,9},{2,18},{10... | collective-permute-start | bytes 491528 | tf_op jit(solution)/shard_map/ppermute | solution.py:18
  46.6 10.5 %collective-permute-start.6 = (bf16[4,64,256]{2,1,0:T(8,128)(2,1)S(1)}, bf16[4,64,256]{2,1,0:T(8,128)(2,1)S(1)}, u32[]{:S(2)}, u32[]{:S(2)}) collective-permute-start(bf16[4,64,256]{2,1,0:T(8,128)(2,1)S(1)} %get-tuple-element.57), channel_id=1, source_target_pairs={{0,16},{8,24},{16,0},{24,8},{1,17},{9,25},{17,1},{25,9},{2,18},{10... | collective-permute-start | bytes 393224 | tf_op jit(solution)/shard_map/ppermute | solution.py:18
  62.3 7.6 %collective-permute-start.19 = (bf16[4,112,256]{2,1,0:T(8,128)(2,1)S(1)}, bf16[4,112,256]{2,1,0:T(8,128)(2,1)S(1)}, u32[]{:S(2)}, u32[]{:S(2)}) collective-permute-start(bf16[4,112,256]{2,1,0:T(8,128)(2,1)S(1)} %get-tuple-element.74), channel_id=1, source_target_pairs={{0,1},{1,0},{2,3},{3,2},{4,5},{5,4},{6,7},{7,6},{8,9},{9,8},{10,11... | collective-permute-start | bytes 688136 | tf_op jit(solution)/shard_map/ppermute | solution.py:18
  62.3 5.7 %collective-permute-start.14 = (bf16[4,80,256]{2,1,0:T(8,128)(2,1)S(1)}, bf16[4,80,256]{2,1,0:T(8,128)(2,1)S(1)}, u32[]{:S(2)}, u32[]{:S(2)}) collective-permute-start(bf16[4,80,256]{2,1,0:T(8,128)(2,1)S(1)} %get-tuple-element.68), channel_id=1, source_target_pairs={{0,1},{1,0},{2,3},{3,2},{4,5},{5,4},{6,7},{7,6},{8,9},{9,8},{10,11... | collective-permute-start | bytes 491528 | tf_op jit(solution)/shard_map/ppermute | solution.py:18
  62.8 1.4 %collective-permute-start.9 = (bf16[4,64,256]{2,1,0:T(8,128)(2,1)S(1)}, bf16[4,64,256]{2,1,0:T(8,128)(2,1)S(1)}, u32[]{:S(2)}, u32[]{:S(2)}) collective-permute-start(bf16[4,64,256]{2,1,0:T(8,128)(2,1)S(1)} %get-tuple-element.62), channel_id=1, source_target_pairs={{0,1},{1,0},{2,3},{3,2},{4,5},{5,4},{6,7},{7,6},{8,9},{9,8},{10,11... | collective-permute-start | bytes 393224 | tf_op jit(solution)/shard_map/ppermute | solution.py:18
  64.3 6.0 %collective-permute-start.10 = (bf16[2,64,256]{2,1,0:T(8,128)(2,1)S(1)}, bf16[2,64,256]{2,1,0:T(8,128)(2,1)S(1)}, u32[]{:S(2)}, u32[]{:S(2)}) collective-permute-start(bf16[2,64,256]{2,1,0:T(8,128)(2,1)S(1)} %get-tuple-element.64), channel_id=1, source_target_pairs={{0,2},{1,3},{2,0},{3,1},{4,6},{5,7},{6,4},{7,5},{8,10},{9,11},{10,... | collective-permute-start | bytes 196616 | tf_op jit(solution)/shard_map/ppermute | solution.py:18
  65.4 7.6 %collective-permute-start.11 = (bf16[2,64,256]{2,1,0:T(8,128)(2,1)S(1)}, bf16[2,64,256]{2,1,0:T(8,128)(2,1)S(1)}, u32[]{:S(2)}, u32[]{:S(2)}) collective-permute-start(bf16[2,64,256]{2,1,0:T(8,128)(2,1)S(1)} %get-tuple-element.65), channel_id=1, source_target_pairs={{0,4},{1,5},{2,6},{3,7},{4,0},{5,1},{6,2},{7,3},{8,12},{9,13},{10,... | collective-permute-start | bytes 196616 | tf_op jit(solution)/shard_map/ppermute | solution.py:18
  68.1 8.9 %collective-permute-start.15 = (bf16[2,80,256]{2,1,0:T(8,128)(2,1)S(1)}, bf16[2,80,256]{2,1,0:T(8,128)(2,1)S(1)}, u32[]{:S(2)}, u32[]{:S(2)}) collective-permute-start(bf16[2,80,256]{2,1,0:T(8,128)(2,1)S(1)} %get-tuple-element.70), channel_id=1, source_target_pairs={{0,2},{1,3},{2,0},{3,1},{4,6},{5,7},{6,4},{7,5},{8,10},{9,11},{10,... | collective-permute-start | bytes 245768 | tf_op jit(solution)/shard_map/ppermute | solution.py:18
  68.6 7.2 %collective-permute-start.12 = (bf16[2,64,256]{2,1,0:T(8,128)(2,1)S(1)}, bf16[2,64,256]{2,1,0:T(8,128)(2,1)S(1)}, u32[]{:S(2)}, u32[]{:S(2)}) collective-permute-start(bf16[2,64,256]{2,1,0:T(8,128)(2,1)S(1)} %get-tuple-element.66), channel_id=1, source_target_pairs={{0,6},{1,7},{2,4},{3,5},{4,2},{5,3},{6,0},{7,1},{8,14},{9,15},{10,... | collective-permute-start | bytes 196616 | tf_op jit(solution)/shard_map/ppermute | solution.py:18
  69.9 20.8 %collective-permute-start.20 = (bf16[2,112,256]{2,1,0:T(8,128)(2,1)S(1)}, bf16[2,112,256]{2,1,0:T(8,128)(2,1)S(1)}, u32[]{:S(2)}, u32[]{:S(2)}) collective-permute-start(bf16[2,112,256]{2,1,0:T(8,128)(2,1)S(1)} %get-tuple-element.76), channel_id=1, source_target_pairs={{0,2},{1,3},{2,0},{3,1},{4,6},{5,7},{6,4},{7,5},{8,10},{9,11},{10,... | collective-permute-start | bytes 344072 | tf_op jit(solution)/shard_map/ppermute | solution.py:18
  70.3 20.5 %collective-permute-start.21 = (bf16[2,112,256]{2,1,0:T(8,128)(2,1)S(1)}, bf16[2,112,256]{2,1,0:T(8,128)(2,1)S(1)}, u32[]{:S(2)}, u32[]{:S(2)}) collective-permute-start(bf16[2,112,256]{2,1,0:T(8,128)(2,1)S(1)} %get-tuple-element.77), channel_id=1, source_target_pairs={{0,4},{1,5},{2,6},{3,7},{4,0},{5,1},{6,2},{7,3},{8,12},{9,13},{10,... | collective-permute-start | bytes 344072 | tf_op jit(solution)/shard_map/ppermute | solution.py:18
  73.1 17.7 %collective-permute-start.22 = (bf16[2,112,256]{2,1,0:T(8,128)(2,1)S(1)}, bf16[2,112,256]{2,1,0:T(8,128)(2,1)S(1)}, u32[]{:S(2)}, u32[]{:S(2)}) collective-permute-start(bf16[2,112,256]{2,1,0:T(8,128)(2,1)S(1)} %get-tuple-element.78), channel_id=1, source_target_pairs={{0,6},{1,7},{2,4},{3,5},{4,2},{5,3},{6,0},{7,1},{8,14},{9,15},{10,... | collective-permute-start | bytes 344072 | tf_op jit(solution)/shard_map/ppermute | solution.py:18
  75.8 14.9 %collective-permute-start.16 = (bf16[2,80,256]{2,1,0:T(8,128)(2,1)S(1)}, bf16[2,80,256]{2,1,0:T(8,128)(2,1)S(1)}, u32[]{:S(2)}, u32[]{:S(2)}) collective-permute-start(bf16[2,80,256]{2,1,0:T(8,128)(2,1)S(1)} %get-tuple-element.71), channel_id=1, source_target_pairs={{0,4},{1,5},{2,6},{3,7},{4,0},{5,1},{6,2},{7,3},{8,12},{9,13},{10,... | collective-permute-start | bytes 245768 | tf_op jit(solution)/shard_map/ppermute | solution.py:18
  77.0 13.8 %collective-permute-start.17 = (bf16[2,80,256]{2,1,0:T(8,128)(2,1)S(1)}, bf16[2,80,256]{2,1,0:T(8,128)(2,1)S(1)}, u32[]{:S(2)}, u32[]{:S(2)}) collective-permute-start(bf16[2,80,256]{2,1,0:T(8,128)(2,1)S(1)} %get-tuple-element.72), channel_id=1, source_target_pairs={{0,6},{1,7},{2,4},{3,5},{4,2},{5,3},{6,0},{7,1},{8,14},{9,15},{10,... | collective-permute-start | bytes 245768 | tf_op jit(solution)/shard_map/ppermute | solution.py:18

commit v2 on v1

v2 whole, which is shorter than its diff:
```python
import functools

import jax
import jax.numpy as jnp
from jax import lax
from jax.experimental import pallas as pl
from jax.experimental.pallas import tpu as pltpu
from jax.sharding import PartitionSpec as P

INNER_LEVELS = 2
PARTS = (4, 5, 7)
COSTS = {}
ORDER = ("f", "w", "m0a", "m0b", "m0c", "m1a", "m1b", "j", "m2a", "m1c", "m2b", "oa", "m2c", "ob", "qa", "ec", "pc", "qb")
LEAF_ROOM = 52
LOAD_ROOM = 48
HBM = pl.BlockSpec(memory_space=pltpu.HBM)
VMEM = pl.BlockSpec(memory_space=pltpu.VMEM)
ANY = pl.BlockSpec(memory_space=pl.ANY)
SMEM = pl.BlockSpec(memory_space=pltpu.SMEM)


def swapped(array, axis, step):
    return lax.ppermute(array, axis, [(i, i ^ step) for i in range(lax.axis_size(axis))])


def level_axis(level):
    return ("inner", level) if level < INNER_LEVELS else ("outer", level - INNER_LEVELS)


def bit_of(level):
    axis, bit = level_axis(level)
    return jnp.bitwise_and(jnp.right_shift(lax.axis_index(axis), bit), 1)


def arr(*shape):
    return jax.ShapeDtypeStruct(shape, jnp.bfloat16)


def dot(a, b, dims=((1,), (0,))):
    return lax.dot_general(a, b, (dims, ((), ())), preferred_element_type=jnp.float32)


def call(kernel, outs, ins, specs, scratch=(), name=None, room=24):
    run = pl.pallas_call(
        kernel,
        name=name,
        out_shape=outs,
        in_specs=specs,
        out_specs=[VMEM] * len(outs),
        scratch_shapes=list(scratch),
        compiler_params=pltpu.CompilerParams(vmem_limit_bytes=room * 1024 * 1024),
        cost_estimate=pl.CostEstimate(
            flops=int(COSTS.get(name, 2) * 1e9), bytes_accessed=0, transcendentals=0
        ),
    )
    return list(run(*ins))


def copy_all(copies):
    for copy in copies:
        copy.start()
    return copies


def load_kernel(w_hbm, after_ref, w_out, sem):
    load = pltpu.make_async_copy(w_hbm.at[0, 0, 0], w_out, sem)
    load.start()
    load.wait()


def leaf_kernel(cuts, x_hbm, v_hbm, *refs):
    outs, (x_ref, v_ref, sems) = refs[:-3], refs[-3:]
    half = outs[0].shape[0]
    flag = bit_of(0)
    rows = x_ref.shape[0] // (2 * half)

    def window(slot):
        side = 1 - flag if slot < half else flag
        return pl.ds(pl.multiple_of((side * half + slot % half) * rows, rows), rows)

    loads = []
    for slot in range(2 * half):
        at = window(slot)
        loads.append(
            copy_all(
                [
                    pltpu.make_async_copy(x_hbm.at[at], x_ref.at[at], sems.at[0, slot]),
                    pltpu.make_async_copy(v_hbm.at[at], v_ref.at[at], sems.at[1, slot]),
                ]
            )
        )
    for slot in range(2 * half):
        at = window(slot)
        for load in loads[slot]:
            load.wait()
        state = dot(x_ref[at, :].T, v_ref[at, :]).astype(jnp.bfloat16)
        for n, (begin, size) in enumerate(cuts):
            outs[2 * n + (slot >= half)][slot % half] = state[begin : begin + size]


def join_kernel(level, order_ref, w_ref, core_ref, u_ref, after_ref, joint_out):
    width = joint_out.shape[2]
    for n in range(joint_out.shape[0]):
        box = n * width // (u_ref.shape[0] // core_ref.shape[2])
        inside = dot(core_ref[0, 0, box], u_ref[n * width : (n + 1) * width, :], ((1,), (1,)))
        joint = dot(w_ref[level, 0, 0, order_ref[0, 0, box]], inside.astype(jnp.bfloat16))
        joint_out[n] = joint.astype(jnp.bfloat16)


def merged(level, begin, size, kept_ref, got_ref, w_ref, k, box):
    rank = kept_ref.shape[2]
    flag = bit_of(level)
    at = pl.ds(begin, size)
    place = (level, 0, 0, box) if len(w_ref.shape) == 6 else (box,)
    mine = w_ref[(*place, pl.ds(pl.multiple_of(flag * rank, rank), rank), slice(None))]
    other = w_ref[(*place, pl.ds(pl.multiple_of((1 - flag) * rank, rank), rank), slice(None))]
    total = dot(kept_ref[k, at, :], mine) + dot(got_ref[k, at, :], other)
    return total.astype(jnp.bfloat16)


def merge_kernel(level, begin, size, kept_ref, got_ref, w_ref, after_ref, sent_out, kept_out):
    half = kept_ref.shape[0]
    flag = bit_of(level + 1)
    for slot in range(2 * half):
        side = 1 - flag if slot < half else flag
        box = side * half + slot % half
        out = sent_out if slot < half else kept_out
        out[slot % half] = merged(level, begin, size, kept_ref, got_ref, w_ref, box // 2, box)


def last_kernel(
    level, early, begin, size, order_ref, kept_ref, got_ref, joint_ref, after_ref, *outs
):
    half = kept_ref.shape[0]
    me = lax.axis_index("inner")
    width = joint_ref.shape[2]
    piece = outs[0].shape[2]
    pieces = joint_ref.shape[0] * width // piece
    per_box = joint_ref.shape[0] // (2 * half)
    for t in range(pieces // 2):
        for odd in range(2):
            out = (outs[1 + t] if odd else outs[0].at[t]) if early else outs[t].at[odd]
            first = jnp.bitwise_xor(me, 2 * t + odd) * (piece // width)
            for n in range(piece // width):
                k = order_ref[0, 0, (first + n) // per_box] // 2
                out[:, n * width : (n + 1) * width] = merged(
                    level, begin, size, kept_ref, got_ref, joint_ref, k, first + n
                )


def early_pack_kernel(mine_ref, *refs):
    count = mine_ref.shape[0]
    for t, out in enumerate(refs[count + 1 :], 1):
        out[0] = mine_ref[t]
        out[1] = refs[t][...]


def late_pack_kernel(*refs):
    out = refs[-1]
    for t, ref in enumerate(refs[:-2]):
        out[t] = ref[1]


def place_kernel(cuts, *refs):
    out, ins = refs[-1], refs[:-1]
    me = lax.axis_index("inner")
    rows = ins[0].shape[2]
    per = out.shape[0] // rows // 2 + 1
    for n, (begin, size) in enumerate(cuts):
        chunk = ins[n * per : (n + 1) * per]
        last = n == len(cuts) - 1
        for t in range(per - 1):
            for odd in range(2):
                if last:
                    block = chunk[t + 1][odd]
                    if t == 0:
                        block = chunk[1][...] if odd else chunk[0][0]
                else:
                    block = chunk[per - 1][t] if odd else chunk[t][0]
                owner = jnp.bitwise_xor(me, 2 * t + odd)
                window = pl.ds(pl.multiple_of(owner * rows, rows), rows)
                out[window, begin : begin + size] = block.T


def on_device(vectors, leaf_basis, transfer, core_mats, row_basis, box_order):
    boxes = transfer.shape[3]
    half = boxes // 2
    rank = leaf_basis.shape[1]
    columns = vectors.shape[1]
    levels = transfer.shape[0]
    inner = lax.axis_size("inner")
    piece = vectors.shape[0] // inner
    width = min(piece, vectors.shape[0] // boxes)
    edges = [columns * sum(PARTS[:n]) // sum(PARTS) for n in range(len(PARTS) + 1)]
    cuts = [(a, b - a) for a, b in zip(edges, edges[1:])]
    count = len(cuts)
    held = [None] * count
    done = [None] * count
    level_w = joint = after = None

    for step in ORDER:
        kind, n = step[0], "abcdefgh".find(step[-1])
        if kind == "f":
            firsts = [cuts[0], (cuts[1][0], columns - cuts[1][0])]
            sent_a, kept_a, sent_b, kept_b = call(
                functools.partial(leaf_kernel, firsts),
                [arr(half, size, rank) for _, size in firsts for _ in range(2)],
                [vectors, leaf_basis],
                [HBM] * 2,
                [
                    pltpu.VMEM(vectors.shape, jnp.bfloat16),
                    pltpu.VMEM(leaf_basis.shape, jnp.bfloat16),
                    pltpu.SemaphoreType.DMA((2, boxes)),
                ],
                name="leaves",
                room=LEAF_ROOM,
            )
            got_a, got_b = swapped(sent_a, "inner", 1), swapped(sent_b, "inner", 1)
            held = [(kept_a, got_a, 0)]
            held += [(kept_b, got_b, begin - cuts[1][0]) for begin, _ in cuts[1:]]
            after = kept_b
        elif kind == "w":
            level_w = call(
                load_kernel,
                [arr(boxes, 2 * rank, rank)],
                [transfer, after],
                [HBM, ANY],
                [pltpu.SemaphoreType.DMA],
                name="weights",
                room=LOAD_ROOM,
            )[0]
            after = level_w
        elif kind == "j":
            joint = call(
                functools.partial(join_kernel, levels - 1),
                [arr(vectors.shape[0] // width, 2 * rank, width)],
                [box_order, transfer, core_mats, row_basis, after],
                [SMEM, VMEM, VMEM, VMEM, ANY],
                name="join",
            )[0]
            after = joint
        elif kind == "m":
            level = int(step[1])
            size = cuts[n][1]
            kept, got, begin = held[n]
            sent, kept = call(
                functools.partial(merge_kernel, level, begin, size),
                [arr(half, size, rank)] * 2,
                [kept, got, transfer if level else level_w, after],
                [VMEM, VMEM, VMEM, ANY],
                name=f"merge{level}{step[-1]}",
            )
            after = kept
            axis, bit = level_axis(level + 1)
            held[n] = (kept, swapped(sent, axis, 1 << bit), 0)
        elif kind in "eo":
            size = cuts[n][1]
            kept, got, begin = held[n]
            early = kind == "e"
            shapes = [arr(2, size, piece)] * (inner // 2)
            if early:
                shapes = [arr(inner // 2, size, piece)] + [arr(size, piece)] * (inner // 2)
            outs = call(
                functools.partial(last_kernel, levels - 1, early, begin, size),
                shapes,
                [box_order, kept, got, joint, after],
                [SMEM, VMEM, VMEM, VMEM, ANY],
                name=f"last{step[-1]}",
            )
            after = outs[0]
            if early:
                done[n] = outs[:1] + [swapped(x, "inner", 1) for x in outs[1:]]
            else:
                done[n] = outs[:1] + [swapped(x, "inner", 2 * t) for t, x in enumerate(outs[1:], 1)]
        elif kind == "p":
            outs = call(
                early_pack_kernel,
                [arr(2, cuts[n][1], piece)] * (inner // 2 - 1),
                done[n] + [after],
                [VMEM] * len(done[n]) + [ANY],
                name=f"pack{step[-1]}",
            )
            after = outs[0]
            done[n] = done[n][:2] + [swapped(x, "inner", 2 * t) for t, x in enumerate(outs, 1)]
        elif kind == "q":
            cross = call(
                late_pack_kernel,
                [arr(inner // 2, cuts[n][1], piece)],
                done[n] + [after],
                [VMEM] * len(done[n]) + [ANY],
                name=f"pack{step[-1]}",
            )[0]
            after = cross
            done[n].append(swapped(cross, "inner", 1))
    flat = [x for part in done for x in part]
    return call(
        functools.partial(place_kernel, cuts),
        [arr(*vectors.shape)],
        flat,
        [VMEM] * len(flat),
        name="place",
    )[0]


def solution(mesh):
    in_specs = (
        P(("outer", "inner"), None),
        P(("outer", "inner"), None),
        P(None, "outer", "inner", None, None, None),
        P("outer", "inner", None, None, None),
        P(("outer", "inner"), None),
        P("outer", "inner", None),
    )
    out_specs = P(("outer", "inner"), None)
    return jax.shard_map(
        on_device, mesh=mesh, in_specs=in_specs, out_specs=out_specs, check_vma=False
    )
```

time: 93 us -> 68.5 us (0.74)
  waiting for transfers between devices: 44.1 us -> 23.8 us
  local copies, waits for them, and re-layouts: 8.74 us -> 0.02 us
  Pallas kernels: 12 us -> 16.3 us
    ppermute x23 -> x26, waiting for transfers between devices: 44.1 us -> 23.8 us  [swapped(): lax.ppermute(array, axis, [(i, i ^ step) for i in range(lax.axis_size(axi...]
    unnamed x14 -> x10, local copies, waits for them, and re-layouts: 8.74 us -> 0.02 us
    pallas_call x17 -> x19, Pallas kernels: 12 us -> 16.3 us  [call(): return list(run(*ins))]
    ppermute x23 -> x26, starting transfers between devices: 27.7 us -> 28 us  [swapped(): lax.ppermute(array, axis, [(i, i ^ step) for i in range(lax.axis_size(axi...]
  transfers between devices with their start and end apart: 23 -> 26, of which waited for: 6 -> 7; matrix products, arithmetic and copies ran while one was open for 0% -> 0% of each run, Pallas kernels for 6% -> 15%
where the time goes in v2:
time: 68.5 us; the launch traced here: 68.3 us
  starting transfers between devices  28 us (41%)
  waiting for transfers between devices  23.8 us (35%)
  Pallas kernels  16.3 us (24%)
    ppermute x26, starting transfers between devices, swapped(): lax.ppermute(array, axis, [(i, i ^ step) for i in range(lax.axis_size(axi...  28 us
    ppermute x26, waiting for transfers between devices, swapped(): lax.ppermute(array, axis, [(i, i ^ step) for i in range(lax.axis_size(axi...  23.8 us
    pallas_call x19, Pallas kernels, call(): return list(run(*ins))  16.3 us
  transfers between devices with their start and end apart: 26, of which 7 were waited for; matrix products, arithmetic and copies ran while one was open for 0% of the time, Pallas kernels for 15%

profile of v2, /device:TPU:0, one launch (start us, length us, event | category | flops | bytes accessed | tf_op | source)
XLA Modules:
  0.0 68.3 jit_solution(814761339013177168)
XLA Ops:
  0.0 3.0 %leaves.1 = (bf16[4,64,256]{2,1,0:T(8,128)(2,1)S(1)}, bf16[4,64,256]{2,1,0:T(8,128)(2,1)S(1)}, bf16[4,192,256]{2,1,0:T(8,128)(2,1)S(1)}, bf16[4,192,256]{2,1,0:T(8,128)(2,1)S(1)}) custom-call(bf16[2048,256]{1,0:T(8,128)(2,1)} %x_hbm.1, bf16[2048,256]{1,0:T(8,128)(2,1)} %v_hbm.1), custom_call_target="tpu_custom_call" | custom-call | flops 2000000000 | tf_op jit(solution)/shard_map/leaves/pallas_call | solution.py:56
  3.0 0.5 collective-permute-start.2
  3.6 0.1 collective-permute-start
  3.6 1.6 %weights.1.w_ref.after_ref = bf16[8,512,256]{2,1,0:T(8,128)(2,1)S(1)} custom-call(bf16[4,1,1,8,512,256]{5,4,3,2,1,0:T(8,128)(2,1)} %w_ref.13, bf16[4,192,256]{2,1,0:T(8,128)(2,1)S(1)} %get-tuple-element.45.after_ref.kept_ref), custom_call_target="tpu_custom_call" | custom-call | flops 2000000000 | tf_op jit(solution)/shard_map/weights/pallas_call | solution.py:56
  5.3 0.5 merge0a.1
  5.8 3.1 %collective-permute-start.1 = (bf16[4,64,256]{2,1,0:T(8,128)(2,1)S(1)}, bf16[4,64,256]{2,1,0:T(8,128)(2,1)S(1)}, u32[]{:S(2)}, u32[]{:S(2)}) collective-permute-start(bf16[4,64,256]{2,1,0:T(8,128)(2,1)S(1)} %get-tuple-element.47), channel_id=1, source_target_pairs={{0,2},{1,3},{2,0},{3,1},{4,6},{5,7},{6,4},{7,5},{8,10},{9,11},{10,... | collective-permute-start | bytes 393224 | tf_op jit(solution)/shard_map/ppermute | solution.py:23
  8.8 0.5 merge0b.1
  9.3 0.1 collective-permute-start.4
  9.4 0.4 merge0c.1
  9.9 3.2 %collective-permute-done.1.got_ref = bf16[4,64,256]{2,1,0:T(8,128)(2,1)S(1)} collective-permute-done((bf16[4,64,256]{2,1,0:T(8,128)(2,1)S(1)}, bf16[4,64,256]{2,1,0:T(8,128)(2,1)S(1)}, u32[]{:S(2)}, u32[]{:S(2)}) %collective-permute-start.1) | collective-permute-done | bytes 131104 | tf_op jit(solution)/shard_map/ppermute | solution.py:23
  13.1 0.5 merge1a.1
  13.6 2.0 %collective-permute-start.3 = (bf16[4,64,256]{2,1,0:T(8,128)(2,1)S(1)}, bf16[4,64,256]{2,1,0:T(8,128)(2,1)S(1)}, u32[]{:S(2)}, u32[]{:S(2)}) collective-permute-start(bf16[4,64,256]{2,1,0:T(8,128)(2,1)S(1)} %get-tuple-element.52), channel_id=1, source_target_pairs={{0,8},{8,0},{16,24},{24,16},{1,9},{9,1},{17,25},{25,17},{2,10},{10... | collective-permute-start | bytes 393224 | tf_op jit(solution)/shard_map/ppermute | solution.py:23
  15.7 1.6 %collective-permute-start.7 = (bf16[4,112,256]{2,1,0:T(8,128)(2,1)S(1)}, bf16[4,112,256]{2,1,0:T(8,128)(2,1)S(1)}, u32[]{:S(2)}, u32[]{:S(2)}) collective-permute-start(bf16[4,112,256]{2,1,0:T(8,128)(2,1)S(1)} %get-tuple-element.58), channel_id=1, source_target_pairs={{0,2},{1,3},{2,0},{3,1},{4,6},{5,7},{6,4},{7,5},{8,10},{9,11},{10,... | collective-permute-start | bytes 688136 | tf_op jit(solution)/shard_map/ppermute | solution.py:23
  17.3 0.5 merge1b.1
  17.8 1.2 %collective-permute-start.6 = (bf16[4,80,256]{2,1,0:T(8,128)(2,1)S(1)}, bf16[4,80,256]{2,1,0:T(8,128)(2,1)S(1)}, u32[]{:S(2)}, u32[]{:S(2)}) collective-permute-start(bf16[4,80,256]{2,1,0:T(8,128)(2,1)S(1)} %get-tuple-element.57), channel_id=1, source_target_pairs={{0,8},{8,0},{16,24},{24,16},{1,9},{9,1},{17,25},{25,17},{2,10},{10... | collective-permute-start | bytes 491528 | tf_op jit(solution)/shard_map/ppermute | solution.py:23
  19.0 2.1 %join.1.after_ref.joint_ref = bf16[8,512,256]{2,1,0:T(8,128)(2,1)S(1)} custom-call(s32[1,1,8]{2,1,0:T(1,128)S(1)} %copy-done.2, bf16[4,1,1,8,512,256]{5,4,3,2,1,0:T(8,128)(2,1)S(1)} %bitcast.1, bf16[1,1,8,256,256]{4,3,2,1,0:T(8,128)(2,1)S(1)} %copy-done, bf16[2048,256]{1,0:T(8,128)(2,1)S(1)} %copy-done.1, ...), custom_call_target="tpu_custom_call" | custom-call | flops 2000000000 | tf_op jit(solution)/shard_map/join/pallas_call | solution.py:56
  21.1 0.5 merge2a.1
  21.6 1.7 %collective-permute-start.5 = (bf16[4,64,256]{2,1,0:T(8,128)(2,1)S(1)}, bf16[4,64,256]{2,1,0:T(8,128)(2,1)S(1)}, u32[]{:S(2)}, u32[]{:S(2)}) collective-permute-start(bf16[4,64,256]{2,1,0:T(8,128)(2,1)S(1)} %get-tuple-element.56), channel_id=1, source_target_pairs={{0,16},{8,24},{16,0},{24,8},{1,17},{9,25},{17,1},{25,9},{2,18},{10... | collective-permute-start | bytes 393224 | tf_op jit(solution)/shard_map/ppermute | solution.py:23
  23.3 0.5 merge1c.1
  23.8 1.0 %collective-permute-start.12 = (bf16[4,112,256]{2,1,0:T(8,128)(2,1)S(1)}, bf16[4,112,256]{2,1,0:T(8,128)(2,1)S(1)}, u32[]{:S(2)}, u32[]{:S(2)}) collective-permute-start(bf16[4,112,256]{2,1,0:T(8,128)(2,1)S(1)} %get-tuple-element.66), channel_id=1, source_target_pairs={{0,8},{8,0},{16,24},{24,16},{1,9},{9,1},{17,25},{25,17},{2,10},{10... | collective-permute-start | bytes 688136 | tf_op jit(solution)/shard_map/ppermute | solution.py:23
  24.9 0.5 merge2b.1
  25.4 1.3 %collective-permute-done.5.got_ref = bf16[4,64,256]{2,1,0:T(8,128)(2,1)S(1)} collective-permute-done((bf16[4,64,256]{2,1,0:T(8,128)(2,1)S(1)}, bf16[4,64,256]{2,1,0:T(8,128)(2,1)S(1)}, u32[]{:S(2)}, u32[]{:S(2)}) %collective-permute-start.5) | collective-permute-done | bytes 131104 | tf_op jit(solution)/shard_map/ppermute | solution.py:23
  26.6 1.0 %lasta.1 = (bf16[2,64,256]{2,1,0:T(8,128)(2,1)S(1)}, bf16[2,64,256]{2,1,0:T(8,128)(2,1)S(1)}, bf16[2,64,256]{2,1,0:T(8,128)(2,1)S(1)}, bf16[2,64,256]{2,1,0:T(8,128)(2,1)S(1)}) custom-call(s32[1,1,8]{2,1,0:T(1,128)S(1)} %copy-done.2, bf16[4,64,256]{2,1,0:T(8,128)(2,1)S(1)} %get-tuple-element.55.after_ref.kept_ref, ...), custom_call_target="tpu_custom_call" | custom-call | flops 2000000000 | tf_op jit(solution)/shard_map/lasta/pallas_call | solution.py:56
  27.7 1.8 %collective-permute-start.8 = (bf16[2,64,256]{2,1,0:T(8,128)(2,1)S(1)}, bf16[2,64,256]{2,1,0:T(8,128)(2,1)S(1)}, u32[]{:S(2)}, u32[]{:S(2)}) collective-permute-start(bf16[2,64,256]{2,1,0:T(8,128)(2,1)S(1)} %get-tuple-element.62), channel_id=1, source_target_pairs={{0,2},{1,3},{2,0},{3,1},{4,6},{5,7},{6,4},{7,5},{8,10},{9,11},{10,... | collective-permute-start | bytes 196616 | tf_op jit(solution)/shard_map/ppermute | solution.py:23
  29.5 2.6 %collective-permute-start.9 = (bf16[2,64,256]{2,1,0:T(8,128)(2,1)S(1)}, bf16[2,64,256]{2,1,0:T(8,128)(2,1)S(1)}, u32[]{:S(2)}, u32[]{:S(2)}) collective-permute-start(bf16[2,64,256]{2,1,0:T(8,128)(2,1)S(1)} %get-tuple-element.63), channel_id=1, source_target_pairs={{0,4},{1,5},{2,6},{3,7},{4,0},{5,1},{6,2},{7,3},{8,12},{9,13},{10,... | collective-permute-start | bytes 196616 | tf_op jit(solution)/shard_map/ppermute | solution.py:23
  32.1 0.1 collective-permute-start.10
  32.1 1.7 %collective-permute-start.11 = (bf16[4,80,256]{2,1,0:T(8,128)(2,1)S(1)}, bf16[4,80,256]{2,1,0:T(8,128)(2,1)S(1)}, u32[]{:S(2)}, u32[]{:S(2)}) collective-permute-start(bf16[4,80,256]{2,1,0:T(8,128)(2,1)S(1)} %get-tuple-element.65), channel_id=1, source_target_pairs={{0,16},{8,24},{16,0},{24,8},{1,17},{9,25},{17,1},{25,9},{2,18},{10... | collective-permute-start | bytes 491528 | tf_op jit(solution)/shard_map/ppermute | solution.py:23
  33.8 0.5 merge2c.1
  34.3 0.4 collective-permute-start.17
  34.7 2.8 %collective-permute-done.11.got_ref = bf16[4,80,256]{2,1,0:T(8,128)(2,1)S(1)} collective-permute-done((bf16[4,80,256]{2,1,0:T(8,128)(2,1)S(1)}, bf16[4,80,256]{2,1,0:T(8,128)(2,1)S(1)}, u32[]{:S(2)}, u32[]{:S(2)}) %collective-permute-start.11) | collective-permute-done | bytes 163872 | tf_op jit(solution)/shard_map/ppermute | solution.py:23
  37.4 1.0 %lastb.1 = (bf16[2,80,256]{2,1,0:T(8,128)(2,1)S(1)}, bf16[2,80,256]{2,1,0:T(8,128)(2,1)S(1)}, bf16[2,80,256]{2,1,0:T(8,128)(2,1)S(1)}, bf16[2,80,256]{2,1,0:T(8,128)(2,1)S(1)}) custom-call(s32[1,1,8]{2,1,0:T(1,128)S(1)} %copy-done.2, bf16[4,80,256]{2,1,0:T(8,128)(2,1)S(1)} %get-tuple-element.60.after_ref.kept_ref, ...), custom_call_target="tpu_custom_call" | custom-call | flops 2000000000 | tf_op jit(solution)/shard_map/lastb/pallas_call | solution.py:56
  38.5 1.8 %collective-permute-done.17.got_ref = bf16[4,112,256]{2,1,0:T(8,128)(2,1)S(1)} collective-permute-done((bf16[4,112,256]{2,1,0:T(8,128)(2,1)S(1)}, bf16[4,112,256]{2,1,0:T(8,128)(2,1)S(1)}, u32[]{:S(2)}, u32[]{:S(2)}) %collective-permute-start.17) | collective-permute-done | bytes 229408 | tf_op jit(solution)/shard_map/ppermute | solution.py:23
  40.4 1.0 %lastc.1 = (bf16[4,112,256]{2,1,0:T(8,128)(2,1)S(1)}, bf16[112,256]{1,0:T(8,128)(2,1)S(1)}, bf16[112,256]{1,0:T(8,128)(2,1)S(1)}, bf16[112,256]{1,0:T(8,128)(2,1)S(1)}, bf16[112,256]{1,0:T(8,128)(2,1)S(1)}) custom-call(s32[1,1,8]{2,1,0:T(1,128)S(1)} %copy-done.2, bf16[4,112,256]{2,1,0:T(8,128)(2,1)S(1)} %get-tuple-element.67.after_ref.kept_ref, ...), custom_call_target="tpu_custom_call" | custom-call | flops 2000000000 | tf_op jit(solution)/shard_map/lastc/pallas_call | solution.py:56
  41.4 0.1 collective-permute-start.18
  41.5 0.5 collective-permute-start.19
  42.0 0.1 collective-permute-start.20
  42.0 0.4 collective-permute-start.21
  42.5 0.7 collective-permute-start.14
  43.2 3.5 %collective-permute-start.15 = (bf16[2,80,256]{2,1,0:T(8,128)(2,1)S(1)}, bf16[2,80,256]{2,1,0:T(8,128)(2,1)S(1)}, u32[]{:S(2)}, u32[]{:S(2)}) collective-permute-start(bf16[2,80,256]{2,1,0:T(8,128)(2,1)S(1)} %get-tuple-element.70), channel_id=1, source_target_pairs={{0,4},{1,5},{2,6},{3,7},{4,0},{5,1},{6,2},{7,3},{8,12},{9,13},{10,... | collective-permute-start | bytes 245768 | tf_op jit(solution)/shard_map/ppermute | solution.py:23
  46.6 0.2 collective-permute-start.16
  46.9 6.2 %collective-permute-done.15.refs_2_.refs_7_ = bf16[2,80,256]{2,1,0:T(8,128)(2,1)S(1)} collective-permute-done((bf16[2,80,256]{2,1,0:T(8,128)(2,1)S(1)}, bf16[2,80,256]{2,1,0:T(8,128)(2,1)S(1)}, u32[]{:S(2)}, u32[]{:S(2)}) %collective-permute-start.15) | collective-permute-done | bytes 81952 | tf_op jit(solution)/shard_map/ppermute | solution.py:23
  53.2 0.1 collective-permute-start.22
  53.2 0.5 collective-permute-start.13
  53.7 2.9 %collective-permute-start.24 = (bf16[2,112,256]{2,1,0:T(8,128)(2,1)S(1)}, bf16[2,112,256]{2,1,0:T(8,128)(2,1)S(1)}, u32[]{:S(2)}, u32[]{:S(2)}) collective-permute-start(bf16[2,112,256]{2,1,0:T(8,128)(2,1)S(1)} %get-tuple-element.79), channel_id=1, source_target_pairs={{0,4},{1,5},{2,6},{3,7},{4,0},{5,1},{6,2},{7,3},{8,12},{9,13},{10,... | collective-permute-start | bytes 344072 | tf_op jit(solution)/shard_map/ppermute | solution.py:23
  56.7 1.2 %collective-permute-start.25 = (bf16[2,112,256]{2,1,0:T(8,128)(2,1)S(1)}, bf16[2,112,256]{2,1,0:T(8,128)(2,1)S(1)}, u32[]{:S(2)}, u32[]{:S(2)}) collective-permute-start(bf16[2,112,256]{2,1,0:T(8,128)(2,1)S(1)} %get-tuple-element.80), channel_id=1, source_target_pairs={{0,6},{1,7},{2,4},{3,5},{4,2},{5,3},{6,0},{7,1},{8,14},{9,15},{10,... | collective-permute-start | bytes 344072 | tf_op jit(solution)/shard_map/ppermute | solution.py:23
  57.8 7.7 %collective-permute-done.24.refs_13_ = bf16[2,112,256]{2,1,0:T(8,128)(2,1)S(1)} collective-permute-done((bf16[2,112,256]{2,1,0:T(8,128)(2,1)S(1)}, bf16[2,112,256]{2,1,0:T(8,128)(2,1)S(1)}, u32[]{:S(2)}, u32[]{:S(2)}) %collective-permute-start.24) | collective-permute-done | bytes 114720 | tf_op jit(solution)/shard_map/ppermute | solution.py:23
  65.6 0.8 %collective-permute-done.23.refs_12_ = bf16[2,112,256]{2,1,0:T(8,128)(2,1)S(1)} collective-permute-done((bf16[2,112,256]{2,1,0:T(8,128)(2,1)S(1)}, bf16[2,112,256]{2,1,0:T(8,128)(2,1)S(1)}, u32[]{:S(2)}, u32[]{:S(2)}) %collective-permute-start.23) | collective-permute-done | bytes 114720 | tf_op jit(solution)/shard_map/ppermute | solution.py:23
  66.3 2.0 %place.1 = bf16[2048,256]{1,0:T(8,128)(2,1)} custom-call(bf16[2,64,256]{2,1,0:T(8,128)(2,1)S(1)} %get-tuple-element.61.after_ref.refs_0_, bf16[2,64,256]{2,1,0:T(8,128)(2,1)S(1)} %collective-permute-done.8.refs_1_, bf16[2,64,256]{2,1,0:T(8,128)(2,1)S(1)} %collective-permute-done.9.refs_2_, bf16[2,64,256]{2,1,0:T(8,128)(2,1)S(1)} %collective-permute-done.10.refs_3_, ...), custom_call_target="tpu_custom_call" | custom-call | flops 2000000000 | tf_op jit(solution)/shard_map/place/pallas_call | solution.py:56
  (34 shorter events, 0.1 us)
Async XLA Ops:
  3.0 5.8 %collective-permute-start.2 = (bf16[4,192,256]{2,1,0:T(8,128)(2,1)S(1)}, bf16[4,192,256]{2,1,0:T(8,128)(2,1)S(1)}, u32[]{:S(2)}, u32[]{:S(2)}) collective-permute-start(bf16[4,192,256]{2,1,0:T(8,128)(2,1)S(1)} %get-tuple-element.48), channel_id=1, source_target_pairs={{0,1},{1,0},{2,3},{3,2},{4,5},{5,4},{6,7},{7,6},{8,9},{9,8},{10,11... | collective-permute-start | bytes 1179656 | tf_op jit(solution)/shard_map/ppermute | solution.py:23
  3.6 1.7 %collective-permute-start = (bf16[4,64,256]{2,1,0:T(8,128)(2,1)S(1)}, bf16[4,64,256]{2,1,0:T(8,128)(2,1)S(1)}, u32[]{:S(2)}, u32[]{:S(2)}) collective-permute-start(bf16[4,64,256]{2,1,0:T(8,128)(2,1)S(1)} %get-tuple-element.44), channel_id=1, source_target_pairs={{0,1},{1,0},{2,3},{3,2},{4,5},{5,4},{6,7},{7,6},{8,9},{9,8},{10,11... | collective-permute-start | bytes 393224 | tf_op jit(solution)/shard_map/ppermute | solution.py:23
  5.3 7.9 %slice-start = ((s8[8388608]{0:T(1024)(128)(4,1)}), s8[4194304]{0:T(1024)(128)(4,1)S(1)}, s32[]{:S(2)}) async-start(s8[8388608]{0:T(1024)(128)(4,1)} %bitcast), calls=%async_computation | async-start | bytes 8388608
  5.8 7.4 %collective-permute-start.1 = (bf16[4,64,256]{2,1,0:T(8,128)(2,1)S(1)}, bf16[4,64,256]{2,1,0:T(8,128)(2,1)S(1)}, u32[]{:S(2)}, u32[]{:S(2)}) collective-permute-start(bf16[4,64,256]{2,1,0:T(8,128)(2,1)S(1)} %get-tuple-element.47), channel_id=1, source_target_pairs={{0,2},{1,3},{2,0},{3,1},{4,6},{5,7},{6,4},{7,5},{8,10},{9,11},{10,... | collective-permute-start | bytes 393224 | tf_op jit(solution)/shard_map/ppermute | solution.py:23
  8.8 4.3 %slice-start.1 = ((s8[8388608]{0:T(1024)(128)(4,1)}), s8[4194304]{0:T(1024)(128)(4,1)S(1)}, s32[]{:S(2)}) async-start(s8[8388608]{0:T(1024)(128)(4,1)} %bitcast), calls=%async_computation.1 | async-start | bytes 8388608
  9.3 7.9 %collective-permute-start.4 = (bf16[4,80,256]{2,1,0:T(8,128)(2,1)S(1)}, bf16[4,80,256]{2,1,0:T(8,128)(2,1)S(1)}, u32[]{:S(2)}, u32[]{:S(2)}) collective-permute-start(bf16[4,80,256]{2,1,0:T(8,128)(2,1)S(1)} %get-tuple-element.53), channel_id=1, source_target_pairs={{0,2},{1,3},{2,0},{3,1},{4,6},{5,7},{6,4},{7,5},{8,10},{9,11},{10,... | collective-permute-start | bytes 491528 | tf_op jit(solution)/shard_map/ppermute | solution.py:23
  13.6 7.4 %collective-permute-start.3 = (bf16[4,64,256]{2,1,0:T(8,128)(2,1)S(1)}, bf16[4,64,256]{2,1,0:T(8,128)(2,1)S(1)}, u32[]{:S(2)}, u32[]{:S(2)}) collective-permute-start(bf16[4,64,256]{2,1,0:T(8,128)(2,1)S(1)} %get-tuple-element.52), channel_id=1, source_target_pairs={{0,8},{8,0},{16,24},{24,16},{1,9},{9,1},{17,25},{25,17},{2,10},{10... | collective-permute-start | bytes 393224 | tf_op jit(solution)/shard_map/ppermute | solution.py:23
  15.7 7.7 %collective-permute-start.7 = (bf16[4,112,256]{2,1,0:T(8,128)(2,1)S(1)}, bf16[4,112,256]{2,1,0:T(8,128)(2,1)S(1)}, u32[]{:S(2)}, u32[]{:S(2)}) collective-permute-start(bf16[4,112,256]{2,1,0:T(8,128)(2,1)S(1)} %get-tuple-element.58), channel_id=1, source_target_pairs={{0,2},{1,3},{2,0},{3,1},{4,6},{5,7},{6,4},{7,5},{8,10},{9,11},{10,... | collective-permute-start | bytes 688136 | tf_op jit(solution)/shard_map/ppermute | solution.py:23
  17.2 1.7 %copy-start = (bf16[1,1,8,256,256]{4,3,2,1,0:T(8,128)(2,1)S(1)}, bf16[1,1,8,256,256]{4,3,2,1,0:T(8,128)(2,1)}, u32[]{:S(2)}) copy-start(bf16[1,1,8,256,256]{4,3,2,1,0:T(8,128)(2,1)} %core_ref.1) | copy-start | bytes 3145732
  17.3 1.7 %copy-start.1 = (bf16[2048,256]{1,0:T(8,128)(2,1)S(1)}, bf16[2048,256]{1,0:T(8,128)(2,1)}, u32[]{:S(2)}) copy-start(bf16[2048,256]{1,0:T(8,128)(2,1)} %u_ref.1) | copy-start | bytes 3145732
  17.3 1.7 %copy-start.2 = (s32[1,1,8]{2,1,0:T(1,128)S(1)}, s32[1,1,8]{2,1,0:T(1,128)}, u32[]{:S(2)}) copy-start(s32[1,1,8]{2,1,0:T(1,128)} %order_ref.7) | copy-start | bytes 100
  17.8 7.1 %collective-permute-start.6 = (bf16[4,80,256]{2,1,0:T(8,128)(2,1)S(1)}, bf16[4,80,256]{2,1,0:T(8,128)(2,1)S(1)}, u32[]{:S(2)}, u32[]{:S(2)}) collective-permute-start(bf16[4,80,256]{2,1,0:T(8,128)(2,1)S(1)} %get-tuple-element.57), channel_id=1, source_target_pairs={{0,8},{8,0},{16,24},{24,16},{1,9},{9,1},{17,25},{25,17},{2,10},{10... | collective-permute-start | bytes 491528 | tf_op jit(solution)/shard_map/ppermute | solution.py:23
  21.6 5.0 %collective-permute-start.5 = (bf16[4,64,256]{2,1,0:T(8,128)(2,1)S(1)}, bf16[4,64,256]{2,1,0:T(8,128)(2,1)S(1)}, u32[]{:S(2)}, u32[]{:S(2)}) collective-permute-start(bf16[4,64,256]{2,1,0:T(8,128)(2,1)S(1)} %get-tuple-element.56), channel_id=1, source_target_pairs={{0,16},{8,24},{16,0},{24,8},{1,17},{9,25},{17,1},{25,9},{2,18},{10... | collective-permute-start | bytes 393224 | tf_op jit(solution)/shard_map/ppermute | solution.py:23
  23.8 10.0 %collective-permute-start.12 = (bf16[4,112,256]{2,1,0:T(8,128)(2,1)S(1)}, bf16[4,112,256]{2,1,0:T(8,128)(2,1)S(1)}, u32[]{:S(2)}, u32[]{:S(2)}) collective-permute-start(bf16[4,112,256]{2,1,0:T(8,128)(2,1)S(1)} %get-tuple-element.66), channel_id=1, source_target_pairs={{0,8},{8,0},{16,24},{24,16},{1,9},{9,1},{17,25},{25,17},{2,10},{10... | collective-permute-start | bytes 688136 | tf_op jit(solution)/shard_map/ppermute | solution.py:23
  27.7 10.8 %collective-permute-start.8 = (bf16[2,64,256]{2,1,0:T(8,128)(2,1)S(1)}, bf16[2,64,256]{2,1,0:T(8,128)(2,1)S(1)}, u32[]{:S(2)}, u32[]{:S(2)}) collective-permute-start(bf16[2,64,256]{2,1,0:T(8,128)(2,1)S(1)} %get-tuple-element.62), channel_id=1, source_target_pairs={{0,2},{1,3},{2,0},{3,1},{4,6},{5,7},{6,4},{7,5},{8,10},{9,11},{10,... | collective-permute-start | bytes 196616 | tf_op jit(solution)/shard_map/ppermute | solution.py:23
  29.5 9.0 %collective-permute-start.9 = (bf16[2,64,256]{2,1,0:T(8,128)(2,1)S(1)}, bf16[2,64,256]{2,1,0:T(8,128)(2,1)S(1)}, u32[]{:S(2)}, u32[]{:S(2)}) collective-permute-start(bf16[2,64,256]{2,1,0:T(8,128)(2,1)S(1)} %get-tuple-element.63), channel_id=1, source_target_pairs={{0,4},{1,5},{2,6},{3,7},{4,0},{5,1},{6,2},{7,3},{8,12},{9,13},{10,... | collective-permute-start | bytes 196616 | tf_op jit(solution)/shard_map/ppermute | solution.py:23
  32.1 6.5 %collective-permute-start.10 = (bf16[2,64,256]{2,1,0:T(8,128)(2,1)S(1)}, bf16[2,64,256]{2,1,0:T(8,128)(2,1)S(1)}, u32[]{:S(2)}, u32[]{:S(2)}) collective-permute-start(bf16[2,64,256]{2,1,0:T(8,128)(2,1)S(1)} %get-tuple-element.64), channel_id=1, source_target_pairs={{0,6},{1,7},{2,4},{3,5},{4,2},{5,3},{6,0},{7,1},{8,14},{9,15},{10,... | collective-permute-start | bytes 196616 | tf_op jit(solution)/shard_map/ppermute | solution.py:23
  32.1 5.3 %collective-permute-start.11 = (bf16[4,80,256]{2,1,0:T(8,128)(2,1)S(1)}, bf16[4,80,256]{2,1,0:T(8,128)(2,1)S(1)}, u32[]{:S(2)}, u32[]{:S(2)}) collective-permute-start(bf16[4,80,256]{2,1,0:T(8,128)(2,1)S(1)} %get-tuple-element.65), channel_id=1, source_target_pairs={{0,16},{8,24},{16,0},{24,8},{1,17},{9,25},{17,1},{25,9},{2,18},{10... | collective-permute-start | bytes 491528 | tf_op jit(solution)/shard_map/ppermute | solution.py:23
  34.3 6.1 %collective-permute-start.17 = (bf16[4,112,256]{2,1,0:T(8,128)(2,1)S(1)}, bf16[4,112,256]{2,1,0:T(8,128)(2,1)S(1)}, u32[]{:S(2)}, u32[]{:S(2)}) collective-permute-start(bf16[4,112,256]{2,1,0:T(8,128)(2,1)S(1)} %get-tuple-element.72), channel_id=1, source_target_pairs={{0,16},{8,24},{16,0},{24,8},{1,17},{9,25},{17,1},{25,9},{2,18},{10... | collective-permute-start | bytes 688136 | tf_op jit(solution)/shard_map/ppermute | solution.py:23
  41.4 1.8 %collective-permute-start.18 = (bf16[112,256]{1,0:T(8,128)(2,1)S(1)}, bf16[112,256]{1,0:T(8,128)(2,1)S(1)}, u32[]{:S(2)}, u32[]{:S(2)}) collective-permute-start(bf16[112,256]{1,0:T(8,128)(2,1)S(1)} %get-tuple-element.74), channel_id=1, source_target_pairs={{0,1},{1,0},{2,3},{3,2},{4,5},{5,4},{6,7},{7,6},{8,9},{9,8},{10,11... | collective-permute-start | bytes 172040 | tf_op jit(solution)/shard_map/ppermute | solution.py:23
  41.5 5.2 %collective-permute-start.19 = (bf16[112,256]{1,0:T(8,128)(2,1)S(1)}, bf16[112,256]{1,0:T(8,128)(2,1)S(1)}, u32[]{:S(2)}, u32[]{:S(2)}) collective-permute-start(bf16[112,256]{1,0:T(8,128)(2,1)S(1)} %get-tuple-element.75), channel_id=1, source_target_pairs={{0,1},{1,0},{2,3},{3,2},{4,5},{5,4},{6,7},{7,6},{8,9},{9,8},{10,11... | collective-permute-start | bytes 172040 | tf_op jit(solution)/shard_map/ppermute | solution.py:23
  42.0 4.9 %collective-permute-start.20 = (bf16[112,256]{1,0:T(8,128)(2,1)S(1)}, bf16[112,256]{1,0:T(8,128)(2,1)S(1)}, u32[]{:S(2)}, u32[]{:S(2)}) collective-permute-start(bf16[112,256]{1,0:T(8,128)(2,1)S(1)} %get-tuple-element.76), channel_id=1, source_target_pairs={{0,1},{1,0},{2,3},{3,2},{4,5},{5,4},{6,7},{7,6},{8,9},{9,8},{10,11... | collective-permute-start | bytes 172040 | tf_op jit(solution)/shard_map/ppermute | solution.py:23
  42.0 4.8 %collective-permute-start.21 = (bf16[112,256]{1,0:T(8,128)(2,1)S(1)}, bf16[112,256]{1,0:T(8,128)(2,1)S(1)}, u32[]{:S(2)}, u32[]{:S(2)}) collective-permute-start(bf16[112,256]{1,0:T(8,128)(2,1)S(1)} %get-tuple-element.77), channel_id=1, source_target_pairs={{0,1},{1,0},{2,3},{3,2},{4,5},{5,4},{6,7},{7,6},{8,9},{9,8},{10,11... | collective-permute-start | bytes 172040 | tf_op jit(solution)/shard_map/ppermute | solution.py:23
  42.5 4.4 %collective-permute-start.14 = (bf16[2,80,256]{2,1,0:T(8,128)(2,1)S(1)}, bf16[2,80,256]{2,1,0:T(8,128)(2,1)S(1)}, u32[]{:S(2)}, u32[]{:S(2)}) collective-permute-start(bf16[2,80,256]{2,1,0:T(8,128)(2,1)S(1)} %get-tuple-element.69), channel_id=1, source_target_pairs={{0,2},{1,3},{2,0},{3,1},{4,6},{5,7},{6,4},{7,5},{8,10},{9,11},{10,... | collective-permute-start | bytes 245768 | tf_op jit(solution)/shard_map/ppermute | solution.py:23
  43.2 10.0 %collective-permute-start.15 = (bf16[2,80,256]{2,1,0:T(8,128)(2,1)S(1)}, bf16[2,80,256]{2,1,0:T(8,128)(2,1)S(1)}, u32[]{:S(2)}, u32[]{:S(2)}) collective-permute-start(bf16[2,80,256]{2,1,0:T(8,128)(2,1)S(1)} %get-tuple-element.70), channel_id=1, source_target_pairs={{0,4},{1,5},{2,6},{3,7},{4,0},{5,1},{6,2},{7,3},{8,12},{9,13},{10,... | collective-permute-start | bytes 245768 | tf_op jit(solution)/shard_map/ppermute | solution.py:23
  46.6 6.5 %collective-permute-start.16 = (bf16[2,80,256]{2,1,0:T(8,128)(2,1)S(1)}, bf16[2,80,256]{2,1,0:T(8,128)(2,1)S(1)}, u32[]{:S(2)}, u32[]{:S(2)}) collective-permute-start(bf16[2,80,256]{2,1,0:T(8,128)(2,1)S(1)} %get-tuple-element.71), channel_id=1, source_target_pairs={{0,6},{1,7},{2,4},{3,5},{4,2},{5,3},{6,0},{7,1},{8,14},{9,15},{10,... | collective-permute-start | bytes 245768 | tf_op jit(solution)/shard_map/ppermute | solution.py:23
  53.2 13.2 %collective-permute-start.22 = (bf16[4,80,256]{2,1,0:T(8,128)(2,1)S(1)}, bf16[4,80,256]{2,1,0:T(8,128)(2,1)S(1)}, u32[]{:S(2)}, u32[]{:S(2)}) collective-permute-start(bf16[4,80,256]{2,1,0:T(8,128)(2,1)S(1)} %packb.1), channel_id=1, source_target_pairs={{0,1},{1,0},{2,3},{3,2},{4,5},{5,4},{6,7},{7,6},{8,9},{9,8},{10,11... | collective-permute-start | bytes 491528 | tf_op jit(solution)/shard_map/ppermute | solution.py:23
  53.2 4.6 %collective-permute-start.13 = (bf16[4,64,256]{2,1,0:T(8,128)(2,1)S(1)}, bf16[4,64,256]{2,1,0:T(8,128)(2,1)S(1)}, u32[]{:S(2)}, u32[]{:S(2)}) collective-permute-start(bf16[4,64,256]{2,1,0:T(8,128)(2,1)S(1)} %packa.1.after_ref), channel_id=1, source_target_pairs={{0,1},{1,0},{2,3},{3,2},{4,5},{5,4},{6,7},{7,6},{8,9},{9,8},{10,11... | collective-permute-start | bytes 393224 | tf_op jit(solution)/shard_map/ppermute | solution.py:23
  53.7 11.8 %collective-permute-start.24 = (bf16[2,112,256]{2,1,0:T(8,128)(2,1)S(1)}, bf16[2,112,256]{2,1,0:T(8,128)(2,1)S(1)}, u32[]{:S(2)}, u32[]{:S(2)}) collective-permute-start(bf16[2,112,256]{2,1,0:T(8,128)(2,1)S(1)} %get-tuple-element.79), channel_id=1, source_target_pairs={{0,4},{1,5},{2,6},{3,7},{4,0},{5,1},{6,2},{7,3},{8,12},{9,13},{10,... | collective-permute-start | bytes 344072 | tf_op jit(solution)/shard_map/ppermute | solution.py:23
  56.7 8.9 %collective-permute-start.25 = (bf16[2,112,256]{2,1,0:T(8,128)(2,1)S(1)}, bf16[2,112,256]{2,1,0:T(8,128)(2,1)S(1)}, u32[]{:S(2)}, u32[]{:S(2)}) collective-permute-start(bf16[2,112,256]{2,1,0:T(8,128)(2,1)S(1)} %get-tuple-element.80), channel_id=1, source_target_pairs={{0,6},{1,7},{2,4},{3,5},{4,2},{5,3},{6,0},{7,1},{8,14},{9,15},{10,... | collective-permute-start | bytes 344072 | tf_op jit(solution)/shard_map/ppermute | solution.py:23
  57.8 8.5 %collective-permute-start.23 = (bf16[2,112,256]{2,1,0:T(8,128)(2,1)S(1)}, bf16[2,112,256]{2,1,0:T(8,128)(2,1)S(1)}, u32[]{:S(2)}, u32[]{:S(2)}) collective-permute-start(bf16[2,112,256]{2,1,0:T(8,128)(2,1)S(1)} %get-tuple-element.78.refs_4_), channel_id=1, source_target_pairs={{0,2},{1,3},{2,0},{3,1},{4,6},{5,7},{6,4},{7,5},{8,10},{9,11},{10,... | collective-permute-start | bytes 344072 | tf_op jit(solution)/shard_map/ppermute | solution.py:23

commit v3 on v2

--- a/solution.py
+++ b/solution.py
@@ -9,8 +9,8 @@
 
 INNER_LEVELS = 2
 PARTS = (4, 5, 7)
-COSTS = {}
-ORDER = ("f", "w", "m0a", "m0b", "m0c", "m1a", "m1b", "j", "m2a", "m1c", "m2b", "oa", "m2c", "ob", "qa", "ec", "pc", "qb")
+COSTS = {"merge2c":.4,"lastb":.1,"lastc":.4,"packc":0,"lasta":1,"packa":2,"packb":1,"merge1b":.4,"join":.3,"inside":.3,"merge2a":.4,"merge1a":1}
+ORDER = ("f", "w", "m0a", "m0b", "m0c", "i", "m1a", "m1b", "j", "m2a", "m1c", "m2b", "oa", "m2c", "ob", "qa", "oc", "qb", "rc")
 LEAF_ROOM = 52
 LOAD_ROOM = 48
 HBM = pl.BlockSpec(memory_space=pltpu.HBM)
@@ -19,6 +19,10 @@
 SMEM = pl.BlockSpec(memory_space=pltpu.SMEM)
 
 
+def turns(count):
+    return sorted(range(1, count), key=lambda t: (t < count // 2, t))
+
+
 def swapped(array, axis, step):
     return lax.ppermute(array, axis, [(i, i ^ step) for i in range(lax.axis_size(axis))])
 
@@ -40,13 +44,13 @@
     return lax.dot_general(a, b, (dims, ((), ())), preferred_element_type=jnp.float32)
 
 
-def call(kernel, outs, ins, specs, scratch=(), name=None, room=24):
+def call(kernel, outs, ins, specs, scratch=(), name=None, room=24, out_spec=VMEM):
     run = pl.pallas_call(
         kernel,
         name=name,
         out_shape=outs,
         in_specs=specs,
-        out_specs=[VMEM] * len(outs),
+        out_specs=[out_spec] * len(outs),
         scratch_shapes=list(scratch),
         compiler_params=pltpu.CompilerParams(vmem_limit_bytes=room * 1024 * 1024),
         cost_estimate=pl.CostEstimate(
@@ -98,13 +102,19 @@
             outs[2 * n + (slot >= half)][slot % half] = state[begin : begin + size]
 
 
-def join_kernel(level, order_ref, w_ref, core_ref, u_ref, after_ref, joint_out):
-    width = joint_out.shape[2]
-    for n in range(joint_out.shape[0]):
+def inside_kernel(core_ref, u_ref, after_ref, out):
+    width = out.shape[2]
+    for n in range(out.shape[0]):
         box = n * width // (u_ref.shape[0] // core_ref.shape[2])
         inside = dot(core_ref[0, 0, box], u_ref[n * width : (n + 1) * width, :], ((1,), (1,)))
-        joint = dot(w_ref[level, 0, 0, order_ref[0, 0, box]], inside.astype(jnp.bfloat16))
-        joint_out[n] = joint.astype(jnp.bfloat16)
+        out[n] = inside.astype(jnp.bfloat16)
+
+
+def join_kernel(level, order_ref, w_ref, inside_ref, after_ref, out):
+    per_box = inside_ref.shape[0] // w_ref.shape[3]
+    for n in range(out.shape[0]):
+        joint = dot(w_ref[level, 0, 0, order_ref[0, 0, n // per_box]], inside_ref[n])
+        out[n] = joint.astype(jnp.bfloat16)
 
 
 def merged(level, begin, size, kept_ref, got_ref, w_ref, k, box):
@@ -129,7 +139,7 @@
 
 
 def last_kernel(
-    level, early, begin, size, order_ref, kept_ref, got_ref, joint_ref, after_ref, *outs
+    level, begin, size, order_ref, kept_ref, got_ref, joint_ref, after_ref, *outs
 ):
     half = kept_ref.shape[0]
     me = lax.axis_index("inner")
@@ -139,7 +149,7 @@
     per_box = joint_ref.shape[0] // (2 * half)
     for t in range(pieces // 2):
         for odd in range(2):
-            out = (outs[1 + t] if odd else outs[0].at[t]) if early else outs[t].at[odd]
+            out = outs[t].at[odd]
             first = jnp.bitwise_xor(me, 2 * t + odd) * (piece // width)
             for n in range(piece // width):
                 k = order_ref[0, 0, (first + n) // per_box] // 2
@@ -148,38 +158,32 @@
                 )
 
 
-def early_pack_kernel(mine_ref, *refs):
-    count = mine_ref.shape[0]
-    for t, out in enumerate(refs[count + 1 :], 1):
-        out[0] = mine_ref[t]
-        out[1] = refs[t][...]
-
-
-def late_pack_kernel(*refs):
+def pack_kernel(*refs):
     out = refs[-1]
-    for t, ref in enumerate(refs[:-2]):
-        out[t] = ref[1]
-
-
-def place_kernel(cuts, *refs):
-    out, ins = refs[-1], refs[:-1]
+    for t in range(out.shape[0]):
+        out[t] = refs[t][1]
+
+
+def place_kernel(cuts, counts, *refs):
+    out, held, sems = refs[-3:]
+    rows = refs[0].shape[2]
+    owners = out.shape[0] // rows
     me = lax.axis_index("inner")
-    rows = ins[0].shape[2]
-    per = out.shape[0] // rows // 2 + 1
-    for n, (begin, size) in enumerate(cuts):
-        chunk = ins[n * per : (n + 1) * per]
-        last = n == len(cuts) - 1
-        for t in range(per - 1):
-            for odd in range(2):
-                if last:
-                    block = chunk[t + 1][odd]
-                    if t == 0:
-                        block = chunk[1][...] if odd else chunk[0][0]
-                else:
-                    block = chunk[per - 1][t] if odd else chunk[t][0]
-                owner = jnp.bitwise_xor(me, 2 * t + odd)
-                window = pl.ds(pl.multiple_of(owner * rows, rows), rows)
-                out[window, begin : begin + size] = block.T
+    copies = []
+    for step in range(owners):
+        owner = jnp.bitwise_xor(me, step)
+        window = pl.ds(pl.multiple_of(owner * rows, rows), rows)
+        for n, (begin, size) in enumerate(cuts):
+            chunk = refs[sum(counts[:n]) : sum(counts[: n + 1])]
+            block = chunk[step // 2][0]
+            if step % 2:
+                late = [(ref, t) for ref in chunk[owners // 2 :] for t in range(ref.shape[0])]
+                ref, t = late[step // 2]
+                block = ref[t]
+            held[step, :, begin : begin + size] = block.T
+        copies += copy_all([pltpu.make_async_copy(held.at[step], out.at[window], sems.at[step])])
+    for copy in copies:
+        copy.wait()
 
 
 def on_device(vectors, leaf_basis, transfer, core_mats, row_basis, box_order):
@@ -196,7 +200,7 @@
     count = len(cuts)
     held = [None] * count
     done = [None] * count
-    level_w = joint = after = None
+    level_w = inside = joint = after = None
 
     for step in ORDER:
         kind, n = step[0], "abcdefgh".find(step[-1])
@@ -230,12 +234,21 @@
                 room=LOAD_ROOM,
             )[0]
             after = level_w
+        elif kind == "i":
+            inside = call(
+                inside_kernel,
+                [arr(vectors.shape[0] // width, rank, width)],
+                [core_mats, row_basis, after],
+                [VMEM, VMEM, ANY],
+                name="inside",
+            )[0]
+            after = inside
         elif kind == "j":
             joint = call(
                 functools.partial(join_kernel, levels - 1),
                 [arr(vectors.shape[0] // width, 2 * rank, width)],
-                [box_order, transfer, core_mats, row_basis, after],
-                [SMEM, VMEM, VMEM, VMEM, ANY],
+                [box_order, transfer, inside, after],
+                [SMEM, VMEM, VMEM, ANY],
                 name="join",
             )[0]
             after = joint
@@ -253,52 +266,44 @@
             after = kept
             axis, bit = level_axis(level + 1)
             held[n] = (kept, swapped(sent, axis, 1 << bit), 0)
-        elif kind in "eo":
+        elif kind == "o":
             size = cuts[n][1]
             kept, got, begin = held[n]
-            early = kind == "e"
-            shapes = [arr(2, size, piece)] * (inner // 2)
-            if early:
-                shapes = [arr(inner // 2, size, piece)] + [arr(size, piece)] * (inner // 2)
             outs = call(
-                functools.partial(last_kernel, levels - 1, early, begin, size),
-                shapes,
+                functools.partial(last_kernel, levels - 1, begin, size),
+                [arr(2, size, piece)] * (inner // 2),
                 [box_order, kept, got, joint, after],
                 [SMEM, VMEM, VMEM, VMEM, ANY],
                 name=f"last{step[-1]}",
             )
             after = outs[0]
-            if early:
-                done[n] = outs[:1] + [swapped(x, "inner", 1) for x in outs[1:]]
-            else:
-                done[n] = outs[:1] + [swapped(x, "inner", 2 * t) for t, x in enumerate(outs[1:], 1)]
-        elif kind == "p":
-            outs = call(
-                early_pack_kernel,
-                [arr(2, cuts[n][1], piece)] * (inner // 2 - 1),
-                done[n] + [after],
-                [VMEM] * len(done[n]) + [ANY],
-                name=f"pack{step[-1]}",
-            )
-            after = outs[0]
-            done[n] = done[n][:2] + [swapped(x, "inner", 2 * t) for t, x in enumerate(outs, 1)]
-        elif kind == "q":
-            cross = call(
-                late_pack_kernel,
-                [arr(inner // 2, cuts[n][1], piece)],
-                done[n] + [after],
-                [VMEM] * len(done[n]) + [ANY],
-                name=f"pack{step[-1]}",
-            )[0]
-            after = cross
-            done[n].append(swapped(cross, "inner", 1))
+            sent = [None] * (inner // 2)
+            for t in turns(inner // 2):
+                sent[t] = swapped(outs[t], "inner", 2 * t)
+            done[n] = [outs[0]] + sent[1:]
+        elif kind in "qr":
+            groups = [done[n]] if kind == "q" else [[x] for x in done[n]]
+            for group in groups:
+                after = call(
+                    pack_kernel,
+                    [arr(len(group), cuts[n][1], piece)],
+                    group + [after],
+                    [VMEM] * len(group) + [ANY],
+                    name=f"pack{step[-1]}",
+                )[0]
+                done[n] = done[n] + [swapped(after, "inner", 1)]
     flat = [x for part in done for x in part]
     return call(
-        functools.partial(place_kernel, cuts),
+        functools.partial(place_kernel, cuts, [len(part) for part in done]),
         [arr(*vectors.shape)],
         flat,
         [VMEM] * len(flat),
+        [
+            pltpu.VMEM((inner, piece, columns), jnp.bfloat16),
+            pltpu.SemaphoreType.DMA((inner,)),
+        ],
         name="place",
+        out_spec=HBM,
     )[0]
 
 

time: 68.5 us -> 57.7 us (0.84)
  waiting for transfers between devices: 23.8 us -> 12.7 us
  starting transfers between devices: 28 us -> 28.9 us
    ppermute x26, waiting for transfers between devices: 23.8 us -> 12.7 us  [swapped(): lax.ppermute(array, axis, [(i, i ^ step) for i in range(lax.axis_size(axi...]
    ppermute x26, starting transfers between devices: 28 us -> 28.9 us  [swapped(): lax.ppermute(array, axis, [(i, i ^ step) for i in range(lax.axis_size(axi...]
    pallas_call x19 -> x23, Pallas kernels: 16.3 us -> 15.7 us  [call(): return list(run(*ins))]
  transfers between devices with their start and end apart: 26 -> 26, of which waited for: 7 -> 8; matrix products, arithmetic and copies ran while one was open for 0% -> 0% of each run, Pallas kernels for 15% -> 19%
where the time goes in v3:
time: 57.7 us; the launch traced here: 57.6 us
  starting transfers between devices  28.9 us (50%)
  Pallas kernels  15.7 us (27%)
  waiting for transfers between devices  12.7 us (22%)
    ppermute x26, starting transfers between devices, swapped(): lax.ppermute(array, axis, [(i, i ^ step) for i in range(lax.axis_size(axi...  28.9 us
    pallas_call x23, Pallas kernels, call(): return list(run(*ins))  15.7 us
    ppermute x26, waiting for transfers between devices, swapped(): lax.ppermute(array, axis, [(i, i ^ step) for i in range(lax.axis_size(axi...  12.7 us
  transfers between devices with their start and end apart: 26, of which 8 were waited for; matrix products, arithmetic and copies ran while one was open for 0% of the time, Pallas kernels for 19%

profile of v3, /device:TPU:0, one launch (start us, length us, event | category | flops | bytes accessed | tf_op | source)
XLA Modules:
  0.0 57.6 jit_solution(13427979232048714512)
XLA Ops:
  0.0 3.0 %leaves.1 = (bf16[4,64,256]{2,1,0:T(8,128)(2,1)S(1)}, bf16[4,64,256]{2,1,0:T(8,128)(2,1)S(1)}, bf16[4,192,256]{2,1,0:T(8,128)(2,1)S(1)}, bf16[4,192,256]{2,1,0:T(8,128)(2,1)S(1)}) custom-call(bf16[2048,256]{1,0:T(8,128)(2,1)} %x_hbm.1, bf16[2048,256]{1,0:T(8,128)(2,1)} %v_hbm.1), custom_call_target="tpu_custom_call" | custom-call | flops 2000000000 | tf_op jit(solution)/shard_map/leaves/pallas_call | solution.py:60
  3.0 0.5 collective-permute-start.2
  3.6 0.1 collective-permute-start
  3.6 1.6 %weights.1.w_ref.after_ref = bf16[8,512,256]{2,1,0:T(8,128)(2,1)S(1)} custom-call(bf16[4,1,1,8,512,256]{5,4,3,2,1,0:T(8,128)(2,1)} %w_ref.13, bf16[4,192,256]{2,1,0:T(8,128)(2,1)S(1)} %get-tuple-element.41.after_ref.kept_ref), custom_call_target="tpu_custom_call" | custom-call | flops 2000000000 | tf_op jit(solution)/shard_map/weights/pallas_call | solution.py:60
  5.3 0.5 merge0a.1
  5.8 3.1 %collective-permute-start.1 = (bf16[4,64,256]{2,1,0:T(8,128)(2,1)S(1)}, bf16[4,64,256]{2,1,0:T(8,128)(2,1)S(1)}, u32[]{:S(2)}, u32[]{:S(2)}) collective-permute-start(bf16[4,64,256]{2,1,0:T(8,128)(2,1)S(1)} %get-tuple-element.43), channel_id=1, source_target_pairs={{0,2},{1,3},{2,0},{3,1},{4,6},{5,7},{6,4},{7,5},{8,10},{9,11},{10,... | collective-permute-start | bytes 393224 | tf_op jit(solution)/shard_map/ppermute | solution.py:27
  8.8 0.5 merge0b.1
  9.3 0.1 collective-permute-start.4
  9.4 0.5 merge0c.1
  9.9 2.1 %collective-permute-start.7 = (bf16[4,112,256]{2,1,0:T(8,128)(2,1)S(1)}, bf16[4,112,256]{2,1,0:T(8,128)(2,1)S(1)}, u32[]{:S(2)}, u32[]{:S(2)}) collective-permute-start(bf16[4,112,256]{2,1,0:T(8,128)(2,1)S(1)} %get-tuple-element.54), channel_id=1, source_target_pairs={{0,2},{1,3},{2,0},{3,1},{4,6},{5,7},{6,4},{7,5},{8,10},{9,11},{10,... | collective-permute-start | bytes 688136 | tf_op jit(solution)/shard_map/ppermute | solution.py:27
  12.0 0.5 inside.1.after_ref.inside_ref
  12.4 0.7 %collective-permute-done.1.got_ref = bf16[4,64,256]{2,1,0:T(8,128)(2,1)S(1)} collective-permute-done((bf16[4,64,256]{2,1,0:T(8,128)(2,1)S(1)}, bf16[4,64,256]{2,1,0:T(8,128)(2,1)S(1)}, u32[]{:S(2)}, u32[]{:S(2)}) %collective-permute-start.1) | collective-permute-done | bytes 131104 | tf_op jit(solution)/shard_map/ppermute | solution.py:27
  13.1 0.5 merge1a.1
  13.6 2.0 %collective-permute-start.3 = (bf16[4,64,256]{2,1,0:T(8,128)(2,1)S(1)}, bf16[4,64,256]{2,1,0:T(8,128)(2,1)S(1)}, u32[]{:S(2)}, u32[]{:S(2)}) collective-permute-start(bf16[4,64,256]{2,1,0:T(8,128)(2,1)S(1)} %get-tuple-element.48), channel_id=1, source_target_pairs={{0,8},{8,0},{16,24},{24,16},{1,9},{9,1},{17,25},{25,17},{2,10},{10... | collective-permute-start | bytes 393224 | tf_op jit(solution)/shard_map/ppermute | solution.py:27
  15.7 1.0 %collective-permute-done.4.got_ref = bf16[4,80,256]{2,1,0:T(8,128)(2,1)S(1)} collective-permute-done((bf16[4,80,256]{2,1,0:T(8,128)(2,1)S(1)}, bf16[4,80,256]{2,1,0:T(8,128)(2,1)S(1)}, u32[]{:S(2)}, u32[]{:S(2)}) %collective-permute-start.4) | collective-permute-done | bytes 163872 | tf_op jit(solution)/shard_map/ppermute | solution.py:27
  16.6 0.5 merge1b.1
  17.1 2.0 %collective-permute-start.6 = (bf16[4,80,256]{2,1,0:T(8,128)(2,1)S(1)}, bf16[4,80,256]{2,1,0:T(8,128)(2,1)S(1)}, u32[]{:S(2)}, u32[]{:S(2)}) collective-permute-start(bf16[4,80,256]{2,1,0:T(8,128)(2,1)S(1)} %get-tuple-element.53), channel_id=1, source_target_pairs={{0,8},{8,0},{16,24},{24,16},{1,9},{9,1},{17,25},{25,17},{2,10},{10... | collective-permute-start | bytes 491528 | tf_op jit(solution)/shard_map/ppermute | solution.py:27
  19.2 1.3 %join.1.after_ref.joint_ref = bf16[8,512,256]{2,1,0:T(8,128)(2,1)S(1)} custom-call(s32[1,1,8]{2,1,0:T(1,128)S(1)} %copy-done.2, bf16[4,1,1,8,512,256]{5,4,3,2,1,0:T(8,128)(2,1)S(1)} %bitcast.1, bf16[8,256,256]{2,1,0:T(8,128)(2,1)S(1)} %inside.1.after_ref.inside_ref, bf16[4,80,256]{2,1,0:T(8,128)(2,1)S(1)} %get-tuple-element.50.after_ref.kept_ref), custom_call_target="tpu_custom_call" | custom-call | flops 300000000 | tf_op jit(solution)/shard_map/join/pallas_call | solution.py:60
  20.5 0.5 merge2a.1
  21.0 1.6 %collective-permute-start.5 = (bf16[4,64,256]{2,1,0:T(8,128)(2,1)S(1)}, bf16[4,64,256]{2,1,0:T(8,128)(2,1)S(1)}, u32[]{:S(2)}, u32[]{:S(2)}) collective-permute-start(bf16[4,64,256]{2,1,0:T(8,128)(2,1)S(1)} %get-tuple-element.52), channel_id=1, source_target_pairs={{0,16},{8,24},{16,0},{24,8},{1,17},{9,25},{17,1},{25,9},{2,18},{10... | collective-permute-start | bytes 393224 | tf_op jit(solution)/shard_map/ppermute | solution.py:27
  22.6 0.5 merge1c.1
  23.1 0.7 %collective-permute-start.12 = (bf16[4,112,256]{2,1,0:T(8,128)(2,1)S(1)}, bf16[4,112,256]{2,1,0:T(8,128)(2,1)S(1)}, u32[]{:S(2)}, u32[]{:S(2)}) collective-permute-start(bf16[4,112,256]{2,1,0:T(8,128)(2,1)S(1)} %get-tuple-element.62), channel_id=1, source_target_pairs={{0,8},{8,0},{16,24},{24,16},{1,9},{9,1},{17,25},{25,17},{2,10},{10... | collective-permute-start | bytes 688136 | tf_op jit(solution)/shard_map/ppermute | solution.py:27
  23.8 0.5 merge2b.1
  24.3 1.0 %collective-permute-start.11 = (bf16[4,80,256]{2,1,0:T(8,128)(2,1)S(1)}, bf16[4,80,256]{2,1,0:T(8,128)(2,1)S(1)}, u32[]{:S(2)}, u32[]{:S(2)}) collective-permute-start(bf16[4,80,256]{2,1,0:T(8,128)(2,1)S(1)} %get-tuple-element.61), channel_id=1, source_target_pairs={{0,16},{8,24},{16,0},{24,8},{1,17},{9,25},{17,1},{25,9},{2,18},{10... | collective-permute-start | bytes 491528 | tf_op jit(solution)/shard_map/ppermute | solution.py:27
  25.3 1.4 %collective-permute-done.5.got_ref = bf16[4,64,256]{2,1,0:T(8,128)(2,1)S(1)} collective-permute-done((bf16[4,64,256]{2,1,0:T(8,128)(2,1)S(1)}, bf16[4,64,256]{2,1,0:T(8,128)(2,1)S(1)}, u32[]{:S(2)}, u32[]{:S(2)}) %collective-permute-start.5) | collective-permute-done | bytes 131104 | tf_op jit(solution)/shard_map/ppermute | solution.py:27
  26.7 1.0 %lasta.1 = (bf16[2,64,256]{2,1,0:T(8,128)(2,1)S(1)}, bf16[2,64,256]{2,1,0:T(8,128)(2,1)S(1)}, bf16[2,64,256]{2,1,0:T(8,128)(2,1)S(1)}, bf16[2,64,256]{2,1,0:T(8,128)(2,1)S(1)}) custom-call(s32[1,1,8]{2,1,0:T(1,128)S(1)} %copy-done.2, bf16[4,64,256]{2,1,0:T(8,128)(2,1)S(1)} %get-tuple-element.51.after_ref.kept_ref, ...), custom_call_target="tpu_custom_call" | custom-call | flops 1000000000 | tf_op jit(solution)/shard_map/lasta/pallas_call | solution.py:60
  27.7 1.6 %collective-permute-start.8 = (bf16[2,64,256]{2,1,0:T(8,128)(2,1)S(1)}, bf16[2,64,256]{2,1,0:T(8,128)(2,1)S(1)}, u32[]{:S(2)}, u32[]{:S(2)}) collective-permute-start(bf16[2,64,256]{2,1,0:T(8,128)(2,1)S(1)} %get-tuple-element.58), channel_id=1, source_target_pairs={{0,2},{1,3},{2,0},{3,1},{4,6},{5,7},{6,4},{7,5},{8,10},{9,11},{10,... | collective-permute-start | bytes 196616 | tf_op jit(solution)/shard_map/ppermute | solution.py:27
  29.4 2.6 %collective-permute-start.9 = (bf16[2,64,256]{2,1,0:T(8,128)(2,1)S(1)}, bf16[2,64,256]{2,1,0:T(8,128)(2,1)S(1)}, u32[]{:S(2)}, u32[]{:S(2)}) collective-permute-start(bf16[2,64,256]{2,1,0:T(8,128)(2,1)S(1)} %get-tuple-element.59), channel_id=1, source_target_pairs={{0,4},{1,5},{2,6},{3,7},{4,0},{5,1},{6,2},{7,3},{8,12},{9,13},{10,... | collective-permute-start | bytes 196616 | tf_op jit(solution)/shard_map/ppermute | solution.py:27
  32.0 0.2 collective-permute-start.10
  32.2 0.5 merge2c.1
  32.7 1.6 %collective-permute-start.17 = (bf16[4,112,256]{2,1,0:T(8,128)(2,1)S(1)}, bf16[4,112,256]{2,1,0:T(8,128)(2,1)S(1)}, u32[]{:S(2)}, u32[]{:S(2)}) collective-permute-start(bf16[4,112,256]{2,1,0:T(8,128)(2,1)S(1)} %get-tuple-element.68), channel_id=1, source_target_pairs={{0,16},{8,24},{16,0},{24,8},{1,17},{9,25},{17,1},{25,9},{2,18},{10... | collective-permute-start | bytes 688136 | tf_op jit(solution)/shard_map/ppermute | solution.py:27
  34.3 1.0 %lastb.1 = (bf16[2,80,256]{2,1,0:T(8,128)(2,1)S(1)}, bf16[2,80,256]{2,1,0:T(8,128)(2,1)S(1)}, bf16[2,80,256]{2,1,0:T(8,128)(2,1)S(1)}, bf16[2,80,256]{2,1,0:T(8,128)(2,1)S(1)}) custom-call(s32[1,1,8]{2,1,0:T(1,128)S(1)} %copy-done.2, bf16[4,80,256]{2,1,0:T(8,128)(2,1)S(1)} %get-tuple-element.56.after_ref.kept_ref, ...), custom_call_target="tpu_custom_call" | custom-call | flops 100000000 | tf_op jit(solution)/shard_map/lastb/pallas_call | solution.py:60
  35.3 0.7 %collective-permute-start.14 = (bf16[2,80,256]{2,1,0:T(8,128)(2,1)S(1)}, bf16[2,80,256]{2,1,0:T(8,128)(2,1)S(1)}, u32[]{:S(2)}, u32[]{:S(2)}) collective-permute-start(bf16[2,80,256]{2,1,0:T(8,128)(2,1)S(1)} %get-tuple-element.65), channel_id=1, source_target_pairs={{0,2},{1,3},{2,0},{3,1},{4,6},{5,7},{6,4},{7,5},{8,10},{9,11},{10,... | collective-permute-start | bytes 245768 | tf_op jit(solution)/shard_map/ppermute | solution.py:27
  36.1 3.5 %collective-permute-start.15 = (bf16[2,80,256]{2,1,0:T(8,128)(2,1)S(1)}, bf16[2,80,256]{2,1,0:T(8,128)(2,1)S(1)}, u32[]{:S(2)}, u32[]{:S(2)}) collective-permute-start(bf16[2,80,256]{2,1,0:T(8,128)(2,1)S(1)} %get-tuple-element.66), channel_id=1, source_target_pairs={{0,4},{1,5},{2,6},{3,7},{4,0},{5,1},{6,2},{7,3},{8,12},{9,13},{10,... | collective-permute-start | bytes 245768 | tf_op jit(solution)/shard_map/ppermute | solution.py:27
  39.5 0.2 collective-permute-start.16
  39.8 0.1 collective-permute-start.13
  39.9 1.0 %lastc.1 = (bf16[2,112,256]{2,1,0:T(8,128)(2,1)S(1)}, bf16[2,112,256]{2,1,0:T(8,128)(2,1)S(1)}, bf16[2,112,256]{2,1,0:T(8,128)(2,1)S(1)}, bf16[2,112,256]{2,1,0:T(8,128)(2,1)S(1)}) custom-call(s32[1,1,8]{2,1,0:T(1,128)S(1)} %copy-done.2, bf16[4,112,256]{2,1,0:T(8,128)(2,1)S(1)} %get-tuple-element.63.after_ref.kept_ref, ...), custom_call_target="tpu_custom_call" | custom-call | flops 400000000 | tf_op jit(solution)/shard_map/lastc/pallas_call | solution.py:60
  40.9 0.5 collective-permute-start.19
  41.4 3.8 %collective-permute-start.20 = (bf16[2,112,256]{2,1,0:T(8,128)(2,1)S(1)}, bf16[2,112,256]{2,1,0:T(8,128)(2,1)S(1)}, u32[]{:S(2)}, u32[]{:S(2)}) collective-permute-start(bf16[2,112,256]{2,1,0:T(8,128)(2,1)S(1)} %get-tuple-element.71), channel_id=1, source_target_pairs={{0,4},{1,5},{2,6},{3,7},{4,0},{5,1},{6,2},{7,3},{8,12},{9,13},{10,... | collective-permute-start | bytes 344072 | tf_op jit(solution)/shard_map/ppermute | solution.py:27
  45.1 0.2 collective-permute-start.21
  45.4 0.5 collective-permute-done.16.refs_3_.refs_8_
  46.0 3.6 %collective-permute-done.19.refs_0_.refs_11_ = bf16[2,112,256]{2,1,0:T(8,128)(2,1)S(1)} collective-permute-done((bf16[2,112,256]{2,1,0:T(8,128)(2,1)S(1)}, bf16[2,112,256]{2,1,0:T(8,128)(2,1)S(1)}, u32[]{:S(2)}, u32[]{:S(2)}) %collective-permute-start.19) | collective-permute-done | bytes 114720 | tf_op jit(solution)/shard_map/ppermute | solution.py:27
  49.6 4.4 %collective-permute-done.20.refs_0_.refs_12_ = bf16[2,112,256]{2,1,0:T(8,128)(2,1)S(1)} collective-permute-done((bf16[2,112,256]{2,1,0:T(8,128)(2,1)S(1)}, bf16[2,112,256]{2,1,0:T(8,128)(2,1)S(1)}, u32[]{:S(2)}, u32[]{:S(2)}) %collective-permute-start.20) | collective-permute-done | bytes 114720 | tf_op jit(solution)/shard_map/ppermute | solution.py:27
  54.0 0.6 collective-permute-start.25
  54.6 0.1 collective-permute-start.23
  54.7 0.8 %collective-permute-done.25.refs_17_ = bf16[1,112,256]{2,1,0:T(8,128)(2,1)S(1)} collective-permute-done((bf16[1,112,256]{2,1,0:T(8,128)(2,1)S(1)}, bf16[1,112,256]{2,1,0:T(8,128)(2,1)S(1)}, u32[]{:S(2)}, u32[]{:S(2)}) %collective-permute-start.25) | collective-permute-done | bytes 57376 | tf_op jit(solution)/shard_map/ppermute | solution.py:27
  55.5 0.4 collective-permute-done.23.refs_15_
  55.8 1.8 %place.1 = bf16[2048,256]{1,0:T(8,128)(2,1)} custom-call(bf16[2,64,256]{2,1,0:T(8,128)(2,1)S(1)} %get-tuple-element.57.after_ref.refs_0_, bf16[2,64,256]{2,1,0:T(8,128)(2,1)S(1)} %collective-permute-done.8.refs_1_, bf16[2,64,256]{2,1,0:T(8,128)(2,1)S(1)} %collective-permute-done.9.refs_2_, bf16[2,64,256]{2,1,0:T(8,128)(2,1)S(1)} %collective-permute-done.10.refs_3_, ...), custom_call_target="tpu_custom_call" | custom-call | flops 2000000000 | tf_op jit(solution)/shard_map/place/pallas_call | solution.py:60
  (38 shorter events, 0.2 us)
Async XLA Ops:
  3.0 5.8 %collective-permute-start.2 = (bf16[4,192,256]{2,1,0:T(8,128)(2,1)S(1)}, bf16[4,192,256]{2,1,0:T(8,128)(2,1)S(1)}, u32[]{:S(2)}, u32[]{:S(2)}) collective-permute-start(bf16[4,192,256]{2,1,0:T(8,128)(2,1)S(1)} %get-tuple-element.44), channel_id=1, source_target_pairs={{0,1},{1,0},{2,3},{3,2},{4,5},{5,4},{6,7},{7,6},{8,9},{9,8},{10,11... | collective-permute-start | bytes 1179656 | tf_op jit(solution)/shard_map/ppermute | solution.py:27
  3.6 1.7 %collective-permute-start = (bf16[4,64,256]{2,1,0:T(8,128)(2,1)S(1)}, bf16[4,64,256]{2,1,0:T(8,128)(2,1)S(1)}, u32[]{:S(2)}, u32[]{:S(2)}) collective-permute-start(bf16[4,64,256]{2,1,0:T(8,128)(2,1)S(1)} %get-tuple-element.40), channel_id=1, source_target_pairs={{0,1},{1,0},{2,3},{3,2},{4,5},{5,4},{6,7},{7,6},{8,9},{9,8},{10,11... | collective-permute-start | bytes 393224 | tf_op jit(solution)/shard_map/ppermute | solution.py:27
  5.8 7.4 %collective-permute-start.1 = (bf16[4,64,256]{2,1,0:T(8,128)(2,1)S(1)}, bf16[4,64,256]{2,1,0:T(8,128)(2,1)S(1)}, u32[]{:S(2)}, u32[]{:S(2)}) collective-permute-start(bf16[4,64,256]{2,1,0:T(8,128)(2,1)S(1)} %get-tuple-element.43), channel_id=1, source_target_pairs={{0,2},{1,3},{2,0},{3,1},{4,6},{5,7},{6,4},{7,5},{8,10},{9,11},{10,... | collective-permute-start | bytes 393224 | tf_op jit(solution)/shard_map/ppermute | solution.py:27
  8.8 4.3 %slice-start = ((s8[8388608]{0:T(1024)(128)(4,1)}), s8[4194304]{0:T(1024)(128)(4,1)S(1)}, s32[]{:S(2)}) async-start(s8[8388608]{0:T(1024)(128)(4,1)} %bitcast), calls=%async_computation | async-start | bytes 8388608
  9.3 7.3 %collective-permute-start.4 = (bf16[4,80,256]{2,1,0:T(8,128)(2,1)S(1)}, bf16[4,80,256]{2,1,0:T(8,128)(2,1)S(1)}, u32[]{:S(2)}, u32[]{:S(2)}) collective-permute-start(bf16[4,80,256]{2,1,0:T(8,128)(2,1)S(1)} %get-tuple-element.49), channel_id=1, source_target_pairs={{0,2},{1,3},{2,0},{3,1},{4,6},{5,7},{6,4},{7,5},{8,10},{9,11},{10,... | collective-permute-start | bytes 491528 | tf_op jit(solution)/shard_map/ppermute | solution.py:27
  9.4 2.5 %copy-start = (bf16[1,1,8,256,256]{4,3,2,1,0:T(8,128)(2,1)S(1)}, bf16[1,1,8,256,256]{4,3,2,1,0:T(8,128)(2,1)}, u32[]{:S(2)}) copy-start(bf16[1,1,8,256,256]{4,3,2,1,0:T(8,128)(2,1)} %core_ref.1) | copy-start | bytes 3145732
  9.4 2.5 %copy-start.1 = (bf16[2048,256]{1,0:T(8,128)(2,1)S(1)}, bf16[2048,256]{1,0:T(8,128)(2,1)}, u32[]{:S(2)}) copy-start(bf16[2048,256]{1,0:T(8,128)(2,1)} %u_ref.1) | copy-start | bytes 3145732
  9.4 3.7 %slice-start.1 = ((s8[8388608]{0:T(1024)(128)(4,1)}), s8[4194304]{0:T(1024)(128)(4,1)S(1)}, s32[]{:S(2)}) async-start(s8[8388608]{0:T(1024)(128)(4,1)} %bitcast), calls=%async_computation.1 | async-start | bytes 8388608
  9.9 12.7 %collective-permute-start.7 = (bf16[4,112,256]{2,1,0:T(8,128)(2,1)S(1)}, bf16[4,112,256]{2,1,0:T(8,128)(2,1)S(1)}, u32[]{:S(2)}, u32[]{:S(2)}) collective-permute-start(bf16[4,112,256]{2,1,0:T(8,128)(2,1)S(1)} %get-tuple-element.54), channel_id=1, source_target_pairs={{0,2},{1,3},{2,0},{3,1},{4,6},{5,7},{6,4},{7,5},{8,10},{9,11},{10,... | collective-permute-start | bytes 688136 | tf_op jit(solution)/shard_map/ppermute | solution.py:27
  13.6 6.8 %collective-permute-start.3 = (bf16[4,64,256]{2,1,0:T(8,128)(2,1)S(1)}, bf16[4,64,256]{2,1,0:T(8,128)(2,1)S(1)}, u32[]{:S(2)}, u32[]{:S(2)}) collective-permute-start(bf16[4,64,256]{2,1,0:T(8,128)(2,1)S(1)} %get-tuple-element.48), channel_id=1, source_target_pairs={{0,8},{8,0},{16,24},{24,16},{1,9},{9,1},{17,25},{25,17},{2,10},{10... | collective-permute-start | bytes 393224 | tf_op jit(solution)/shard_map/ppermute | solution.py:27
  16.6 2.5 %copy-start.2 = (s32[1,1,8]{2,1,0:T(1,128)S(1)}, s32[1,1,8]{2,1,0:T(1,128)}, u32[]{:S(2)}) copy-start(s32[1,1,8]{2,1,0:T(1,128)} %order_ref.7) | copy-start | bytes 100
  17.1 6.7 %collective-permute-start.6 = (bf16[4,80,256]{2,1,0:T(8,128)(2,1)S(1)}, bf16[4,80,256]{2,1,0:T(8,128)(2,1)S(1)}, u32[]{:S(2)}, u32[]{:S(2)}) collective-permute-start(bf16[4,80,256]{2,1,0:T(8,128)(2,1)S(1)} %get-tuple-element.53), channel_id=1, source_target_pairs={{0,8},{8,0},{16,24},{24,16},{1,9},{9,1},{17,25},{25,17},{2,10},{10... | collective-permute-start | bytes 491528 | tf_op jit(solution)/shard_map/ppermute | solution.py:27
  21.0 5.7 %collective-permute-start.5 = (bf16[4,64,256]{2,1,0:T(8,128)(2,1)S(1)}, bf16[4,64,256]{2,1,0:T(8,128)(2,1)S(1)}, u32[]{:S(2)}, u32[]{:S(2)}) collective-permute-start(bf16[4,64,256]{2,1,0:T(8,128)(2,1)S(1)} %get-tuple-element.52), channel_id=1, source_target_pairs={{0,16},{8,24},{16,0},{24,8},{1,17},{9,25},{17,1},{25,9},{2,18},{10... | collective-permute-start | bytes 393224 | tf_op jit(solution)/shard_map/ppermute | solution.py:27
  23.1 9.1 %collective-permute-start.12 = (bf16[4,112,256]{2,1,0:T(8,128)(2,1)S(1)}, bf16[4,112,256]{2,1,0:T(8,128)(2,1)S(1)}, u32[]{:S(2)}, u32[]{:S(2)}) collective-permute-start(bf16[4,112,256]{2,1,0:T(8,128)(2,1)S(1)} %get-tuple-element.62), channel_id=1, source_target_pairs={{0,8},{8,0},{16,24},{24,16},{1,9},{9,1},{17,25},{25,17},{2,10},{10... | collective-permute-start | bytes 688136 | tf_op jit(solution)/shard_map/ppermute | solution.py:27
  24.3 10.0 %collective-permute-start.11 = (bf16[4,80,256]{2,1,0:T(8,128)(2,1)S(1)}, bf16[4,80,256]{2,1,0:T(8,128)(2,1)S(1)}, u32[]{:S(2)}, u32[]{:S(2)}) collective-permute-start(bf16[4,80,256]{2,1,0:T(8,128)(2,1)S(1)} %get-tuple-element.61), channel_id=1, source_target_pairs={{0,16},{8,24},{16,0},{24,8},{1,17},{9,25},{17,1},{25,9},{2,18},{10... | collective-permute-start | bytes 491528 | tf_op jit(solution)/shard_map/ppermute | solution.py:27
  27.7 8.3 %collective-permute-start.8 = (bf16[2,64,256]{2,1,0:T(8,128)(2,1)S(1)}, bf16[2,64,256]{2,1,0:T(8,128)(2,1)S(1)}, u32[]{:S(2)}, u32[]{:S(2)}) collective-permute-start(bf16[2,64,256]{2,1,0:T(8,128)(2,1)S(1)} %get-tuple-element.58), channel_id=1, source_target_pairs={{0,2},{1,3},{2,0},{3,1},{4,6},{5,7},{6,4},{7,5},{8,10},{9,11},{10,... | collective-permute-start | bytes 196616 | tf_op jit(solution)/shard_map/ppermute | solution.py:27
  29.4 10.2 %collective-permute-start.9 = (bf16[2,64,256]{2,1,0:T(8,128)(2,1)S(1)}, bf16[2,64,256]{2,1,0:T(8,128)(2,1)S(1)}, u32[]{:S(2)}, u32[]{:S(2)}) collective-permute-start(bf16[2,64,256]{2,1,0:T(8,128)(2,1)S(1)} %get-tuple-element.59), channel_id=1, source_target_pairs={{0,4},{1,5},{2,6},{3,7},{4,0},{5,1},{6,2},{7,3},{8,12},{9,13},{10,... | collective-permute-start | bytes 196616 | tf_op jit(solution)/shard_map/ppermute | solution.py:27
  32.0 7.8 %collective-permute-start.10 = (bf16[2,64,256]{2,1,0:T(8,128)(2,1)S(1)}, bf16[2,64,256]{2,1,0:T(8,128)(2,1)S(1)}, u32[]{:S(2)}, u32[]{:S(2)}) collective-permute-start(bf16[2,64,256]{2,1,0:T(8,128)(2,1)S(1)} %get-tuple-element.60), channel_id=1, source_target_pairs={{0,6},{1,7},{2,4},{3,5},{4,2},{5,3},{6,0},{7,1},{8,14},{9,15},{10,... | collective-permute-start | bytes 196616 | tf_op jit(solution)/shard_map/ppermute | solution.py:27
  32.7 7.2 %collective-permute-start.17 = (bf16[4,112,256]{2,1,0:T(8,128)(2,1)S(1)}, bf16[4,112,256]{2,1,0:T(8,128)(2,1)S(1)}, u32[]{:S(2)}, u32[]{:S(2)}) collective-permute-start(bf16[4,112,256]{2,1,0:T(8,128)(2,1)S(1)} %get-tuple-element.68), channel_id=1, source_target_pairs={{0,16},{8,24},{16,0},{24,8},{1,17},{9,25},{17,1},{25,9},{2,18},{10... | collective-permute-start | bytes 688136 | tf_op jit(solution)/shard_map/ppermute | solution.py:27
  35.3 6.1 %collective-permute-start.14 = (bf16[2,80,256]{2,1,0:T(8,128)(2,1)S(1)}, bf16[2,80,256]{2,1,0:T(8,128)(2,1)S(1)}, u32[]{:S(2)}, u32[]{:S(2)}) collective-permute-start(bf16[2,80,256]{2,1,0:T(8,128)(2,1)S(1)} %get-tuple-element.65), channel_id=1, source_target_pairs={{0,2},{1,3},{2,0},{3,1},{4,6},{5,7},{6,4},{7,5},{8,10},{9,11},{10,... | collective-permute-start | bytes 245768 | tf_op jit(solution)/shard_map/ppermute | solution.py:27
  36.1 9.1 %collective-permute-start.15 = (bf16[2,80,256]{2,1,0:T(8,128)(2,1)S(1)}, bf16[2,80,256]{2,1,0:T(8,128)(2,1)S(1)}, u32[]{:S(2)}, u32[]{:S(2)}) collective-permute-start(bf16[2,80,256]{2,1,0:T(8,128)(2,1)S(1)} %get-tuple-element.66), channel_id=1, source_target_pairs={{0,4},{1,5},{2,6},{3,7},{4,0},{5,1},{6,2},{7,3},{8,12},{9,13},{10,... | collective-permute-start | bytes 245768 | tf_op jit(solution)/shard_map/ppermute | solution.py:27
  39.5 6.3 %collective-permute-start.16 = (bf16[2,80,256]{2,1,0:T(8,128)(2,1)S(1)}, bf16[2,80,256]{2,1,0:T(8,128)(2,1)S(1)}, u32[]{:S(2)}, u32[]{:S(2)}) collective-permute-start(bf16[2,80,256]{2,1,0:T(8,128)(2,1)S(1)} %get-tuple-element.67), channel_id=1, source_target_pairs={{0,6},{1,7},{2,4},{3,5},{4,2},{5,3},{6,0},{7,1},{8,14},{9,15},{10,... | collective-permute-start | bytes 245768 | tf_op jit(solution)/shard_map/ppermute | solution.py:27
  39.8 14.8 %collective-permute-start.13 = (bf16[4,64,256]{2,1,0:T(8,128)(2,1)S(1)}, bf16[4,64,256]{2,1,0:T(8,128)(2,1)S(1)}, u32[]{:S(2)}, u32[]{:S(2)}) collective-permute-start(bf16[4,64,256]{2,1,0:T(8,128)(2,1)S(1)} %packa.1.after_ref), channel_id=1, source_target_pairs={{0,1},{1,0},{2,3},{3,2},{4,5},{5,4},{6,7},{7,6},{8,9},{9,8},{10,11... | collective-permute-start | bytes 393224 | tf_op jit(solution)/shard_map/ppermute | solution.py:27
  40.9 8.6 %collective-permute-start.19 = (bf16[2,112,256]{2,1,0:T(8,128)(2,1)S(1)}, bf16[2,112,256]{2,1,0:T(8,128)(2,1)S(1)}, u32[]{:S(2)}, u32[]{:S(2)}) collective-permute-start(bf16[2,112,256]{2,1,0:T(8,128)(2,1)S(1)} %get-tuple-element.70), channel_id=1, source_target_pairs={{0,2},{1,3},{2,0},{3,1},{4,6},{5,7},{6,4},{7,5},{8,10},{9,11},{10,... | collective-permute-start | bytes 344072 | tf_op jit(solution)/shard_map/ppermute | solution.py:27
  41.4 12.6 %collective-permute-start.20 = (bf16[2,112,256]{2,1,0:T(8,128)(2,1)S(1)}, bf16[2,112,256]{2,1,0:T(8,128)(2,1)S(1)}, u32[]{:S(2)}, u32[]{:S(2)}) collective-permute-start(bf16[2,112,256]{2,1,0:T(8,128)(2,1)S(1)} %get-tuple-element.71), channel_id=1, source_target_pairs={{0,4},{1,5},{2,6},{3,7},{4,0},{5,1},{6,2},{7,3},{8,12},{9,13},{10,... | collective-permute-start | bytes 344072 | tf_op jit(solution)/shard_map/ppermute | solution.py:27
  45.1 8.8 %collective-permute-start.21 = (bf16[2,112,256]{2,1,0:T(8,128)(2,1)S(1)}, bf16[2,112,256]{2,1,0:T(8,128)(2,1)S(1)}, u32[]{:S(2)}, u32[]{:S(2)}) collective-permute-start(bf16[2,112,256]{2,1,0:T(8,128)(2,1)S(1)} %get-tuple-element.72), channel_id=1, source_target_pairs={{0,6},{1,7},{2,4},{3,5},{4,2},{5,3},{6,0},{7,1},{8,14},{9,15},{10,... | collective-permute-start | bytes 344072 | tf_op jit(solution)/shard_map/ppermute | solution.py:27
  45.9 8.8 %collective-permute-start.18 = (bf16[4,80,256]{2,1,0:T(8,128)(2,1)S(1)}, bf16[4,80,256]{2,1,0:T(8,128)(2,1)S(1)}, u32[]{:S(2)}, u32[]{:S(2)}) collective-permute-start(bf16[4,80,256]{2,1,0:T(8,128)(2,1)S(1)} %packb.1.refs_1_), channel_id=1, source_target_pairs={{0,1},{1,0},{2,3},{3,2},{4,5},{5,4},{6,7},{7,6},{8,9},{9,8},{10,11... | collective-permute-start | bytes 491528 | tf_op jit(solution)/shard_map/ppermute | solution.py:27
  49.5 5.1 %collective-permute-start.22 = (bf16[1,112,256]{2,1,0:T(8,128)(2,1)S(1)}, bf16[1,112,256]{2,1,0:T(8,128)(2,1)S(1)}, u32[]{:S(2)}, u32[]{:S(2)}) collective-permute-start(bf16[1,112,256]{2,1,0:T(8,128)(2,1)S(1)} %packc.4.refs_1_), channel_id=1, source_target_pairs={{0,1},{1,0},{2,3},{3,2},{4,5},{5,4},{6,7},{7,6},{8,9},{9,8},{10,11... | collective-permute-start | bytes 172040 | tf_op jit(solution)/shard_map/ppermute | solution.py:27
  54.0 1.5 %collective-permute-start.24 = (bf16[1,112,256]{2,1,0:T(8,128)(2,1)S(1)}, bf16[1,112,256]{2,1,0:T(8,128)(2,1)S(1)}, u32[]{:S(2)}, u32[]{:S(2)}) collective-permute-start(bf16[1,112,256]{2,1,0:T(8,128)(2,1)S(1)} %packc.6.refs_1_), channel_id=1, source_target_pairs={{0,1},{1,0},{2,3},{3,2},{4,5},{5,4},{6,7},{7,6},{8,9},{9,8},{10,11... | collective-permute-start | bytes 172040 | tf_op jit(solution)/shard_map/ppermute | solution.py:27
  54.0 1.4 %collective-permute-start.25 = (bf16[1,112,256]{2,1,0:T(8,128)(2,1)S(1)}, bf16[1,112,256]{2,1,0:T(8,128)(2,1)S(1)}, u32[]{:S(2)}, u32[]{:S(2)}) collective-permute-start(bf16[1,112,256]{2,1,0:T(8,128)(2,1)S(1)} %packc.7), channel_id=1, source_target_pairs={{0,1},{1,0},{2,3},{3,2},{4,5},{5,4},{6,7},{7,6},{8,9},{9,8},{10,11... | collective-permute-start | bytes 172040 | tf_op jit(solution)/shard_map/ppermute | solution.py:27
  54.6 1.2 %collective-permute-start.23 = (bf16[1,112,256]{2,1,0:T(8,128)(2,1)S(1)}, bf16[1,112,256]{2,1,0:T(8,128)(2,1)S(1)}, u32[]{:S(2)}, u32[]{:S(2)}) collective-permute-start(bf16[1,112,256]{2,1,0:T(8,128)(2,1)S(1)} %packc.5.refs_1_), channel_id=1, source_target_pairs={{0,1},{1,0},{2,3},{3,2},{4,5},{5,4},{6,7},{7,6},{8,9},{9,8},{10,11... | collective-permute-start | bytes 172040 | tf_op jit(solution)/shard_map/ppermute | solution.py:27

commit v4 on v3

--- a/solution.py
+++ b/solution.py
@@ -9,8 +9,8 @@
 
 INNER_LEVELS = 2
 PARTS = (4, 5, 7)
-COSTS = {"merge2c":.4,"lastb":.1,"lastc":.4,"packc":0,"lasta":1,"packa":2,"packb":1,"merge1b":.4,"join":.3,"inside":.3,"merge2a":.4,"merge1a":1}
-ORDER = ("f", "w", "m0a", "m0b", "m0c", "i", "m1a", "m1b", "j", "m2a", "m1c", "m2b", "oa", "m2c", "ob", "qa", "oc", "qb", "rc")
+COSTS = {"merge2c":.4,"lastb":.1,"lastc":.4,"packc":2,"lasta":1,"packa":2,"packb":1,"merge1b":.4,"join":.3,"inside":.3,"merge2a":.4,"merge1a":1,"place":5,"space":10}
+ORDER = ("f", "w", "m0a", "m0b", "m0c", "i", "m1a", "m1b", "j", "m2a", "m1c", "m2b", "oa", "m2c", "ob", "qa", "oc", "qb", "uc", "x", "z", "tc")
 LEAF_ROOM = 52
 LOAD_ROOM = 48
 HBM = pl.BlockSpec(memory_space=pltpu.HBM)
@@ -44,13 +44,14 @@
     return lax.dot_general(a, b, (dims, ((), ())), preferred_element_type=jnp.float32)
 
 
-def call(kernel, outs, ins, specs, scratch=(), name=None, room=24, out_spec=VMEM):
+def call(kernel, outs, ins, specs, scratch=(), name=None, room=24, out_specs=None, aliases=None):
     run = pl.pallas_call(
         kernel,
         name=name,
         out_shape=outs,
         in_specs=specs,
-        out_specs=[out_spec] * len(outs),
+        out_specs=out_specs or [VMEM] * len(outs),
+        input_output_aliases=aliases or {},
         scratch_shapes=list(scratch),
         compiler_params=pltpu.CompilerParams(vmem_limit_bytes=room * 1024 * 1024),
         cost_estimate=pl.CostEstimate(
@@ -66,40 +67,49 @@
     return copies
 
 
-def load_kernel(w_hbm, after_ref, w_out, sem):
-    load = pltpu.make_async_copy(w_hbm.at[0, 0, 0], w_out, sem)
-    load.start()
-    load.wait()
+def load_kernel(w_hbm, after_ref, w_out, sems):
+    parts = sems.shape[0]
+    each = w_out.shape[0] // parts
+    loads = copy_all(
+        [
+            pltpu.make_async_copy(
+                w_hbm.at[0, 0, 0, pl.ds(n * each, each)],
+                w_out.at[pl.ds(n * each, each)],
+                sems.at[n],
+            )
+            for n in range(parts)
+        ]
+    )
+    for load in loads:
+        load.wait()
 
 
 def leaf_kernel(cuts, x_hbm, v_hbm, *refs):
     outs, (x_ref, v_ref, sems) = refs[:-3], refs[-3:]
     half = outs[0].shape[0]
     flag = bit_of(0)
-    rows = x_ref.shape[0] // (2 * half)
-
-    def window(slot):
-        side = 1 - flag if slot < half else flag
-        return pl.ds(pl.multiple_of((side * half + slot % half) * rows, rows), rows)
-
+    depth = x_ref.shape[1]
+    rows = depth // half
     loads = []
-    for slot in range(2 * half):
-        at = window(slot)
+    for late in range(2):
+        side = flag if late else 1 - flag
+        at = pl.ds(pl.multiple_of(side * depth, depth), depth)
         loads.append(
             copy_all(
                 [
-                    pltpu.make_async_copy(x_hbm.at[at], x_ref.at[at], sems.at[0, slot]),
-                    pltpu.make_async_copy(v_hbm.at[at], v_ref.at[at], sems.at[1, slot]),
+                    pltpu.make_async_copy(x_hbm.at[at], x_ref.at[late], sems.at[0, late]),
+                    pltpu.make_async_copy(v_hbm.at[at], v_ref.at[late], sems.at[1, late]),
                 ]
             )
         )
-    for slot in range(2 * half):
-        at = window(slot)
-        for load in loads[slot]:
+    for late in range(2):
+        for load in loads[late]:
             load.wait()
-        state = dot(x_ref[at, :].T, v_ref[at, :]).astype(jnp.bfloat16)
-        for n, (begin, size) in enumerate(cuts):
-            outs[2 * n + (slot >= half)][slot % half] = state[begin : begin + size]
+        for slot in range(half):
+            at = pl.ds(slot * rows, rows)
+            state = dot(x_ref[late, at, :].T, v_ref[late, at, :]).astype(jnp.bfloat16)
+            for n, (begin, size) in enumerate(cuts):
+                outs[2 * n + late][slot] = state[begin : begin + size]
 
 
 def inside_kernel(core_ref, u_ref, after_ref, out):
@@ -110,8 +120,10 @@
         out[n] = inside.astype(jnp.bfloat16)
 
 
-def join_kernel(level, order_ref, w_ref, inside_ref, after_ref, out):
+def join_kernel(level, order_ref, w_ref, inside_ref, after_ref, out, slots_out):
     per_box = inside_ref.shape[0] // w_ref.shape[3]
+    for box in range(slots_out.shape[0]):
+        slots_out[box] = jnp.full(slots_out.shape[1:], order_ref[0, 0, box] // 2, jnp.int32)
     for n in range(out.shape[0]):
         joint = dot(w_ref[level, 0, 0, order_ref[0, 0, n // per_box]], inside_ref[n])
         out[n] = joint.astype(jnp.bfloat16)
@@ -139,7 +151,7 @@
 
 
 def last_kernel(
-    level, begin, size, order_ref, kept_ref, got_ref, joint_ref, after_ref, *outs
+    level, begin, size, slots_ref, kept_ref, got_ref, joint_ref, after_ref, *outs
 ):
     half = kept_ref.shape[0]
     me = lax.axis_index("inner")
@@ -152,7 +164,7 @@
             out = outs[t].at[odd]
             first = jnp.bitwise_xor(me, 2 * t + odd) * (piece // width)
             for n in range(piece // width):
-                k = order_ref[0, 0, (first + n) // per_box] // 2
+                k = jnp.max(slots_ref[(first + n) // per_box])
                 out[:, n * width : (n + 1) * width] = merged(
                     level, begin, size, kept_ref, got_ref, joint_ref, k, first + n
                 )
@@ -164,23 +176,53 @@
         out[t] = refs[t][1]
 
 
-def place_kernel(cuts, counts, *refs):
-    out, held, sems = refs[-3:]
+def space_kernel(after_ref, out):
+    out[...] = jnp.zeros_like(out)
+
+
+def place_kernel(cuts, counts, early, *refs):
+    out, held_out, held, sems = refs[-4:]
     rows = refs[0].shape[2]
     owners = out.shape[0] // rows
     me = lax.axis_index("inner")
     copies = []
     for step in range(owners):
-        owner = jnp.bitwise_xor(me, step)
-        window = pl.ds(pl.multiple_of(owner * rows, rows), rows)
-        for n, (begin, size) in enumerate(cuts):
-            chunk = refs[sum(counts[:n]) : sum(counts[: n + 1])]
+        whole = step < 2 * early
+        block_out = held.at[step] if whole else held_out.at[step - 2 * early]
+        for n, (begin, size) in enumerate(cuts[: None if whole else -1]):
+            at = sum(counts[:n])
+            chunk = refs[at : at + counts[n]]
             block = chunk[step // 2][0]
             if step % 2:
-                late = [(ref, t) for ref in chunk[owners // 2 :] for t in range(ref.shape[0])]
+                mine = early if n == len(cuts) - 1 else owners // 2
+                late = [(ref, t) for ref in chunk[mine:] for t in range(ref.shape[0])]
                 ref, t = late[step // 2]
                 block = ref[t]
-            held[step, :, begin : begin + size] = block.T
+            block_out[:, begin : begin + size] = block.T
+        if whole:
+            owner = jnp.bitwise_xor(me, step)
+            window = pl.ds(pl.multiple_of(owner * rows, rows), rows)
+            copies += copy_all(
+                [pltpu.make_async_copy(held.at[step], out.at[window], sems.at[step])]
+            )
+    for copy in copies:
+        copy.wait()
+
+
+def finish_kernel(cut, first_ref, held_ref, *refs):
+    even_refs, (odd_ref, out, held, sems) = refs[:-4], refs[-4:]
+    begin, size = cut
+    rows = held.shape[1]
+    late = held.shape[0]
+    first = out.shape[0] // rows - late
+    me = lax.axis_index("inner")
+    copies = []
+    for step in range(late):
+        block = odd_ref[step // 2] if step % 2 else even_refs[step // 2][0]
+        held[step] = held_ref[step]
+        held[step, :, begin : begin + size] = block.T
+        owner = jnp.bitwise_xor(me, first + step)
+        window = pl.ds(pl.multiple_of(owner * rows, rows), rows)
         copies += copy_all([pltpu.make_async_copy(held.at[step], out.at[window], sems.at[step])])
     for copy in copies:
         copy.wait()
@@ -200,6 +242,8 @@
     count = len(cuts)
     held = [None] * count
     done = [None] * count
+    swaps = [[] for _ in cuts]
+    early = inner // 4
     level_w = inside = joint = after = None
 
     for step in ORDER:
@@ -212,9 +256,9 @@
                 [vectors, leaf_basis],
                 [HBM] * 2,
                 [
-                    pltpu.VMEM(vectors.shape, jnp.bfloat16),
-                    pltpu.VMEM(leaf_basis.shape, jnp.bfloat16),
-                    pltpu.SemaphoreType.DMA((2, boxes)),
+                    pltpu.VMEM((2, vectors.shape[0] // 2, columns), jnp.bfloat16),
+                    pltpu.VMEM((2, vectors.shape[0] // 2, rank), jnp.bfloat16),
+                    pltpu.SemaphoreType.DMA((2, 2)),
                 ],
                 name="leaves",
                 room=LEAF_ROOM,
@@ -229,7 +273,7 @@
                 [arr(boxes, 2 * rank, rank)],
                 [transfer, after],
                 [HBM, ANY],
-                [pltpu.SemaphoreType.DMA],
+                [pltpu.SemaphoreType.DMA((2,))],
                 name="weights",
                 room=LOAD_ROOM,
             )[0]
@@ -244,13 +288,16 @@
             )[0]
             after = inside
         elif kind == "j":
-            joint = call(
+            joint, slots = call(
                 functools.partial(join_kernel, levels - 1),
-                [arr(vectors.shape[0] // width, 2 * rank, width)],
+                [
+                    arr(vectors.shape[0] // width, 2 * rank, width),
+                    jax.ShapeDtypeStruct((boxes, 8, 128), jnp.int32),
+                ],
                 [box_order, transfer, inside, after],
                 [SMEM, VMEM, VMEM, ANY],
                 name="join",
-            )[0]
+            )
             after = joint
         elif kind == "m":
             level = int(step[1])
@@ -272,18 +319,23 @@
             outs = call(
                 functools.partial(last_kernel, levels - 1, begin, size),
                 [arr(2, size, piece)] * (inner // 2),
-                [box_order, kept, got, joint, after],
-                [SMEM, VMEM, VMEM, VMEM, ANY],
+                [slots, kept, got, joint, after],
+                [VMEM, VMEM, VMEM, VMEM, ANY],
                 name=f"last{step[-1]}",
             )
             after = outs[0]
-            sent = [None] * (inner // 2)
+            sent = [outs[0]] + [None] * (inner // 2 - 1)
             for t in turns(inner // 2):
                 sent[t] = swapped(outs[t], "inner", 2 * t)
-            done[n] = [outs[0]] + sent[1:]
-        elif kind in "qr":
-            groups = [done[n]] if kind == "q" else [[x] for x in done[n]]
-            for group in groups:
+            done[n] = sent
+        elif kind == "x":
+            after = call(space_kernel, [arr(16, 128)], [after], [ANY], name="space")[0]
+        elif kind in "qut":
+            pairs = inner // 2
+            begin = early if kind == "t" else 0
+            end = early if kind == "u" else pairs
+            if begin < end:
+                group = done[n][begin:end]
                 after = call(
                     pack_kernel,
                     [arr(len(group), cuts[n][1], piece)],
@@ -291,19 +343,37 @@
                     [VMEM] * len(group) + [ANY],
                     name=f"pack{step[-1]}",
                 )[0]
-                done[n] = done[n] + [swapped(after, "inner", 1)]
-    flat = [x for part in done for x in part]
+                swaps[n].append(swapped(after, "inner", 1))
+        elif kind == "z":
+            counts = [len(a) + len(b) for a, b in zip(done[:-1], swaps)] + [early + 1]
+            flat = [x for n in range(count - 1) for x in done[n] + swaps[n]]
+            flat += done[-1][:early] + swaps[-1]
+            placed, rest = call(
+                functools.partial(place_kernel, cuts, counts, early),
+                [arr(*vectors.shape), arr(inner - 2 * early, piece, columns)],
+                flat + [after],
+                [VMEM] * len(flat) + [ANY],
+                [
+                    pltpu.VMEM((2 * early, piece, columns), jnp.bfloat16),
+                    pltpu.SemaphoreType.DMA((2 * early,)),
+                ],
+                name="place",
+                out_specs=[HBM, VMEM],
+            )
+            after = rest
+    flat = done[-1][early:] + swaps[-1][-1:]
     return call(
-        functools.partial(place_kernel, cuts, [len(part) for part in done]),
+        functools.partial(finish_kernel, cuts[-1]),
         [arr(*vectors.shape)],
-        flat,
-        [VMEM] * len(flat),
+        [placed, rest, *flat],
+        [HBM, VMEM] + [VMEM] * len(flat),
         [
-            pltpu.VMEM((inner, piece, columns), jnp.bfloat16),
-            pltpu.SemaphoreType.DMA((inner,)),
+            pltpu.VMEM((inner - 2 * early, piece, columns), jnp.bfloat16),
+            pltpu.SemaphoreType.DMA((inner - 2 * early,)),
         ],
-        name="place",
-        out_spec=HBM,
+        name="finish",
+        out_specs=[HBM],
+        aliases={0: 0},
     )[0]
 
 

time: 57.7 us -> 54.4 us (0.943)
  Pallas kernels: 15.7 us -> 14 us
  starting transfers between devices: 28.9 us -> 27.4 us
    pallas_call x23, Pallas kernels: 15.7 us -> 14 us  [call(): return list(run(*ins))]
    ppermute x26 -> x24, starting transfers between devices: 28.9 us -> 27.4 us  [swapped(): lax.ppermute(array, axis, [(i, i ^ step) for i in range(lax.axis_size(axi...]
    ppermute x26 -> x24, waiting for transfers between devices: 12.7 us -> 12.6 us  [swapped(): lax.ppermute(array, axis, [(i, i ^ step) for i in range(lax.axis_size(axi...]
  transfers between devices with their start and end apart: 26 -> 24, of which waited for: 8 -> 10; matrix products, arithmetic and copies ran while one was open for 0% -> 0% of each run, Pallas kernels for 19% -> 20%
where the time goes in v4:
time: 54.4 us; the launch traced here: 54.3 us
  starting transfers between devices  27.4 us (50%)
  Pallas kernels  14 us (26%)
  waiting for transfers between devices  12.6 us (23%)
    ppermute x24, starting transfers between devices, swapped(): lax.ppermute(array, axis, [(i, i ^ step) for i in range(lax.axis_size(axi...  27.4 us
    pallas_call x23, Pallas kernels, call(): return list(run(*ins))  14 us
    ppermute x24, waiting for transfers between devices, swapped(): lax.ppermute(array, axis, [(i, i ^ step) for i in range(lax.axis_size(axi...  12.6 us
  transfers between devices with their start and end apart: 24, of which 10 were waited for; matrix products, arithmetic and copies ran while one was open for 0% of the time, Pallas kernels for 20%

profile of v4, /device:TPU:0, one launch (start us, length us, event | category | flops | bytes accessed | tf_op | source)
XLA Modules:
  0.0 54.3 jit_solution(14115315730658813620)
XLA Ops:
  0.0 1.9 %leaves.1 = (bf16[4,64,256]{2,1,0:T(8,128)(2,1)S(1)}, bf16[4,64,256]{2,1,0:T(8,128)(2,1)S(1)}, bf16[4,192,256]{2,1,0:T(8,128)(2,1)S(1)}, bf16[4,192,256]{2,1,0:T(8,128)(2,1)S(1)}) custom-call(bf16[2048,256]{1,0:T(8,128)(2,1)} %x_hbm.1, bf16[2048,256]{1,0:T(8,128)(2,1)} %v_hbm.1), custom_call_target="tpu_custom_call" | custom-call | flops 2000000000 | tf_op jit(solution)/shard_map/leaves/pallas_call | solution.py:61
  1.9 0.5 collective-permute-start
  2.5 1.6 %weights.1.w_ref.after_ref = bf16[8,512,256]{2,1,0:T(8,128)(2,1)S(1)} custom-call(bf16[4,1,1,8,512,256]{5,4,3,2,1,0:T(8,128)(2,1)} %w_ref.13, bf16[4,192,256]{2,1,0:T(8,128)(2,1)S(1)} %get-tuple-element.43.after_ref.kept_ref), custom_call_target="tpu_custom_call" | custom-call | flops 2000000000 | tf_op jit(solution)/shard_map/weights/pallas_call | solution.py:61
  4.1 0.5 merge0a.1
  4.6 3.1 %collective-permute-start.3 = (bf16[4,64,256]{2,1,0:T(8,128)(2,1)S(1)}, bf16[4,64,256]{2,1,0:T(8,128)(2,1)S(1)}, u32[]{:S(2)}, u32[]{:S(2)}) collective-permute-start(bf16[4,64,256]{2,1,0:T(8,128)(2,1)S(1)} %get-tuple-element.51), channel_id=1, source_target_pairs={{0,2},{1,3},{2,0},{3,1},{4,6},{5,7},{6,4},{7,5},{8,10},{9,11},{10,... | collective-permute-start | bytes 393224 | tf_op jit(solution)/shard_map/ppermute | solution.py:27
  7.7 0.5 merge0b.1
  8.2 0.1 collective-permute-start.2
  8.3 0.5 merge0c.1
  8.8 2.1 %collective-permute-start.7 = (bf16[4,112,256]{2,1,0:T(8,128)(2,1)S(1)}, bf16[4,112,256]{2,1,0:T(8,128)(2,1)S(1)}, u32[]{:S(2)}, u32[]{:S(2)}) collective-permute-start(bf16[4,112,256]{2,1,0:T(8,128)(2,1)S(1)} %get-tuple-element.60), channel_id=1, source_target_pairs={{0,2},{1,3},{2,0},{3,1},{4,6},{5,7},{6,4},{7,5},{8,10},{9,11},{10,... | collective-permute-start | bytes 688136 | tf_op jit(solution)/shard_map/ppermute | solution.py:27
  10.8 0.5 inside.1.after_ref.inside_ref
  11.3 0.7 %collective-permute-done.3.got_ref = bf16[4,64,256]{2,1,0:T(8,128)(2,1)S(1)} collective-permute-done((bf16[4,64,256]{2,1,0:T(8,128)(2,1)S(1)}, bf16[4,64,256]{2,1,0:T(8,128)(2,1)S(1)}, u32[]{:S(2)}, u32[]{:S(2)}) %collective-permute-start.3) | collective-permute-done | bytes 131104 | tf_op jit(solution)/shard_map/ppermute | solution.py:27
  12.0 0.5 merge1a.1
  12.5 2.0 %collective-permute-start.4 = (bf16[4,64,256]{2,1,0:T(8,128)(2,1)S(1)}, bf16[4,64,256]{2,1,0:T(8,128)(2,1)S(1)}, u32[]{:S(2)}, u32[]{:S(2)}) collective-permute-start(bf16[4,64,256]{2,1,0:T(8,128)(2,1)S(1)} %get-tuple-element.55), channel_id=1, source_target_pairs={{0,8},{8,0},{16,24},{24,16},{1,9},{9,1},{17,25},{25,17},{2,10},{10... | collective-permute-start | bytes 393224 | tf_op jit(solution)/shard_map/ppermute | solution.py:27
  14.5 1.0 %collective-permute-done.2.got_ref = bf16[4,80,256]{2,1,0:T(8,128)(2,1)S(1)} collective-permute-done((bf16[4,80,256]{2,1,0:T(8,128)(2,1)S(1)}, bf16[4,80,256]{2,1,0:T(8,128)(2,1)S(1)}, u32[]{:S(2)}, u32[]{:S(2)}) %collective-permute-start.2) | collective-permute-done | bytes 163872 | tf_op jit(solution)/shard_map/ppermute | solution.py:27
  15.5 0.5 merge1b.1
  16.0 2.0 %collective-permute-start.6 = (bf16[4,80,256]{2,1,0:T(8,128)(2,1)S(1)}, bf16[4,80,256]{2,1,0:T(8,128)(2,1)S(1)}, u32[]{:S(2)}, u32[]{:S(2)}) collective-permute-start(bf16[4,80,256]{2,1,0:T(8,128)(2,1)S(1)} %get-tuple-element.59), channel_id=1, source_target_pairs={{0,8},{8,0},{16,24},{24,16},{1,9},{9,1},{17,25},{25,17},{2,10},{10... | collective-permute-start | bytes 491528 | tf_op jit(solution)/shard_map/ppermute | solution.py:27
  18.0 1.3 %join.1 = (bf16[8,512,256]{2,1,0:T(8,128)(2,1)S(1)}, s32[8,8,128]{2,1,0:T(8,128)S(1)}) custom-call(s32[1,1,8]{2,1,0:T(1,128)S(1)} %copy-done.2, bf16[4,1,1,8,512,256]{5,4,3,2,1,0:T(8,128)(2,1)S(1)} %bitcast.1, bf16[8,256,256]{2,1,0:T(8,128)(2,1)S(1)} %inside.1.after_ref.inside_ref, bf16[4,80,256]{2,1,0:T(8,128)(2,1)S(1)} %get-tuple-element.53.after_ref.kept_ref), custom_call_target="tpu_custom_call" | custom-call | flops 300000000 | tf_op jit(solution)/shard_map/join/pallas_call | solution.py:61
  19.3 0.5 merge2a.1
  19.8 1.6 %collective-permute-start.5 = (bf16[4,64,256]{2,1,0:T(8,128)(2,1)S(1)}, bf16[4,64,256]{2,1,0:T(8,128)(2,1)S(1)}, u32[]{:S(2)}, u32[]{:S(2)}) collective-permute-start(bf16[4,64,256]{2,1,0:T(8,128)(2,1)S(1)} %get-tuple-element.58), channel_id=1, source_target_pairs={{0,16},{8,24},{16,0},{24,8},{1,17},{9,25},{17,1},{25,9},{2,18},{10... | collective-permute-start | bytes 393224 | tf_op jit(solution)/shard_map/ppermute | solution.py:27
  21.4 0.5 merge1c.1
  21.9 0.7 %collective-permute-start.12 = (bf16[4,112,256]{2,1,0:T(8,128)(2,1)S(1)}, bf16[4,112,256]{2,1,0:T(8,128)(2,1)S(1)}, u32[]{:S(2)}, u32[]{:S(2)}) collective-permute-start(bf16[4,112,256]{2,1,0:T(8,128)(2,1)S(1)} %get-tuple-element.68), channel_id=1, source_target_pairs={{0,8},{8,0},{16,24},{24,16},{1,9},{9,1},{17,25},{25,17},{2,10},{10... | collective-permute-start | bytes 688136 | tf_op jit(solution)/shard_map/ppermute | solution.py:27
  22.7 0.5 merge2b.1
  23.2 1.0 %collective-permute-start.11 = (bf16[4,80,256]{2,1,0:T(8,128)(2,1)S(1)}, bf16[4,80,256]{2,1,0:T(8,128)(2,1)S(1)}, u32[]{:S(2)}, u32[]{:S(2)}) collective-permute-start(bf16[4,80,256]{2,1,0:T(8,128)(2,1)S(1)} %get-tuple-element.67), channel_id=1, source_target_pairs={{0,16},{8,24},{16,0},{24,8},{1,17},{9,25},{17,1},{25,9},{2,18},{10... | collective-permute-start | bytes 491528 | tf_op jit(solution)/shard_map/ppermute | solution.py:27
  24.2 1.4 %collective-permute-done.5.got_ref = bf16[4,64,256]{2,1,0:T(8,128)(2,1)S(1)} collective-permute-done((bf16[4,64,256]{2,1,0:T(8,128)(2,1)S(1)}, bf16[4,64,256]{2,1,0:T(8,128)(2,1)S(1)}, u32[]{:S(2)}, u32[]{:S(2)}) %collective-permute-start.5) | collective-permute-done | bytes 131104 | tf_op jit(solution)/shard_map/ppermute | solution.py:27
  25.6 0.7 %lasta.1 = (bf16[2,64,256]{2,1,0:T(8,128)(2,1)S(1)}, bf16[2,64,256]{2,1,0:T(8,128)(2,1)S(1)}, bf16[2,64,256]{2,1,0:T(8,128)(2,1)S(1)}, bf16[2,64,256]{2,1,0:T(8,128)(2,1)S(1)}) custom-call(s32[8,8,128]{2,1,0:T(8,128)S(1)} %get-tuple-element.54.slots_ref, bf16[4,64,256]{2,1,0:T(8,128)(2,1)S(1)} %get-tuple-element.57.after_ref.kept_ref, ...), custom_call_target="tpu_custom_call" | custom-call | flops 1000000000 | tf_op jit(solution)/shard_map/lasta/pallas_call | solution.py:61
  26.2 1.6 %collective-permute-start.8 = (bf16[2,64,256]{2,1,0:T(8,128)(2,1)S(1)}, bf16[2,64,256]{2,1,0:T(8,128)(2,1)S(1)}, u32[]{:S(2)}, u32[]{:S(2)}) collective-permute-start(bf16[2,64,256]{2,1,0:T(8,128)(2,1)S(1)} %get-tuple-element.64), channel_id=1, source_target_pairs={{0,2},{1,3},{2,0},{3,1},{4,6},{5,7},{6,4},{7,5},{8,10},{9,11},{10,... | collective-permute-start | bytes 196616 | tf_op jit(solution)/shard_map/ppermute | solution.py:27
  27.9 2.6 %collective-permute-start.9 = (bf16[2,64,256]{2,1,0:T(8,128)(2,1)S(1)}, bf16[2,64,256]{2,1,0:T(8,128)(2,1)S(1)}, u32[]{:S(2)}, u32[]{:S(2)}) collective-permute-start(bf16[2,64,256]{2,1,0:T(8,128)(2,1)S(1)} %get-tuple-element.65), channel_id=1, source_target_pairs={{0,4},{1,5},{2,6},{3,7},{4,0},{5,1},{6,2},{7,3},{8,12},{9,13},{10,... | collective-permute-start | bytes 196616 | tf_op jit(solution)/shard_map/ppermute | solution.py:27
  30.5 0.2 collective-permute-start.10
  30.7 0.5 merge2c.1
  31.2 1.6 %collective-permute-start.17 = (bf16[4,112,256]{2,1,0:T(8,128)(2,1)S(1)}, bf16[4,112,256]{2,1,0:T(8,128)(2,1)S(1)}, u32[]{:S(2)}, u32[]{:S(2)}) collective-permute-start(bf16[4,112,256]{2,1,0:T(8,128)(2,1)S(1)} %get-tuple-element.74), channel_id=1, source_target_pairs={{0,16},{8,24},{16,0},{24,8},{1,17},{9,25},{17,1},{25,9},{2,18},{10... | collective-permute-start | bytes 688136 | tf_op jit(solution)/shard_map/ppermute | solution.py:27
  32.8 0.7 %lastb.1 = (bf16[2,80,256]{2,1,0:T(8,128)(2,1)S(1)}, bf16[2,80,256]{2,1,0:T(8,128)(2,1)S(1)}, bf16[2,80,256]{2,1,0:T(8,128)(2,1)S(1)}, bf16[2,80,256]{2,1,0:T(8,128)(2,1)S(1)}) custom-call(s32[8,8,128]{2,1,0:T(8,128)S(1)} %get-tuple-element.54.slots_ref, bf16[4,80,256]{2,1,0:T(8,128)(2,1)S(1)} %get-tuple-element.62.after_ref.kept_ref, ...), custom_call_target="tpu_custom_call" | custom-call | flops 100000000 | tf_op jit(solution)/shard_map/lastb/pallas_call | solution.py:61
  33.4 0.8 %collective-permute-start.14 = (bf16[2,80,256]{2,1,0:T(8,128)(2,1)S(1)}, bf16[2,80,256]{2,1,0:T(8,128)(2,1)S(1)}, u32[]{:S(2)}, u32[]{:S(2)}) collective-permute-start(bf16[2,80,256]{2,1,0:T(8,128)(2,1)S(1)} %get-tuple-element.71), channel_id=1, source_target_pairs={{0,2},{1,3},{2,0},{3,1},{4,6},{5,7},{6,4},{7,5},{8,10},{9,11},{10,... | collective-permute-start | bytes 245768 | tf_op jit(solution)/shard_map/ppermute | solution.py:27
  34.2 3.5 %collective-permute-start.15 = (bf16[2,80,256]{2,1,0:T(8,128)(2,1)S(1)}, bf16[2,80,256]{2,1,0:T(8,128)(2,1)S(1)}, u32[]{:S(2)}, u32[]{:S(2)}) collective-permute-start(bf16[2,80,256]{2,1,0:T(8,128)(2,1)S(1)} %get-tuple-element.72), channel_id=1, source_target_pairs={{0,4},{1,5},{2,6},{3,7},{4,0},{5,1},{6,2},{7,3},{8,12},{9,13},{10,... | collective-permute-start | bytes 245768 | tf_op jit(solution)/shard_map/ppermute | solution.py:27
  37.7 0.2 collective-permute-start.16
  37.9 0.7 %lastc.1 = (bf16[2,112,256]{2,1,0:T(8,128)(2,1)S(1)}, bf16[2,112,256]{2,1,0:T(8,128)(2,1)S(1)}, bf16[2,112,256]{2,1,0:T(8,128)(2,1)S(1)}, bf16[2,112,256]{2,1,0:T(8,128)(2,1)S(1)}) custom-call(s32[8,8,128]{2,1,0:T(8,128)S(1)} %get-tuple-element.54.slots_ref, bf16[4,112,256]{2,1,0:T(8,128)(2,1)S(1)} %get-tuple-element.69.after_ref.kept_ref, ...), custom_call_target="tpu_custom_call" | custom-call | flops 400000000 | tf_op jit(solution)/shard_map/lastc/pallas_call | solution.py:61
  38.6 0.6 %collective-permute-start.19 = (bf16[2,112,256]{2,1,0:T(8,128)(2,1)S(1)}, bf16[2,112,256]{2,1,0:T(8,128)(2,1)S(1)}, u32[]{:S(2)}, u32[]{:S(2)}) collective-permute-start(bf16[2,112,256]{2,1,0:T(8,128)(2,1)S(1)} %get-tuple-element.76), channel_id=1, source_target_pairs={{0,2},{1,3},{2,0},{3,1},{4,6},{5,7},{6,4},{7,5},{8,10},{9,11},{10,... | collective-permute-start | bytes 344072 | tf_op jit(solution)/shard_map/ppermute | solution.py:27
  39.2 1.2 %collective-permute-done.14.refs_1_.refs_6_ = bf16[2,80,256]{2,1,0:T(8,128)(2,1)S(1)} collective-permute-done((bf16[2,80,256]{2,1,0:T(8,128)(2,1)S(1)}, bf16[2,80,256]{2,1,0:T(8,128)(2,1)S(1)}, u32[]{:S(2)}, u32[]{:S(2)}) %collective-permute-start.14) | collective-permute-done | bytes 81952 | tf_op jit(solution)/shard_map/ppermute | solution.py:27
  40.4 2.5 %collective-permute-start.21 = (bf16[2,112,256]{2,1,0:T(8,128)(2,1)S(1)}, bf16[2,112,256]{2,1,0:T(8,128)(2,1)S(1)}, u32[]{:S(2)}, u32[]{:S(2)}) collective-permute-start(bf16[2,112,256]{2,1,0:T(8,128)(2,1)S(1)} %get-tuple-element.79), channel_id=1, source_target_pairs={{0,4},{1,5},{2,6},{3,7},{4,0},{5,1},{6,2},{7,3},{8,12},{9,13},{10,... | collective-permute-start | bytes 344072 | tf_op jit(solution)/shard_map/ppermute | solution.py:27
  42.8 0.3 collective-permute-start.22
  43.2 0.9 %collective-permute-done.16.refs_3_.refs_8_ = bf16[2,80,256]{2,1,0:T(8,128)(2,1)S(1)} collective-permute-done((bf16[2,80,256]{2,1,0:T(8,128)(2,1)S(1)}, bf16[2,80,256]{2,1,0:T(8,128)(2,1)S(1)}, u32[]{:S(2)}, u32[]{:S(2)}) %collective-permute-start.16) | collective-permute-done | bytes 81952 | tf_op jit(solution)/shard_map/ppermute | solution.py:27
  44.1 0.3 collective-permute-done.19.refs_1_.refs_11_
  44.5 0.2 collective-permute-start.20
  44.7 0.8 %collective-permute-done.18.refs_9_ = bf16[4,80,256]{2,1,0:T(8,128)(2,1)S(1)} collective-permute-done((bf16[4,80,256]{2,1,0:T(8,128)(2,1)S(1)}, bf16[4,80,256]{2,1,0:T(8,128)(2,1)S(1)}, u32[]{:S(2)}, u32[]{:S(2)}) %collective-permute-start.18) | collective-permute-done | bytes 163872 | tf_op jit(solution)/shard_map/ppermute | solution.py:27
  45.5 0.4 collective-permute-done.20.refs_12_
  45.9 1.4 %place.1 = (bf16[2048,256]{1,0:T(8,128)(2,1)}, bf16[4,256,256]{2,1,0:T(8,128)(2,1)S(1)}) custom-call(bf16[2,64,256]{2,1,0:T(8,128)(2,1)S(1)} %get-tuple-element.63.after_ref.refs_0_, bf16[2,64,256]{2,1,0:T(8,128)(2,1)S(1)} %collective-permute-done.8.refs_1_, bf16[2,64,256]{2,1,0:T(8,128)(2,1)S(1)} %collective-permute-done.9.refs_2_, ...), custom_call_target="tpu_custom_call" | custom-call | flops 5000000000 | tf_op jit(solution)/shard_map/place/pallas_call | solution.py:61
  47.3 4.6 %collective-permute-done.21.refs_0_ = bf16[2,112,256]{2,1,0:T(8,128)(2,1)S(1)} collective-permute-done((bf16[2,112,256]{2,1,0:T(8,128)(2,1)S(1)}, bf16[2,112,256]{2,1,0:T(8,128)(2,1)S(1)}, u32[]{:S(2)}, u32[]{:S(2)}) %collective-permute-start.21) | collective-permute-done | bytes 114720 | tf_op jit(solution)/shard_map/ppermute | solution.py:27
  52.0 1.3 %collective-permute-done.23.refs_2_ = bf16[2,112,256]{2,1,0:T(8,128)(2,1)S(1)} collective-permute-done((bf16[2,112,256]{2,1,0:T(8,128)(2,1)S(1)}, bf16[2,112,256]{2,1,0:T(8,128)(2,1)S(1)}, u32[]{:S(2)}, u32[]{:S(2)}) %collective-permute-start.23) | collective-permute-done | bytes 114720 | tf_op jit(solution)/shard_map/ppermute | solution.py:27
  53.3 1.0 %finish.1 = bf16[2048,256]{1,0:T(8,128)(2,1)} custom-call(bf16[2048,256]{1,0:T(8,128)(2,1)} %get-tuple-element.77.first_ref, bf16[4,256,256]{2,1,0:T(8,128)(2,1)S(1)} %get-tuple-element.78.refs_2_.held_ref, bf16[2,112,256]{2,1,0:T(8,128)(2,1)S(1)} %collective-permute-done.21.refs_0_, ...), custom_call_target="tpu_custom_call", output_to_operand_aliasing={{}: (0, {})} | custom-call | flops 2000000000 | tf_op jit(solution)/shard_map/finish/pallas_call | solution.py:61
  (34 shorter events, 0.3 us)
Async XLA Ops:
  1.9 5.7 %collective-permute-start = (bf16[4,192,256]{2,1,0:T(8,128)(2,1)S(1)}, bf16[4,192,256]{2,1,0:T(8,128)(2,1)S(1)}, u32[]{:S(2)}, u32[]{:S(2)}) collective-permute-start(bf16[4,192,256]{2,1,0:T(8,128)(2,1)S(1)} %get-tuple-element.44), channel_id=1, source_target_pairs={{0,1},{1,0},{2,3},{3,2},{4,5},{5,4},{6,7},{7,6},{8,9},{9,8},{10,11... | collective-permute-start | bytes 1179656 | tf_op jit(solution)/shard_map/ppermute | solution.py:27
  2.5 1.6 %collective-permute-start.1 = (bf16[4,64,256]{2,1,0:T(8,128)(2,1)S(1)}, bf16[4,64,256]{2,1,0:T(8,128)(2,1)S(1)}, u32[]{:S(2)}, u32[]{:S(2)}) collective-permute-start(bf16[4,64,256]{2,1,0:T(8,128)(2,1)S(1)} %get-tuple-element.46), channel_id=1, source_target_pairs={{0,1},{1,0},{2,3},{3,2},{4,5},{5,4},{6,7},{7,6},{8,9},{9,8},{10,11... | collective-permute-start | bytes 393224 | tf_op jit(solution)/shard_map/ppermute | solution.py:27
  4.6 7.4 %collective-permute-start.3 = (bf16[4,64,256]{2,1,0:T(8,128)(2,1)S(1)}, bf16[4,64,256]{2,1,0:T(8,128)(2,1)S(1)}, u32[]{:S(2)}, u32[]{:S(2)}) collective-permute-start(bf16[4,64,256]{2,1,0:T(8,128)(2,1)S(1)} %get-tuple-element.51), channel_id=1, source_target_pairs={{0,2},{1,3},{2,0},{3,1},{4,6},{5,7},{6,4},{7,5},{8,10},{9,11},{10,... | collective-permute-start | bytes 393224 | tf_op jit(solution)/shard_map/ppermute | solution.py:27
  7.7 4.3 %slice-start = ((s8[8388608]{0:T(1024)(128)(4,1)}), s8[4194304]{0:T(1024)(128)(4,1)S(1)}, s32[]{:S(2)}) async-start(s8[8388608]{0:T(1024)(128)(4,1)} %bitcast), calls=%async_computation | async-start | bytes 8388608
  8.2 7.3 %collective-permute-start.2 = (bf16[4,80,256]{2,1,0:T(8,128)(2,1)S(1)}, bf16[4,80,256]{2,1,0:T(8,128)(2,1)S(1)}, u32[]{:S(2)}, u32[]{:S(2)}) collective-permute-start(bf16[4,80,256]{2,1,0:T(8,128)(2,1)S(1)} %get-tuple-element.50), channel_id=1, source_target_pairs={{0,2},{1,3},{2,0},{3,1},{4,6},{5,7},{6,4},{7,5},{8,10},{9,11},{10,... | collective-permute-start | bytes 491528 | tf_op jit(solution)/shard_map/ppermute | solution.py:27
  8.3 2.5 %copy-start = (bf16[1,1,8,256,256]{4,3,2,1,0:T(8,128)(2,1)S(1)}, bf16[1,1,8,256,256]{4,3,2,1,0:T(8,128)(2,1)}, u32[]{:S(2)}) copy-start(bf16[1,1,8,256,256]{4,3,2,1,0:T(8,128)(2,1)} %core_ref.1) | copy-start | bytes 3145732
  8.3 2.5 %copy-start.1 = (bf16[2048,256]{1,0:T(8,128)(2,1)S(1)}, bf16[2048,256]{1,0:T(8,128)(2,1)}, u32[]{:S(2)}) copy-start(bf16[2048,256]{1,0:T(8,128)(2,1)} %u_ref.1) | copy-start | bytes 3145732
  8.3 3.7 %slice-start.1 = ((s8[8388608]{0:T(1024)(128)(4,1)}), s8[4194304]{0:T(1024)(128)(4,1)S(1)}, s32[]{:S(2)}) async-start(s8[8388608]{0:T(1024)(128)(4,1)} %bitcast), calls=%async_computation.1 | async-start | bytes 8388608
  8.8 12.7 %collective-permute-start.7 = (bf16[4,112,256]{2,1,0:T(8,128)(2,1)S(1)}, bf16[4,112,256]{2,1,0:T(8,128)(2,1)S(1)}, u32[]{:S(2)}, u32[]{:S(2)}) collective-permute-start(bf16[4,112,256]{2,1,0:T(8,128)(2,1)S(1)} %get-tuple-element.60), channel_id=1, source_target_pairs={{0,2},{1,3},{2,0},{3,1},{4,6},{5,7},{6,4},{7,5},{8,10},{9,11},{10,... | collective-permute-start | bytes 688136 | tf_op jit(solution)/shard_map/ppermute | solution.py:27
  12.5 6.8 %collective-permute-start.4 = (bf16[4,64,256]{2,1,0:T(8,128)(2,1)S(1)}, bf16[4,64,256]{2,1,0:T(8,128)(2,1)S(1)}, u32[]{:S(2)}, u32[]{:S(2)}) collective-permute-start(bf16[4,64,256]{2,1,0:T(8,128)(2,1)S(1)} %get-tuple-element.55), channel_id=1, source_target_pairs={{0,8},{8,0},{16,24},{24,16},{1,9},{9,1},{17,25},{25,17},{2,10},{10... | collective-permute-start | bytes 393224 | tf_op jit(solution)/shard_map/ppermute | solution.py:27
  15.5 2.5 %copy-start.2 = (s32[1,1,8]{2,1,0:T(1,128)S(1)}, s32[1,1,8]{2,1,0:T(1,128)}, u32[]{:S(2)}) copy-start(s32[1,1,8]{2,1,0:T(1,128)} %order_ref.1) | copy-start | bytes 100
  16.0 6.7 %collective-permute-start.6 = (bf16[4,80,256]{2,1,0:T(8,128)(2,1)S(1)}, bf16[4,80,256]{2,1,0:T(8,128)(2,1)S(1)}, u32[]{:S(2)}, u32[]{:S(2)}) collective-permute-start(bf16[4,80,256]{2,1,0:T(8,128)(2,1)S(1)} %get-tuple-element.59), channel_id=1, source_target_pairs={{0,8},{8,0},{16,24},{24,16},{1,9},{9,1},{17,25},{25,17},{2,10},{10... | collective-permute-start | bytes 491528 | tf_op jit(solution)/shard_map/ppermute | solution.py:27
  19.8 5.7 %collective-permute-start.5 = (bf16[4,64,256]{2,1,0:T(8,128)(2,1)S(1)}, bf16[4,64,256]{2,1,0:T(8,128)(2,1)S(1)}, u32[]{:S(2)}, u32[]{:S(2)}) collective-permute-start(bf16[4,64,256]{2,1,0:T(8,128)(2,1)S(1)} %get-tuple-element.58), channel_id=1, source_target_pairs={{0,16},{8,24},{16,0},{24,8},{1,17},{9,25},{17,1},{25,9},{2,18},{10... | collective-permute-start | bytes 393224 | tf_op jit(solution)/shard_map/ppermute | solution.py:27
  21.9 8.8 %collective-permute-start.12 = (bf16[4,112,256]{2,1,0:T(8,128)(2,1)S(1)}, bf16[4,112,256]{2,1,0:T(8,128)(2,1)S(1)}, u32[]{:S(2)}, u32[]{:S(2)}) collective-permute-start(bf16[4,112,256]{2,1,0:T(8,128)(2,1)S(1)} %get-tuple-element.68), channel_id=1, source_target_pairs={{0,8},{8,0},{16,24},{24,16},{1,9},{9,1},{17,25},{25,17},{2,10},{10... | collective-permute-start | bytes 688136 | tf_op jit(solution)/shard_map/ppermute | solution.py:27
  23.2 9.6 %collective-permute-start.11 = (bf16[4,80,256]{2,1,0:T(8,128)(2,1)S(1)}, bf16[4,80,256]{2,1,0:T(8,128)(2,1)S(1)}, u32[]{:S(2)}, u32[]{:S(2)}) collective-permute-start(bf16[4,80,256]{2,1,0:T(8,128)(2,1)S(1)} %get-tuple-element.67), channel_id=1, source_target_pairs={{0,16},{8,24},{16,0},{24,8},{1,17},{9,25},{17,1},{25,9},{2,18},{10... | collective-permute-start | bytes 491528 | tf_op jit(solution)/shard_map/ppermute | solution.py:27
  26.2 8.0 %collective-permute-start.8 = (bf16[2,64,256]{2,1,0:T(8,128)(2,1)S(1)}, bf16[2,64,256]{2,1,0:T(8,128)(2,1)S(1)}, u32[]{:S(2)}, u32[]{:S(2)}) collective-permute-start(bf16[2,64,256]{2,1,0:T(8,128)(2,1)S(1)} %get-tuple-element.64), channel_id=1, source_target_pairs={{0,2},{1,3},{2,0},{3,1},{4,6},{5,7},{6,4},{7,5},{8,10},{9,11},{10,... | collective-permute-start | bytes 196616 | tf_op jit(solution)/shard_map/ppermute | solution.py:27
  27.9 9.8 %collective-permute-start.9 = (bf16[2,64,256]{2,1,0:T(8,128)(2,1)S(1)}, bf16[2,64,256]{2,1,0:T(8,128)(2,1)S(1)}, u32[]{:S(2)}, u32[]{:S(2)}) collective-permute-start(bf16[2,64,256]{2,1,0:T(8,128)(2,1)S(1)} %get-tuple-element.65), channel_id=1, source_target_pairs={{0,4},{1,5},{2,6},{3,7},{4,0},{5,1},{6,2},{7,3},{8,12},{9,13},{10,... | collective-permute-start | bytes 196616 | tf_op jit(solution)/shard_map/ppermute | solution.py:27
  30.5 7.4 %collective-permute-start.10 = (bf16[2,64,256]{2,1,0:T(8,128)(2,1)S(1)}, bf16[2,64,256]{2,1,0:T(8,128)(2,1)S(1)}, u32[]{:S(2)}, u32[]{:S(2)}) collective-permute-start(bf16[2,64,256]{2,1,0:T(8,128)(2,1)S(1)} %get-tuple-element.66), channel_id=1, source_target_pairs={{0,6},{1,7},{2,4},{3,5},{4,2},{5,3},{6,0},{7,1},{8,14},{9,15},{10,... | collective-permute-start | bytes 196616 | tf_op jit(solution)/shard_map/ppermute | solution.py:27
  31.2 6.7 %collective-permute-start.17 = (bf16[4,112,256]{2,1,0:T(8,128)(2,1)S(1)}, bf16[4,112,256]{2,1,0:T(8,128)(2,1)S(1)}, u32[]{:S(2)}, u32[]{:S(2)}) collective-permute-start(bf16[4,112,256]{2,1,0:T(8,128)(2,1)S(1)} %get-tuple-element.74), channel_id=1, source_target_pairs={{0,16},{8,24},{16,0},{24,8},{1,17},{9,25},{17,1},{25,9},{2,18},{10... | collective-permute-start | bytes 688136 | tf_op jit(solution)/shard_map/ppermute | solution.py:27
  33.4 6.9 %collective-permute-start.14 = (bf16[2,80,256]{2,1,0:T(8,128)(2,1)S(1)}, bf16[2,80,256]{2,1,0:T(8,128)(2,1)S(1)}, u32[]{:S(2)}, u32[]{:S(2)}) collective-permute-start(bf16[2,80,256]{2,1,0:T(8,128)(2,1)S(1)} %get-tuple-element.71), channel_id=1, source_target_pairs={{0,2},{1,3},{2,0},{3,1},{4,6},{5,7},{6,4},{7,5},{8,10},{9,11},{10,... | collective-permute-start | bytes 245768 | tf_op jit(solution)/shard_map/ppermute | solution.py:27
  34.2 8.7 %collective-permute-start.15 = (bf16[2,80,256]{2,1,0:T(8,128)(2,1)S(1)}, bf16[2,80,256]{2,1,0:T(8,128)(2,1)S(1)}, u32[]{:S(2)}, u32[]{:S(2)}) collective-permute-start(bf16[2,80,256]{2,1,0:T(8,128)(2,1)S(1)} %get-tuple-element.72), channel_id=1, source_target_pairs={{0,4},{1,5},{2,6},{3,7},{4,0},{5,1},{6,2},{7,3},{8,12},{9,13},{10,... | collective-permute-start | bytes 245768 | tf_op jit(solution)/shard_map/ppermute | solution.py:27
  37.7 6.3 %collective-permute-start.16 = (bf16[2,80,256]{2,1,0:T(8,128)(2,1)S(1)}, bf16[2,80,256]{2,1,0:T(8,128)(2,1)S(1)}, u32[]{:S(2)}, u32[]{:S(2)}) collective-permute-start(bf16[2,80,256]{2,1,0:T(8,128)(2,1)S(1)} %get-tuple-element.73), channel_id=1, source_target_pairs={{0,6},{1,7},{2,4},{3,5},{4,2},{5,3},{6,0},{7,1},{8,14},{9,15},{10,... | collective-permute-start | bytes 245768 | tf_op jit(solution)/shard_map/ppermute | solution.py:27
  38.6 5.9 %collective-permute-start.19 = (bf16[2,112,256]{2,1,0:T(8,128)(2,1)S(1)}, bf16[2,112,256]{2,1,0:T(8,128)(2,1)S(1)}, u32[]{:S(2)}, u32[]{:S(2)}) collective-permute-start(bf16[2,112,256]{2,1,0:T(8,128)(2,1)S(1)} %get-tuple-element.76), channel_id=1, source_target_pairs={{0,2},{1,3},{2,0},{3,1},{4,6},{5,7},{6,4},{7,5},{8,10},{9,11},{10,... | collective-permute-start | bytes 344072 | tf_op jit(solution)/shard_map/ppermute | solution.py:27
  39.2 5.5 %collective-permute-start.13 = (bf16[4,64,256]{2,1,0:T(8,128)(2,1)S(1)}, bf16[4,64,256]{2,1,0:T(8,128)(2,1)S(1)}, u32[]{:S(2)}, u32[]{:S(2)}) collective-permute-start(bf16[4,64,256]{2,1,0:T(8,128)(2,1)S(1)} %packa.1.after_ref), channel_id=1, source_target_pairs={{0,1},{1,0},{2,3},{3,2},{4,5},{5,4},{6,7},{7,6},{8,9},{9,8},{10,11... | collective-permute-start | bytes 393224 | tf_op jit(solution)/shard_map/ppermute | solution.py:27
  40.4 11.5 %collective-permute-start.21 = (bf16[2,112,256]{2,1,0:T(8,128)(2,1)S(1)}, bf16[2,112,256]{2,1,0:T(8,128)(2,1)S(1)}, u32[]{:S(2)}, u32[]{:S(2)}) collective-permute-start(bf16[2,112,256]{2,1,0:T(8,128)(2,1)S(1)} %get-tuple-element.79), channel_id=1, source_target_pairs={{0,4},{1,5},{2,6},{3,7},{4,0},{5,1},{6,2},{7,3},{8,12},{9,13},{10,... | collective-permute-start | bytes 344072 | tf_op jit(solution)/shard_map/ppermute | solution.py:27
  42.8 9.0 %collective-permute-start.22 = (bf16[2,112,256]{2,1,0:T(8,128)(2,1)S(1)}, bf16[2,112,256]{2,1,0:T(8,128)(2,1)S(1)}, u32[]{:S(2)}, u32[]{:S(2)}) collective-permute-start(bf16[2,112,256]{2,1,0:T(8,128)(2,1)S(1)} %get-tuple-element.80), channel_id=1, source_target_pairs={{0,6},{1,7},{2,4},{3,5},{4,2},{5,3},{6,0},{7,1},{8,14},{9,15},{10,... | collective-permute-start | bytes 344072 | tf_op jit(solution)/shard_map/ppermute | solution.py:27
  44.0 1.5 %collective-permute-start.18 = (bf16[4,80,256]{2,1,0:T(8,128)(2,1)S(1)}, bf16[4,80,256]{2,1,0:T(8,128)(2,1)S(1)}, u32[]{:S(2)}, u32[]{:S(2)}) collective-permute-start(bf16[4,80,256]{2,1,0:T(8,128)(2,1)S(1)} %packb.1.refs_2_), channel_id=1, source_target_pairs={{0,1},{1,0},{2,3},{3,2},{4,5},{5,4},{6,7},{7,6},{8,9},{9,8},{10,11... | collective-permute-start | bytes 491528 | tf_op jit(solution)/shard_map/ppermute | solution.py:27
  44.5 1.4 %collective-permute-start.20 = (bf16[2,112,256]{2,1,0:T(8,128)(2,1)S(1)}, bf16[2,112,256]{2,1,0:T(8,128)(2,1)S(1)}, u32[]{:S(2)}, u32[]{:S(2)}) collective-permute-start(bf16[2,112,256]{2,1,0:T(8,128)(2,1)S(1)} %packc.2.after_ref), channel_id=1, source_target_pairs={{0,1},{1,0},{2,3},{3,2},{4,5},{5,4},{6,7},{7,6},{8,9},{9,8},{10,11... | collective-permute-start | bytes 344072 | tf_op jit(solution)/shard_map/ppermute | solution.py:27
  51.9 1.4 %collective-permute-start.23 = (bf16[2,112,256]{2,1,0:T(8,128)(2,1)S(1)}, bf16[2,112,256]{2,1,0:T(8,128)(2,1)S(1)}, u32[]{:S(2)}, u32[]{:S(2)}) collective-permute-start(bf16[2,112,256]{2,1,0:T(8,128)(2,1)S(1)} %packc.3), channel_id=1, source_target_pairs={{0,1},{1,0},{2,3},{3,2},{4,5},{5,4},{6,7},{7,6},{8,9},{9,8},{10,11... | collective-permute-start | bytes 344072 | tf_op jit(solution)/shard_map/ppermute | solution.py:27

commit v5 on v4

--- a/solution.py
+++ b/solution.py
@@ -8,19 +8,64 @@
 from jax.sharding import PartitionSpec as P
 
 INNER_LEVELS = 2
-PARTS = (4, 5, 7)
-COSTS = {"merge2c":.4,"lastb":.1,"lastc":.4,"packc":2,"lasta":1,"packa":2,"packb":1,"merge1b":.4,"join":.3,"inside":.3,"merge2a":.4,"merge1a":1,"place":5,"space":10}
-ORDER = ("f", "w", "m0a", "m0b", "m0c", "i", "m1a", "m1b", "j", "m2a", "m1c", "m2b", "oa", "m2c", "ob", "qa", "oc", "qb", "uc", "x", "z", "tc")
+PARTS = (4, 6, 6)
+GROUPS = ("a", "b", "c")
+XS = 1
+TURN = 1
+COSTS = {
+    "merge2c": 1,
+    "lastb": 0.1,
+    "lastc": 10,
+    "packc": 10,
+    "lasta": 1,
+    "packa": 5,
+    "packb": 10,
+    "merge1b": 0.4,
+    "join": 0.3,
+    "inside": 0.3,
+    "merge2a": 0.4,
+    "merge1a": 1,
+    "place": 10,
+    "space": 10,
+    "merge1c": 1,
+    "weights": 1,
+    "merge0a": 10,
+    "farc": 0.4,
+    "couplec": 10,
+    "holda": 5,
+}
+ORDER = (
+    "f",
+    "w",
+    "m0a",
+    "m0c",
+    "m0b",
+    "i",
+    "m1a",
+    "m1b",
+    "m2a",
+    "j",
+    "m1c",
+    "m2b",
+    "oa",
+    "m2c",
+    "ob",
+    "ya",
+    "efc",
+    "onc",
+    "pc",
+    "qa",
+    "qb",
+    "uc",
+    "x",
+    "z",
+)
 LEAF_ROOM = 52
 LOAD_ROOM = 48
 HBM = pl.BlockSpec(memory_space=pltpu.HBM)
 VMEM = pl.BlockSpec(memory_space=pltpu.VMEM)
 ANY = pl.BlockSpec(memory_space=pl.ANY)
 SMEM = pl.BlockSpec(memory_space=pltpu.SMEM)
-
-
-def turns(count):
-    return sorted(range(1, count), key=lambda t: (t < count // 2, t))
 
 
 def swapped(array, axis, step):
@@ -150,34 +195,42 @@
         out[slot % half] = merged(level, begin, size, kept_ref, got_ref, w_ref, box // 2, box)
 
 
-def last_kernel(
-    level, begin, size, slots_ref, kept_ref, got_ref, joint_ref, after_ref, *outs
-):
-    half = kept_ref.shape[0]
+def last_kernel(level, pairs, apart, parts, slots_ref, joint_ref, after_ref, *refs):
+    states, outs = refs[: 2 * len(parts)], refs[2 * len(parts) :]
+    half = states[0].shape[0]
     me = lax.axis_index("inner")
     width = joint_ref.shape[2]
     piece = outs[0].shape[2]
-    pieces = joint_ref.shape[0] * width // piece
     per_box = joint_ref.shape[0] // (2 * half)
-    for t in range(pieces // 2):
+    for at, t in enumerate(pairs):
         for odd in range(2):
-            out = outs[t].at[odd]
+            out = outs[odd].at[at] if apart else outs[at].at[odd]
             first = jnp.bitwise_xor(me, 2 * t + odd) * (piece // width)
             for n in range(piece // width):
                 k = jnp.max(slots_ref[(first + n) // per_box])
-                out[:, n * width : (n + 1) * width] = merged(
-                    level, begin, size, kept_ref, got_ref, joint_ref, k, first + n
-                )
-
-
-def pack_kernel(*refs):
+                row = 0
+                for i, (begin, size) in enumerate(parts):
+                    kept_ref, got_ref = states[2 * i : 2 * i + 2]
+                    out[row : row + size, n * width : (n + 1) * width] = merged(
+                        level, begin, size, kept_ref, got_ref, joint_ref, k, first + n
+                    )
+                    row += size
+
+
+def couple_kernel(mine_ref, got_ref, after_ref, *outs):
+    for t, out in enumerate(outs):
+        out[0] = mine_ref[t]
+        out[1] = got_ref[t]
+
+
+def pack_kernel(turns, *refs):
     out = refs[-1]
-    for t in range(out.shape[0]):
-        out[t] = refs[t][1]
-
-
-def space_kernel(after_ref, out):
-    out[...] = jnp.zeros_like(out)
+    for at, t in enumerate(turns):
+        out[t] = refs[at][1]
+
+
+def space_kernel(*refs):
+    refs[-1][...] = jnp.zeros_like(refs[-1])
 
 
 def place_kernel(cuts, counts, early, *refs):
@@ -210,7 +263,7 @@
 
 
 def finish_kernel(cut, first_ref, held_ref, *refs):
-    even_refs, (odd_ref, out, held, sems) = refs[:-4], refs[-4:]
+    blocks, (out, held, sems) = refs[:-3], refs[-3:]
     begin, size = cut
     rows = held.shape[1]
     late = held.shape[0]
@@ -218,7 +271,9 @@
     me = lax.axis_index("inner")
     copies = []
     for step in range(late):
-        block = odd_ref[step // 2] if step % 2 else even_refs[step // 2][0]
+        block = blocks[step // 2][step % 2]
+        if step % 2 and len(blocks) > late // 2:
+            block = blocks[-1][step // 2]
         held[step] = held_ref[step]
         held[step, :, begin : begin + size] = block.T
         owner = jnp.bitwise_xor(me, first + step)
@@ -240,14 +295,17 @@
     edges = [columns * sum(PARTS[:n]) // sum(PARTS) for n in range(len(PARTS) + 1)]
     cuts = [(a, b - a) for a, b in zip(edges, edges[1:])]
     count = len(cuts)
+    groups = [["abcdefgh".index(x) for x in names] for names in GROUPS]
+    spans = [(cuts[m[0]][0], sum(cuts[x][1] for x in m)) for m in groups]
     held = [None] * count
-    done = [None] * count
-    swaps = [[] for _ in cuts]
+    done = [[None] * (inner // 2) for _ in groups]
+    swaps = [[] for _ in groups]
     early = inner // 4
     level_w = inside = joint = after = None
 
     for step in ORDER:
         kind, n = step[0], "abcdefgh".find(step[-1])
+        g = [names[0] for names in GROUPS].index(step[-1]) if kind in "oqutepy" else 0
         if kind == "f":
             firsts = [cuts[0], (cuts[1][0], columns - cuts[1][0])]
             sent_a, kept_a, sent_b, kept_b = call(
@@ -313,43 +371,75 @@
             after = kept
             axis, bit = level_axis(level + 1)
             held[n] = (kept, swapped(sent, axis, 1 << bit), 0)
-        elif kind == "o":
-            size = cuts[n][1]
-            kept, got, begin = held[n]
+        elif kind in "oe":
+            apart = kind == "e"
+            near = step[1] == "n"
+            pairs = range(early if apart else 0, early if near else inner // 2)
+            members = groups[g]
+            size = spans[g][1]
+            states = [x for m in members for x in held[m][:2]]
             outs = call(
-                functools.partial(last_kernel, levels - 1, begin, size),
-                [arr(2, size, piece)] * (inner // 2),
-                [slots, kept, got, joint, after],
-                [VMEM, VMEM, VMEM, VMEM, ANY],
-                name=f"last{step[-1]}",
+                functools.partial(
+                    last_kernel,
+                    levels - 1,
+                    pairs,
+                    apart,
+                    [(held[m][2], cuts[m][1]) for m in members],
+                ),
+                [arr(len(pairs), size, piece)] * 2 if apart else [arr(2, size, piece)] * len(pairs),
+                [slots, joint, after, *states],
+                [VMEM, VMEM, ANY] + [VMEM] * len(states),
+                name=("far" if apart else "last") + step[-1],
             )
             after = outs[0]
-            sent = [outs[0]] + [None] * (inner // 2 - 1)
-            for t in turns(inner // 2):
-                sent[t] = swapped(outs[t], "inner", 2 * t)
-            done[n] = sent
+            if apart:
+                coupled = [outs[0], swapped(outs[1], "inner", 1)]
+            else:
+                for t, x in zip(pairs, outs):
+                    done[g][t] = swapped(x, "inner", 2 * t) if t else x
+        elif kind == "p":
+            outs = call(
+                couple_kernel,
+                [arr(2, spans[g][1], piece)] * (inner // 2 - early),
+                coupled + [after],
+                [VMEM, VMEM, ANY],
+                name=f"couple{step[-1]}",
+            )
+            after = outs[0]
+            for t, x in enumerate(outs, early):
+                done[g][t] = swapped(x, "inner", 2 * t)
+        elif kind == "y":
+            after = call(
+                space_kernel, [arr(16, 128)], [after, *done[g]], [ANY] * (1 + len(done[g])), name=f"hold{step[-1]}"
+            )[0]
         elif kind == "x":
-            after = call(space_kernel, [arr(16, 128)], [after], [ANY], name="space")[0]
+            first = [x for part in (swaps[:-2] if XS else []) for x in part]
+            after = call(
+                space_kernel, [arr(16, 128)], [after, *first], [ANY] * (1 + len(first)), name="space"
+            )[0]
         elif kind in "qut":
             pairs = inner // 2
             begin = early if kind == "t" else 0
             end = early if kind == "u" else pairs
             if begin < end:
-                group = done[n][begin:end]
+                turns = list(range(end - begin))
+                if TURN:
+                    turns = turns[early:] + turns[:early]
+                group = [done[g][begin + t] for t in turns]
                 after = call(
-                    pack_kernel,
-                    [arr(len(group), cuts[n][1], piece)],
+                    functools.partial(pack_kernel, turns),
+                    [arr(len(group), spans[g][1], piece)],
                     group + [after],
                     [VMEM] * len(group) + [ANY],
                     name=f"pack{step[-1]}",
                 )[0]
-                swaps[n].append(swapped(after, "inner", 1))
+                swaps[g].append(swapped(after, "inner", 1))
         elif kind == "z":
             counts = [len(a) + len(b) for a, b in zip(done[:-1], swaps)] + [early + 1]
-            flat = [x for n in range(count - 1) for x in done[n] + swaps[n]]
-            flat += done[-1][:early] + swaps[-1]
+            flat = [x for d, w in zip(done[:-1], swaps) for x in d + w]
+            flat += done[-1][:early] + swaps[-1][:1]
             placed, rest = call(
-                functools.partial(place_kernel, cuts, counts, early),
+                functools.partial(place_kernel, spans, counts, early),
                 [arr(*vectors.shape), arr(inner - 2 * early, piece, columns)],
                 flat + [after],
                 [VMEM] * len(flat) + [ANY],
@@ -361,9 +451,9 @@
                 out_specs=[HBM, VMEM],
             )
             after = rest
-    flat = done[-1][early:] + swaps[-1][-1:]
+    flat = done[-1][early:] + swaps[-1][1:]
     return call(
-        functools.partial(finish_kernel, cuts[-1]),
+        functools.partial(finish_kernel, spans[-1]),
         [arr(*vectors.shape)],
         [placed, rest, *flat],
         [HBM, VMEM] + [VMEM] * len(flat),

time: 54.4 us -> 51.5 us (0.947)
  waiting for transfers between devices: 12.6 us -> 7.16 us
  local copies, waits for them, and re-layouts: 0.02 us -> 1.3 us
  starting transfers between devices: 27.4 us -> 28.4 us
    ppermute x24, waiting for transfers between devices: 12.6 us -> 7.16 us  [swapped(): lax.ppermute(array, axis, [(i, i ^ step) for i in range(lax.axis_size(axi...]
    unnamed x10, local copies, waits for them, and re-layouts: 0.02 us -> 1.3 us
    ppermute x24, starting transfers between devices: 27.4 us -> 28.4 us  [swapped(): lax.ppermute(array, axis, [(i, i ^ step) for i in range(lax.axis_size(axi...]
    pallas_call x23 -> x25, Pallas kernels: 14 us -> 14.3 us  [call(): return list(run(*ins))]
  transfers between devices with their start and end apart: 24 -> 24, of which waited for: 10 -> 6; matrix products, arithmetic and copies ran while one was open for 0% -> 0% of each run, Pallas kernels for 20% -> 22%
where the time goes in v5:
time: 51.5 us; the launch traced here: 51.4 us
  starting transfers between devices  28.4 us (55%)
  Pallas kernels  14.3 us (28%)
  waiting for transfers between devices  7.16 us (14%)
  local copies, waits for them, and re-layouts  1.3 us (3%)
    ppermute x24, starting transfers between devices, swapped(): lax.ppermute(array, axis, [(i, i ^ step) for i in range(lax.axis_size(axi...  28.4 us
    pallas_call x25, Pallas kernels, call(): return list(run(*ins))  14.3 us
    ppermute x24, waiting for transfers between devices, swapped(): lax.ppermute(array, axis, [(i, i ^ step) for i in range(lax.axis_size(axi...  7.16 us
    unnamed x10, local copies, waits for them, and re-layouts  1.3 us
  transfers between devices with their start and end apart: 24, of which 6 were waited for; matrix products, arithmetic and copies ran while one was open for 0% of the time, Pallas kernels for 22%

profile of v5, /device:TPU:0, one launch (start us, length us, event | category | flops | bytes accessed | tf_op | source)
XLA Modules:
  0.0 51.4 jit_solution(12298707346237439796)
XLA Ops:
  0.0 1.9 %leaves.1 = (bf16[4,64,256]{2,1,0:T(8,128)(2,1)S(1)}, bf16[4,64,256]{2,1,0:T(8,128)(2,1)S(1)}, bf16[4,192,256]{2,1,0:T(8,128)(2,1)S(1)}, bf16[4,192,256]{2,1,0:T(8,128)(2,1)S(1)}) custom-call(bf16[2048,256]{1,0:T(8,128)(2,1)} %x_hbm.1, bf16[2048,256]{1,0:T(8,128)(2,1)} %v_hbm.1), custom_call_target="tpu_custom_call" | custom-call | flops 2000000000 | tf_op jit(solution)/shard_map/leaves/pallas_call | solution.py:106
  1.9 0.5 %collective-permute-start.1 = (bf16[4,64,256]{2,1,0:T(8,128)(2,1)S(1)}, bf16[4,64,256]{2,1,0:T(8,128)(2,1)S(1)}, u32[]{:S(2)}, u32[]{:S(2)}) collective-permute-start(bf16[4,64,256]{2,1,0:T(8,128)(2,1)S(1)} %get-tuple-element.48), channel_id=1, source_target_pairs={{0,1},{1,0},{2,3},{3,2},{4,5},{5,4},{6,7},{7,6},{8,9},{9,8},{10,11... | collective-permute-start | bytes 393224 | tf_op jit(solution)/shard_map/ppermute | solution.py:72
  2.5 0.1 collective-permute-start
  2.5 1.6 %weights.1.w_ref.after_ref = bf16[8,512,256]{2,1,0:T(8,128)(2,1)S(1)} custom-call(bf16[4,1,1,8,512,256]{5,4,3,2,1,0:T(8,128)(2,1)} %w_ref.13, bf16[4,192,256]{2,1,0:T(8,128)(2,1)S(1)} %get-tuple-element.45.after_ref.kept_ref), custom_call_target="tpu_custom_call" | custom-call | flops 1000000000 | tf_op jit(solution)/shard_map/weights/pallas_call | solution.py:106
  4.1 0.5 merge0a.1
  4.6 3.1 %collective-permute-start.2 = (bf16[4,64,256]{2,1,0:T(8,128)(2,1)S(1)}, bf16[4,64,256]{2,1,0:T(8,128)(2,1)S(1)}, u32[]{:S(2)}, u32[]{:S(2)}) collective-permute-start(bf16[4,64,256]{2,1,0:T(8,128)(2,1)S(1)} %get-tuple-element.52), channel_id=1, source_target_pairs={{0,2},{1,3},{2,0},{3,1},{4,6},{5,7},{6,4},{7,5},{8,10},{9,11},{10,... | collective-permute-start | bytes 393224 | tf_op jit(solution)/shard_map/ppermute | solution.py:72
  7.7 0.5 merge0c.1
  8.2 0.5 merge0b.1
  8.7 0.1 collective-permute-start.4
  8.8 0.8 %copy-done = bf16[1,1,8,256,256]{4,3,2,1,0:T(8,128)(2,1)S(1)} copy-done((bf16[1,1,8,256,256]{4,3,2,1,0:T(8,128)(2,1)S(1)}, bf16[1,1,8,256,256]{4,3,2,1,0:T(8,128)(2,1)}, u32[]{:S(2)}) %copy-start) | copy-done | bytes 1048600
  9.6 0.3 copy-done.1
  9.9 0.5 inside.1.after_ref.inside_ref
  10.4 1.2 %collective-permute-done.2.got_ref = bf16[4,64,256]{2,1,0:T(8,128)(2,1)S(1)} collective-permute-done((bf16[4,64,256]{2,1,0:T(8,128)(2,1)S(1)}, bf16[4,64,256]{2,1,0:T(8,128)(2,1)S(1)}, u32[]{:S(2)}, u32[]{:S(2)}) %collective-permute-start.2) | collective-permute-done | bytes 131104 | tf_op jit(solution)/shard_map/ppermute | solution.py:72
  11.6 0.1 slice-done.1
  11.8 0.5 merge1a.1
  12.3 1.8 %collective-permute-start.3 = (bf16[4,64,256]{2,1,0:T(8,128)(2,1)S(1)}, bf16[4,64,256]{2,1,0:T(8,128)(2,1)S(1)}, u32[]{:S(2)}, u32[]{:S(2)}) collective-permute-start(bf16[4,64,256]{2,1,0:T(8,128)(2,1)S(1)} %get-tuple-element.54), channel_id=1, source_target_pairs={{0,8},{8,0},{16,24},{24,16},{1,9},{9,1},{17,25},{25,17},{2,10},{10... | collective-permute-start | bytes 393224 | tf_op jit(solution)/shard_map/ppermute | solution.py:72
  14.0 2.1 %collective-permute-start.6 = (bf16[4,96,256]{2,1,0:T(8,128)(2,1)S(1)}, bf16[4,96,256]{2,1,0:T(8,128)(2,1)S(1)}, u32[]{:S(2)}, u32[]{:S(2)}) collective-permute-start(bf16[4,96,256]{2,1,0:T(8,128)(2,1)S(1)} %get-tuple-element.61), channel_id=1, source_target_pairs={{0,2},{1,3},{2,0},{3,1},{4,6},{5,7},{6,4},{7,5},{8,10},{9,11},{10,... | collective-permute-start | bytes 589832 | tf_op jit(solution)/shard_map/ppermute | solution.py:72
  16.1 0.5 merge1b.1
  16.6 2.0 %collective-permute-start.5 = (bf16[4,96,256]{2,1,0:T(8,128)(2,1)S(1)}, bf16[4,96,256]{2,1,0:T(8,128)(2,1)S(1)}, u32[]{:S(2)}, u32[]{:S(2)}) collective-permute-start(bf16[4,96,256]{2,1,0:T(8,128)(2,1)S(1)} %get-tuple-element.60), channel_id=1, source_target_pairs={{0,8},{8,0},{16,24},{24,16},{1,9},{9,1},{17,25},{25,17},{2,10},{10... | collective-permute-start | bytes 589832 | tf_op jit(solution)/shard_map/ppermute | solution.py:72
  18.6 0.5 merge2a.1
  19.1 1.6 %collective-permute-start.7 = (bf16[4,64,256]{2,1,0:T(8,128)(2,1)S(1)}, bf16[4,64,256]{2,1,0:T(8,128)(2,1)S(1)}, u32[]{:S(2)}, u32[]{:S(2)}) collective-permute-start(bf16[4,64,256]{2,1,0:T(8,128)(2,1)S(1)} %get-tuple-element.64), channel_id=1, source_target_pairs={{0,16},{8,24},{16,0},{24,8},{1,17},{9,25},{17,1},{25,9},{2,18},{10... | collective-permute-start | bytes 393224 | tf_op jit(solution)/shard_map/ppermute | solution.py:72
  20.7 1.3 %join.1 = (bf16[8,512,256]{2,1,0:T(8,128)(2,1)S(1)}, s32[8,8,128]{2,1,0:T(8,128)S(1)}) custom-call(s32[1,1,8]{2,1,0:T(1,128)S(1)} %copy-done.2, bf16[4,1,1,8,512,256]{5,4,3,2,1,0:T(8,128)(2,1)S(1)} %bitcast.1, bf16[8,256,256]{2,1,0:T(8,128)(2,1)S(1)} %inside.1.after_ref.inside_ref, bf16[4,64,256]{2,1,0:T(8,128)(2,1)S(1)} %get-tuple-element.57.after_ref.refs_0_), custom_call_target="tpu_custom_call" | custom-call | flops 300000000 | tf_op jit(solution)/shard_map/join/pallas_call | solution.py:106
  22.0 0.5 merge1c.1
  22.5 0.5 collective-permute-start.11
  23.0 0.5 merge2b.1
  23.4 1.4 %collective-permute-start.12 = (bf16[4,96,256]{2,1,0:T(8,128)(2,1)S(1)}, bf16[4,96,256]{2,1,0:T(8,128)(2,1)S(1)}, u32[]{:S(2)}, u32[]{:S(2)}) collective-permute-start(bf16[4,96,256]{2,1,0:T(8,128)(2,1)S(1)} %get-tuple-element.71), channel_id=1, source_target_pairs={{0,16},{8,24},{16,0},{24,8},{1,17},{9,25},{17,1},{25,9},{2,18},{10... | collective-permute-start | bytes 589832 | tf_op jit(solution)/shard_map/ppermute | solution.py:72
  24.9 0.7 %lasta.1 = (bf16[2,64,256]{2,1,0:T(8,128)(2,1)S(1)}, bf16[2,64,256]{2,1,0:T(8,128)(2,1)S(1)}, bf16[2,64,256]{2,1,0:T(8,128)(2,1)S(1)}, bf16[2,64,256]{2,1,0:T(8,128)(2,1)S(1)}) custom-call(s32[8,8,128]{2,1,0:T(8,128)S(1)} %get-tuple-element.58.slots_ref, bf16[8,512,256]{2,1,0:T(8,128)(2,1)S(1)} %get-tuple-element.59.after_ref.joint_ref, ...), custom_call_target="tpu_custom_call" | custom-call | flops 1000000000 | tf_op jit(solution)/shard_map/lasta/pallas_call | solution.py:106
  25.5 1.8 %collective-permute-start.8 = (bf16[2,64,256]{2,1,0:T(8,128)(2,1)S(1)}, bf16[2,64,256]{2,1,0:T(8,128)(2,1)S(1)}, u32[]{:S(2)}, u32[]{:S(2)}) collective-permute-start(bf16[2,64,256]{2,1,0:T(8,128)(2,1)S(1)} %get-tuple-element.66), channel_id=1, source_target_pairs={{0,2},{1,3},{2,0},{3,1},{4,6},{5,7},{6,4},{7,5},{8,10},{9,11},{10,... | collective-permute-start | bytes 196616 | tf_op jit(solution)/shard_map/ppermute | solution.py:72
  27.4 2.6 %collective-permute-start.9 = (bf16[2,64,256]{2,1,0:T(8,128)(2,1)S(1)}, bf16[2,64,256]{2,1,0:T(8,128)(2,1)S(1)}, u32[]{:S(2)}, u32[]{:S(2)}) collective-permute-start(bf16[2,64,256]{2,1,0:T(8,128)(2,1)S(1)} %get-tuple-element.67), channel_id=1, source_target_pairs={{0,4},{1,5},{2,6},{3,7},{4,0},{5,1},{6,2},{7,3},{8,12},{9,13},{10,... | collective-permute-start | bytes 196616 | tf_op jit(solution)/shard_map/ppermute | solution.py:72
  30.0 0.5 merge2c.1
  30.5 1.4 %collective-permute-start.13 = (bf16[4,96,256]{2,1,0:T(8,128)(2,1)S(1)}, bf16[4,96,256]{2,1,0:T(8,128)(2,1)S(1)}, u32[]{:S(2)}, u32[]{:S(2)}) collective-permute-start(bf16[4,96,256]{2,1,0:T(8,128)(2,1)S(1)} %get-tuple-element.73), channel_id=1, source_target_pairs={{0,16},{8,24},{16,0},{24,8},{1,17},{9,25},{17,1},{25,9},{2,18},{10... | collective-permute-start | bytes 589832 | tf_op jit(solution)/shard_map/ppermute | solution.py:72
  31.9 0.7 %lastb.1 = (bf16[2,96,256]{2,1,0:T(8,128)(2,1)S(1)}, bf16[2,96,256]{2,1,0:T(8,128)(2,1)S(1)}, bf16[2,96,256]{2,1,0:T(8,128)(2,1)S(1)}, bf16[2,96,256]{2,1,0:T(8,128)(2,1)S(1)}) custom-call(s32[8,8,128]{2,1,0:T(8,128)S(1)} %get-tuple-element.58.slots_ref, bf16[8,512,256]{2,1,0:T(8,128)(2,1)S(1)} %get-tuple-element.59.after_ref.joint_ref, ...), custom_call_target="tpu_custom_call" | custom-call | flops 100000000 | tf_op jit(solution)/shard_map/lastb/pallas_call | solution.py:106
  32.5 1.0 %collective-permute-start.16 = (bf16[2,96,256]{2,1,0:T(8,128)(2,1)S(1)}, bf16[2,96,256]{2,1,0:T(8,128)(2,1)S(1)}, u32[]{:S(2)}, u32[]{:S(2)}) collective-permute-start(bf16[2,96,256]{2,1,0:T(8,128)(2,1)S(1)} %get-tuple-element.78), channel_id=1, source_target_pairs={{0,2},{1,3},{2,0},{3,1},{4,6},{5,7},{6,4},{7,5},{8,10},{9,11},{10,... | collective-permute-start | bytes 294920 | tf_op jit(solution)/shard_map/ppermute | solution.py:72
  33.5 3.5 %collective-permute-start.17 = (bf16[2,96,256]{2,1,0:T(8,128)(2,1)S(1)}, bf16[2,96,256]{2,1,0:T(8,128)(2,1)S(1)}, u32[]{:S(2)}, u32[]{:S(2)}) collective-permute-start(bf16[2,96,256]{2,1,0:T(8,128)(2,1)S(1)} %get-tuple-element.79), channel_id=1, source_target_pairs={{0,4},{1,5},{2,6},{3,7},{4,0},{5,1},{6,2},{7,3},{8,12},{9,13},{10,... | collective-permute-start | bytes 294920 | tf_op jit(solution)/shard_map/ppermute | solution.py:72
  37.0 0.5 farc.1
  37.5 0.1 collective-permute-start.14
  37.6 0.5 lastc.1
  38.1 1.5 %collective-permute-start.20 = (bf16[2,96,256]{2,1,0:T(8,128)(2,1)S(1)}, bf16[2,96,256]{2,1,0:T(8,128)(2,1)S(1)}, u32[]{:S(2)}, u32[]{:S(2)}) collective-permute-start(bf16[2,96,256]{2,1,0:T(8,128)(2,1)S(1)} %get-tuple-element.81), channel_id=1, source_target_pairs={{0,2},{1,3},{2,0},{3,1},{4,6},{5,7},{6,4},{7,5},{8,10},{9,11},{10,... | collective-permute-start | bytes 294920 | tf_op jit(solution)/shard_map/ppermute | solution.py:72
  39.6 3.0 %collective-permute-start.22 = (bf16[2,96,256]{2,1,0:T(8,128)(2,1)S(1)}, bf16[2,96,256]{2,1,0:T(8,128)(2,1)S(1)}, u32[]{:S(2)}, u32[]{:S(2)}) collective-permute-start(bf16[2,96,256]{2,1,0:T(8,128)(2,1)S(1)} %get-tuple-element.77.refs_4_), channel_id=1, source_target_pairs={{0,4},{1,5},{2,6},{3,7},{4,0},{5,1},{6,2},{7,3},{8,12},{9,13},{10,... | collective-permute-start | bytes 294920 | tf_op jit(solution)/shard_map/ppermute | solution.py:72
  42.6 0.3 collective-permute-start.23
  42.9 0.7 %collective-permute-done.18.refs_1_.refs_8_ = bf16[2,96,256]{2,1,0:T(8,128)(2,1)S(1)} collective-permute-done((bf16[2,96,256]{2,1,0:T(8,128)(2,1)S(1)}, bf16[2,96,256]{2,1,0:T(8,128)(2,1)S(1)}, u32[]{:S(2)}, u32[]{:S(2)}) %collective-permute-start.18) | collective-permute-done | bytes 98336 | tf_op jit(solution)/shard_map/ppermute | solution.py:72
  43.6 0.1 collective-permute-start.19
  43.6 2.6 %collective-permute-done.20.refs_1_.refs_11_ = bf16[2,96,256]{2,1,0:T(8,128)(2,1)S(1)} collective-permute-done((bf16[2,96,256]{2,1,0:T(8,128)(2,1)S(1)}, bf16[2,96,256]{2,1,0:T(8,128)(2,1)S(1)}, u32[]{:S(2)}, u32[]{:S(2)}) %collective-permute-start.20) | collective-permute-done | bytes 98336 | tf_op jit(solution)/shard_map/ppermute | solution.py:72
  46.3 1.3 %collective-permute-done.21.refs_12_ = bf16[2,96,256]{2,1,0:T(8,128)(2,1)S(1)} collective-permute-done((bf16[2,96,256]{2,1,0:T(8,128)(2,1)S(1)}, bf16[2,96,256]{2,1,0:T(8,128)(2,1)S(1)}, u32[]{:S(2)}, u32[]{:S(2)}) %collective-permute-start.21) | collective-permute-done | bytes 98336 | tf_op jit(solution)/shard_map/ppermute | solution.py:72
  47.6 1.4 %place.1 = (bf16[2048,256]{1,0:T(8,128)(2,1)}, bf16[4,256,256]{2,1,0:T(8,128)(2,1)S(1)}) custom-call(bf16[2,64,256]{2,1,0:T(8,128)(2,1)S(1)} %get-tuple-element.65.after_ref.refs_1_.refs_2_.refs_0_, bf16[2,64,256]{2,1,0:T(8,128)(2,1)S(1)} %collective-permute-done.8.refs_2_.refs_3_.refs_1_, ...), custom_call_target="tpu_custom_call" | custom-call | flops 10000000000 | tf_op jit(solution)/shard_map/place/pallas_call | solution.py:106
  49.0 0.8 %collective-permute-done.23.refs_1_ = bf16[2,96,256]{2,1,0:T(8,128)(2,1)S(1)} collective-permute-done((bf16[2,96,256]{2,1,0:T(8,128)(2,1)S(1)}, bf16[2,96,256]{2,1,0:T(8,128)(2,1)S(1)}, u32[]{:S(2)}, u32[]{:S(2)}) %collective-permute-start.23) | collective-permute-done | bytes 98336 | tf_op jit(solution)/shard_map/ppermute | solution.py:72
  49.8 0.5 %collective-permute-done.22.refs_0_ = bf16[2,96,256]{2,1,0:T(8,128)(2,1)S(1)} collective-permute-done((bf16[2,96,256]{2,1,0:T(8,128)(2,1)S(1)}, bf16[2,96,256]{2,1,0:T(8,128)(2,1)S(1)}, u32[]{:S(2)}, u32[]{:S(2)}) %collective-permute-start.22) | collective-permute-done | bytes 98336 | tf_op jit(solution)/shard_map/ppermute | solution.py:72
  50.4 1.0 %finish.1 = bf16[2048,256]{1,0:T(8,128)(2,1)} custom-call(bf16[2048,256]{1,0:T(8,128)(2,1)} %get-tuple-element.82.first_ref, bf16[4,256,256]{2,1,0:T(8,128)(2,1)S(1)} %get-tuple-element.83.held_ref, bf16[2,96,256]{2,1,0:T(8,128)(2,1)S(1)} %collective-permute-done.22.refs_0_, ...), custom_call_target="tpu_custom_call", output_to_operand_aliasing={{}: (0, {})} | custom-call | flops 2000000000 | tf_op jit(solution)/shard_map/finish/pallas_call | solution.py:106
  (36 shorter events, 0.2 us)
Async XLA Ops:
  1.9 2.2 %collective-permute-start.1 = (bf16[4,64,256]{2,1,0:T(8,128)(2,1)S(1)}, bf16[4,64,256]{2,1,0:T(8,128)(2,1)S(1)}, u32[]{:S(2)}, u32[]{:S(2)}) collective-permute-start(bf16[4,64,256]{2,1,0:T(8,128)(2,1)S(1)} %get-tuple-element.48), channel_id=1, source_target_pairs={{0,1},{1,0},{2,3},{3,2},{4,5},{5,4},{6,7},{7,6},{8,9},{9,8},{10,11... | collective-permute-start | bytes 393224 | tf_op jit(solution)/shard_map/ppermute | solution.py:72
  2.5 5.2 %collective-permute-start = (bf16[4,192,256]{2,1,0:T(8,128)(2,1)S(1)}, bf16[4,192,256]{2,1,0:T(8,128)(2,1)S(1)}, u32[]{:S(2)}, u32[]{:S(2)}) collective-permute-start(bf16[4,192,256]{2,1,0:T(8,128)(2,1)S(1)} %get-tuple-element.46), channel_id=1, source_target_pairs={{0,1},{1,0},{2,3},{3,2},{4,5},{5,4},{6,7},{7,6},{8,9},{9,8},{10,11... | collective-permute-start | bytes 1179656 | tf_op jit(solution)/shard_map/ppermute | solution.py:72
  4.6 7.0 %collective-permute-start.2 = (bf16[4,64,256]{2,1,0:T(8,128)(2,1)S(1)}, bf16[4,64,256]{2,1,0:T(8,128)(2,1)S(1)}, u32[]{:S(2)}, u32[]{:S(2)}) collective-permute-start(bf16[4,64,256]{2,1,0:T(8,128)(2,1)S(1)} %get-tuple-element.52), channel_id=1, source_target_pairs={{0,2},{1,3},{2,0},{3,1},{4,6},{5,7},{6,4},{7,5},{8,10},{9,11},{10,... | collective-permute-start | bytes 393224 | tf_op jit(solution)/shard_map/ppermute | solution.py:72
  7.7 4.0 %slice-start = ((s8[8388608]{0:T(1024)(128)(4,1)}), s8[4194304]{0:T(1024)(128)(4,1)S(1)}, s32[]{:S(2)}) async-start(s8[8388608]{0:T(1024)(128)(4,1)} %bitcast), calls=%async_computation | async-start | bytes 8388608
  8.2 1.5 %copy-start = (bf16[1,1,8,256,256]{4,3,2,1,0:T(8,128)(2,1)S(1)}, bf16[1,1,8,256,256]{4,3,2,1,0:T(8,128)(2,1)}, u32[]{:S(2)}) copy-start(bf16[1,1,8,256,256]{4,3,2,1,0:T(8,128)(2,1)} %core_ref.1) | copy-start | bytes 3145732
  8.2 1.8 %copy-start.1 = (bf16[2048,256]{1,0:T(8,128)(2,1)S(1)}, bf16[2048,256]{1,0:T(8,128)(2,1)}, u32[]{:S(2)}) copy-start(bf16[2048,256]{1,0:T(8,128)(2,1)} %u_ref.1) | copy-start | bytes 3145732
  8.2 3.6 %slice-start.1 = ((s8[8388608]{0:T(1024)(128)(4,1)}), s8[4194304]{0:T(1024)(128)(4,1)S(1)}, s32[]{:S(2)}) async-start(s8[8388608]{0:T(1024)(128)(4,1)} %bitcast), calls=%async_computation.1 | async-start | bytes 8388608
  8.7 7.4 %collective-permute-start.4 = (bf16[4,96,256]{2,1,0:T(8,128)(2,1)S(1)}, bf16[4,96,256]{2,1,0:T(8,128)(2,1)S(1)}, u32[]{:S(2)}, u32[]{:S(2)}) collective-permute-start(bf16[4,96,256]{2,1,0:T(8,128)(2,1)S(1)} %get-tuple-element.55), channel_id=1, source_target_pairs={{0,2},{1,3},{2,0},{3,1},{4,6},{5,7},{6,4},{7,5},{8,10},{9,11},{10,... | collective-permute-start | bytes 589832 | tf_op jit(solution)/shard_map/ppermute | solution.py:72
  12.3 6.3 %collective-permute-start.3 = (bf16[4,64,256]{2,1,0:T(8,128)(2,1)S(1)}, bf16[4,64,256]{2,1,0:T(8,128)(2,1)S(1)}, u32[]{:S(2)}, u32[]{:S(2)}) collective-permute-start(bf16[4,64,256]{2,1,0:T(8,128)(2,1)S(1)} %get-tuple-element.54), channel_id=1, source_target_pairs={{0,8},{8,0},{16,24},{24,16},{1,9},{9,1},{17,25},{25,17},{2,10},{10... | collective-permute-start | bytes 393224 | tf_op jit(solution)/shard_map/ppermute | solution.py:72
  14.0 7.9 %collective-permute-start.6 = (bf16[4,96,256]{2,1,0:T(8,128)(2,1)S(1)}, bf16[4,96,256]{2,1,0:T(8,128)(2,1)S(1)}, u32[]{:S(2)}, u32[]{:S(2)}) collective-permute-start(bf16[4,96,256]{2,1,0:T(8,128)(2,1)S(1)} %get-tuple-element.61), channel_id=1, source_target_pairs={{0,2},{1,3},{2,0},{3,1},{4,6},{5,7},{6,4},{7,5},{8,10},{9,11},{10,... | collective-permute-start | bytes 589832 | tf_op jit(solution)/shard_map/ppermute | solution.py:72
  16.6 6.4 %collective-permute-start.5 = (bf16[4,96,256]{2,1,0:T(8,128)(2,1)S(1)}, bf16[4,96,256]{2,1,0:T(8,128)(2,1)S(1)}, u32[]{:S(2)}, u32[]{:S(2)}) collective-permute-start(bf16[4,96,256]{2,1,0:T(8,128)(2,1)S(1)} %get-tuple-element.60), channel_id=1, source_target_pairs={{0,8},{8,0},{16,24},{24,16},{1,9},{9,1},{17,25},{25,17},{2,10},{10... | collective-permute-start | bytes 589832 | tf_op jit(solution)/shard_map/ppermute | solution.py:72
  18.6 2.1 %copy-start.2 = (s32[1,1,8]{2,1,0:T(1,128)S(1)}, s32[1,1,8]{2,1,0:T(1,128)}, u32[]{:S(2)}) copy-start(s32[1,1,8]{2,1,0:T(1,128)} %order_ref.1) | copy-start | bytes 100
  19.1 5.8 %collective-permute-start.7 = (bf16[4,64,256]{2,1,0:T(8,128)(2,1)S(1)}, bf16[4,64,256]{2,1,0:T(8,128)(2,1)S(1)}, u32[]{:S(2)}, u32[]{:S(2)}) collective-permute-start(bf16[4,64,256]{2,1,0:T(8,128)(2,1)S(1)} %get-tuple-element.64), channel_id=1, source_target_pairs={{0,16},{8,24},{16,0},{24,8},{1,17},{9,25},{17,1},{25,9},{2,18},{10... | collective-permute-start | bytes 393224 | tf_op jit(solution)/shard_map/ppermute | solution.py:72
  22.5 7.5 %collective-permute-start.11 = (bf16[4,96,256]{2,1,0:T(8,128)(2,1)S(1)}, bf16[4,96,256]{2,1,0:T(8,128)(2,1)S(1)}, u32[]{:S(2)}, u32[]{:S(2)}) collective-permute-start(bf16[4,96,256]{2,1,0:T(8,128)(2,1)S(1)} %get-tuple-element.69), channel_id=1, source_target_pairs={{0,8},{8,0},{16,24},{24,16},{1,9},{9,1},{17,25},{25,17},{2,10},{10... | collective-permute-start | bytes 589832 | tf_op jit(solution)/shard_map/ppermute | solution.py:72
  23.4 8.4 %collective-permute-start.12 = (bf16[4,96,256]{2,1,0:T(8,128)(2,1)S(1)}, bf16[4,96,256]{2,1,0:T(8,128)(2,1)S(1)}, u32[]{:S(2)}, u32[]{:S(2)}) collective-permute-start(bf16[4,96,256]{2,1,0:T(8,128)(2,1)S(1)} %get-tuple-element.71), channel_id=1, source_target_pairs={{0,16},{8,24},{16,0},{24,8},{1,17},{9,25},{17,1},{25,9},{2,18},{10... | collective-permute-start | bytes 589832 | tf_op jit(solution)/shard_map/ppermute | solution.py:72
  25.5 8.0 %collective-permute-start.8 = (bf16[2,64,256]{2,1,0:T(8,128)(2,1)S(1)}, bf16[2,64,256]{2,1,0:T(8,128)(2,1)S(1)}, u32[]{:S(2)}, u32[]{:S(2)}) collective-permute-start(bf16[2,64,256]{2,1,0:T(8,128)(2,1)S(1)} %get-tuple-element.66), channel_id=1, source_target_pairs={{0,2},{1,3},{2,0},{3,1},{4,6},{5,7},{6,4},{7,5},{8,10},{9,11},{10,... | collective-permute-start | bytes 196616 | tf_op jit(solution)/shard_map/ppermute | solution.py:72
  27.4 9.6 %collective-permute-start.9 = (bf16[2,64,256]{2,1,0:T(8,128)(2,1)S(1)}, bf16[2,64,256]{2,1,0:T(8,128)(2,1)S(1)}, u32[]{:S(2)}, u32[]{:S(2)}) collective-permute-start(bf16[2,64,256]{2,1,0:T(8,128)(2,1)S(1)} %get-tuple-element.67), channel_id=1, source_target_pairs={{0,4},{1,5},{2,6},{3,7},{4,0},{5,1},{6,2},{7,3},{8,12},{9,13},{10,... | collective-permute-start | bytes 196616 | tf_op jit(solution)/shard_map/ppermute | solution.py:72
  30.0 7.0 %collective-permute-start.10 = (bf16[2,64,256]{2,1,0:T(8,128)(2,1)S(1)}, bf16[2,64,256]{2,1,0:T(8,128)(2,1)S(1)}, u32[]{:S(2)}, u32[]{:S(2)}) collective-permute-start(bf16[2,64,256]{2,1,0:T(8,128)(2,1)S(1)} %get-tuple-element.68), channel_id=1, source_target_pairs={{0,6},{1,7},{2,4},{3,5},{4,2},{5,3},{6,0},{7,1},{8,14},{9,15},{10,... | collective-permute-start | bytes 196616 | tf_op jit(solution)/shard_map/ppermute | solution.py:72
  30.5 6.5 %collective-permute-start.13 = (bf16[4,96,256]{2,1,0:T(8,128)(2,1)S(1)}, bf16[4,96,256]{2,1,0:T(8,128)(2,1)S(1)}, u32[]{:S(2)}, u32[]{:S(2)}) collective-permute-start(bf16[4,96,256]{2,1,0:T(8,128)(2,1)S(1)} %get-tuple-element.73), channel_id=1, source_target_pairs={{0,16},{8,24},{16,0},{24,8},{1,17},{9,25},{17,1},{25,9},{2,18},{10... | collective-permute-start | bytes 589832 | tf_op jit(solution)/shard_map/ppermute | solution.py:72
  32.5 10.1 %collective-permute-start.16 = (bf16[2,96,256]{2,1,0:T(8,128)(2,1)S(1)}, bf16[2,96,256]{2,1,0:T(8,128)(2,1)S(1)}, u32[]{:S(2)}, u32[]{:S(2)}) collective-permute-start(bf16[2,96,256]{2,1,0:T(8,128)(2,1)S(1)} %get-tuple-element.78), channel_id=1, source_target_pairs={{0,2},{1,3},{2,0},{3,1},{4,6},{5,7},{6,4},{7,5},{8,10},{9,11},{10,... | collective-permute-start | bytes 294920 | tf_op jit(solution)/shard_map/ppermute | solution.py:72
  33.5 9.4 %collective-permute-start.17 = (bf16[2,96,256]{2,1,0:T(8,128)(2,1)S(1)}, bf16[2,96,256]{2,1,0:T(8,128)(2,1)S(1)}, u32[]{:S(2)}, u32[]{:S(2)}) collective-permute-start(bf16[2,96,256]{2,1,0:T(8,128)(2,1)S(1)} %get-tuple-element.79), channel_id=1, source_target_pairs={{0,4},{1,5},{2,6},{3,7},{4,0},{5,1},{6,2},{7,3},{8,12},{9,13},{10,... | collective-permute-start | bytes 294920 | tf_op jit(solution)/shard_map/ppermute | solution.py:72
  37.0 6.6 %collective-permute-start.18 = (bf16[2,96,256]{2,1,0:T(8,128)(2,1)S(1)}, bf16[2,96,256]{2,1,0:T(8,128)(2,1)S(1)}, u32[]{:S(2)}, u32[]{:S(2)}) collective-permute-start(bf16[2,96,256]{2,1,0:T(8,128)(2,1)S(1)} %get-tuple-element.80), channel_id=1, source_target_pairs={{0,6},{1,7},{2,4},{3,5},{4,2},{5,3},{6,0},{7,1},{8,14},{9,15},{10,... | collective-permute-start | bytes 294920 | tf_op jit(solution)/shard_map/ppermute | solution.py:72
  37.5 2.0 %collective-permute-start.14 = (bf16[2,96,256]{2,1,0:T(8,128)(2,1)S(1)}, bf16[2,96,256]{2,1,0:T(8,128)(2,1)S(1)}, u32[]{:S(2)}, u32[]{:S(2)}) collective-permute-start(bf16[2,96,256]{2,1,0:T(8,128)(2,1)S(1)} %get-tuple-element.75), channel_id=1, source_target_pairs={{0,1},{1,0},{2,3},{3,2},{4,5},{5,4},{6,7},{7,6},{8,9},{9,8},{10,11... | collective-permute-start | bytes 294920 | tf_op jit(solution)/shard_map/ppermute | solution.py:72
  38.1 8.1 %collective-permute-start.20 = (bf16[2,96,256]{2,1,0:T(8,128)(2,1)S(1)}, bf16[2,96,256]{2,1,0:T(8,128)(2,1)S(1)}, u32[]{:S(2)}, u32[]{:S(2)}) collective-permute-start(bf16[2,96,256]{2,1,0:T(8,128)(2,1)S(1)} %get-tuple-element.81), channel_id=1, source_target_pairs={{0,2},{1,3},{2,0},{3,1},{4,6},{5,7},{6,4},{7,5},{8,10},{9,11},{10,... | collective-permute-start | bytes 294920 | tf_op jit(solution)/shard_map/ppermute | solution.py:72
  39.6 10.8 %collective-permute-start.22 = (bf16[2,96,256]{2,1,0:T(8,128)(2,1)S(1)}, bf16[2,96,256]{2,1,0:T(8,128)(2,1)S(1)}, u32[]{:S(2)}, u32[]{:S(2)}) collective-permute-start(bf16[2,96,256]{2,1,0:T(8,128)(2,1)S(1)} %get-tuple-element.77.refs_4_), channel_id=1, source_target_pairs={{0,4},{1,5},{2,6},{3,7},{4,0},{5,1},{6,2},{7,3},{8,12},{9,13},{10,... | collective-permute-start | bytes 294920 | tf_op jit(solution)/shard_map/ppermute | solution.py:72
  42.6 7.2 %collective-permute-start.23 = (bf16[2,96,256]{2,1,0:T(8,128)(2,1)S(1)}, bf16[2,96,256]{2,1,0:T(8,128)(2,1)S(1)}, u32[]{:S(2)}, u32[]{:S(2)}) collective-permute-start(bf16[2,96,256]{2,1,0:T(8,128)(2,1)S(1)} %get-tuple-element.84), channel_id=1, source_target_pairs={{0,6},{1,7},{2,4},{3,5},{4,2},{5,3},{6,0},{7,1},{8,14},{9,15},{10,... | collective-permute-start | bytes 294920 | tf_op jit(solution)/shard_map/ppermute | solution.py:72
  42.9 3.4 %collective-permute-start.15 = (bf16[4,64,256]{2,1,0:T(8,128)(2,1)S(1)}, bf16[4,64,256]{2,1,0:T(8,128)(2,1)S(1)}, u32[]{:S(2)}, u32[]{:S(2)}) collective-permute-start(bf16[4,64,256]{2,1,0:T(8,128)(2,1)S(1)} %packa.1.refs_4_), channel_id=1, source_target_pairs={{0,1},{1,0},{2,3},{3,2},{4,5},{5,4},{6,7},{7,6},{8,9},{9,8},{10,11... | collective-permute-start | bytes 393224 | tf_op jit(solution)/shard_map/ppermute | solution.py:72
  43.6 4.0 %collective-permute-start.19 = (bf16[4,96,256]{2,1,0:T(8,128)(2,1)S(1)}, bf16[4,96,256]{2,1,0:T(8,128)(2,1)S(1)}, u32[]{:S(2)}, u32[]{:S(2)}) collective-permute-start(bf16[4,96,256]{2,1,0:T(8,128)(2,1)S(1)} %packb.1.refs_2_), channel_id=1, source_target_pairs={{0,1},{1,0},{2,3},{3,2},{4,5},{5,4},{6,7},{7,6},{8,9},{9,8},{10,11... | collective-permute-start | bytes 589832 | tf_op jit(solution)/shard_map/ppermute | solution.py:72
  46.2 1.4 %collective-permute-start.21 = (bf16[2,96,256]{2,1,0:T(8,128)(2,1)S(1)}, bf16[2,96,256]{2,1,0:T(8,128)(2,1)S(1)}, u32[]{:S(2)}, u32[]{:S(2)}) collective-permute-start(bf16[2,96,256]{2,1,0:T(8,128)(2,1)S(1)} %packc.1.refs_0_), channel_id=1, source_target_pairs={{0,1},{1,0},{2,3},{3,2},{4,5},{5,4},{6,7},{7,6},{8,9},{9,8},{10,11... | collective-permute-start | bytes 294920 | tf_op jit(solution)/shard_map/ppermute | solution.py:72

commit v6 on v5

--- a/solution.py
+++ b/solution.py
@@ -10,19 +10,17 @@
 INNER_LEVELS = 2
 PARTS = (4, 6, 6)
 GROUPS = ("a", "b", "c")
-XS = 1
-TURN = 1
 COSTS = {
     "merge2c": 1,
     "lastb": 0.1,
     "lastc": 10,
     "packc": 10,
     "lasta": 1,
-    "packa": 5,
+    "packa": 10,
     "packb": 10,
     "merge1b": 0.4,
     "join": 0.3,
-    "inside": 0.3,
+    "inside": 0.1,
     "merge2a": 0.4,
     "merge1a": 1,
     "place": 10,
@@ -30,18 +28,25 @@
     "merge1c": 1,
     "weights": 1,
     "merge0a": 10,
+    "nearc": 10,
     "farc": 0.4,
     "couplec": 10,
     "holda": 5,
+    "sent0a": 5,
+    "kept0a": 5,
+    "sent1a": 0.5,
+    "kept1a": 0.5,
 }
 ORDER = (
     "f",
     "w",
-    "m0a",
+    "s0a",
+    "k0a",
+    "m0b",
     "m0c",
-    "m0b",
     "i",
-    "m1a",
+    "s1a",
+    "k1a",
     "m1b",
     "m2a",
     "j",
@@ -185,14 +190,13 @@
     return total.astype(jnp.bfloat16)
 
 
-def merge_kernel(level, begin, size, kept_ref, got_ref, w_ref, after_ref, sent_out, kept_out):
+def merge_kernel(level, begin, size, sides, kept_ref, got_ref, w_ref, after_ref, *outs):
     half = kept_ref.shape[0]
     flag = bit_of(level + 1)
-    for slot in range(2 * half):
-        side = 1 - flag if slot < half else flag
-        box = side * half + slot % half
-        out = sent_out if slot < half else kept_out
-        out[slot % half] = merged(level, begin, size, kept_ref, got_ref, w_ref, box // 2, box)
+    for side, out in zip(sides, outs):
+        for slot in range(half):
+            box = (flag if side else 1 - flag) * half + slot
+            out[slot] = merged(level, begin, size, kept_ref, got_ref, w_ref, box // 2, box)
 
 
 def last_kernel(level, pairs, apart, parts, slots_ref, joint_ref, after_ref, *refs):
@@ -204,7 +208,10 @@
     per_box = joint_ref.shape[0] // (2 * half)
     for at, t in enumerate(pairs):
         for odd in range(2):
-            out = outs[odd].at[at] if apart else outs[at].at[odd]
+            if apart:
+                out = outs[odd].at[at]
+            else:
+                out = outs[at].at[odd]
             first = jnp.bitwise_xor(me, 2 * t + odd) * (piece // width)
             for n in range(piece // width):
                 k = jnp.max(slots_ref[(first + n) // per_box])
@@ -223,17 +230,17 @@
         out[1] = got_ref[t]
 
 
-def pack_kernel(turns, *refs):
+def pack_kernel(turns, bases, *refs):
     out = refs[-1]
     for at, t in enumerate(turns):
-        out[t] = refs[at][1]
+        out[t] = refs[at][bases[at] + 1]
 
 
 def space_kernel(*refs):
     refs[-1][...] = jnp.zeros_like(refs[-1])
 
 
-def place_kernel(cuts, counts, early, *refs):
+def place_kernel(cuts, counts, early, turns, bases, *refs):
     out, held_out, held, sems = refs[-4:]
     rows = refs[0].shape[2]
     owners = out.shape[0] // rows
@@ -245,7 +252,9 @@
         for n, (begin, size) in enumerate(cuts[: None if whole else -1]):
             at = sum(counts[:n])
             chunk = refs[at : at + counts[n]]
-            block = chunk[step // 2][0]
+            block = chunk[turns.index(step // 2) if n < len(cuts) - 1 else step // 2][
+                bases[n][step // 2]
+            ]
             if step % 2:
                 mine = early if n == len(cuts) - 1 else owners // 2
                 late = [(ref, t) for ref in chunk[mine:] for t in range(ref.shape[0])]
@@ -298,6 +307,7 @@
     groups = [["abcdefgh".index(x) for x in names] for names in GROUPS]
     spans = [(cuts[m[0]][0], sum(cuts[x][1] for x in m)) for m in groups]
     held = [None] * count
+    parted = [None] * count
     done = [[None] * (inner // 2) for _ in groups]
     swaps = [[] for _ in groups]
     early = inner // 4
@@ -305,7 +315,7 @@
 
     for step in ORDER:
         kind, n = step[0], "abcdefgh".find(step[-1])
-        g = [names[0] for names in GROUPS].index(step[-1]) if kind in "oqutepy" else 0
+        g = [names[0] for names in GROUPS].index(step[-1]) if kind in "oquepy" else 0
         if kind == "f":
             firsts = [cuts[0], (cuts[1][0], columns - cuts[1][0])]
             sent_a, kept_a, sent_b, kept_b = call(
@@ -324,6 +334,7 @@
             got_a, got_b = swapped(sent_a, "inner", 1), swapped(sent_b, "inner", 1)
             held = [(kept_a, got_a, 0)]
             held += [(kept_b, got_b, begin - cuts[1][0]) for begin, _ in cuts[1:]]
+            held = list(held)
             after = kept_b
         elif kind == "w":
             level_w = call(
@@ -357,24 +368,34 @@
                 name="join",
             )
             after = joint
-        elif kind == "m":
+        elif kind in "msk":
             level = int(step[1])
             size = cuts[n][1]
-            kept, got, begin = held[n]
-            sent, kept = call(
-                functools.partial(merge_kernel, level, begin, size),
-                [arr(half, size, rank)] * 2,
+            sides = {"m": (0, 1), "s": (0,), "k": (1,)}[kind]
+            kept, got, begin = parted[n] if kind == "k" else held[n]
+            outs = call(
+                functools.partial(merge_kernel, level, begin, size, sides),
+                [arr(half, size, rank)] * len(sides),
                 [kept, got, transfer if level else level_w, after],
                 [VMEM, VMEM, VMEM, ANY],
-                name=f"merge{level}{step[-1]}",
-            )
-            after = kept
-            axis, bit = level_axis(level + 1)
-            held[n] = (kept, swapped(sent, axis, 1 << bit), 0)
+                name={"m": "merge", "s": "sent", "k": "kept"}[kind] + step[1:],
+            )
+            after = outs[-1]
+            if kind == "s":
+                parted[n] = held[n]
+            if kind != "k":
+                axis, bit = level_axis(level + 1)
+                arriving = swapped(outs[0], axis, 1 << bit)
+            if kind == "m":
+                held[n] = (outs[1], arriving, 0)
+            elif kind == "s":
+                held[n] = (None, arriving, 0)
+            else:
+                held[n] = (outs[0], held[n][1], 0)
         elif kind in "oe":
             apart = kind == "e"
-            near = step[1] == "n"
-            pairs = range(early if apart else 0, early if near else inner // 2)
+            which = {"f": "far", "n": "near"}.get(step[1:-1], "last")
+            pairs = range(early if which == "far" else 0, early if which == "near" else inner // 2)
             members = groups[g]
             size = spans[g][1]
             states = [x for m in members for x in held[m][:2]]
@@ -389,14 +410,14 @@
                 [arr(len(pairs), size, piece)] * 2 if apart else [arr(2, size, piece)] * len(pairs),
                 [slots, joint, after, *states],
                 [VMEM, VMEM, ANY] + [VMEM] * len(states),
-                name=("far" if apart else "last") + step[-1],
+                name=which + step[-1],
             )
             after = outs[0]
             if apart:
                 coupled = [outs[0], swapped(outs[1], "inner", 1)]
             else:
                 for t, x in zip(pairs, outs):
-                    done[g][t] = swapped(x, "inner", 2 * t) if t else x
+                    done[g][t] = (swapped(x, "inner", 2 * t) if t else x, 0)
         elif kind == "p":
             outs = call(
                 couple_kernel,
@@ -407,27 +428,30 @@
             )
             after = outs[0]
             for t, x in enumerate(outs, early):
-                done[g][t] = swapped(x, "inner", 2 * t)
+                done[g][t] = (swapped(x, "inner", 2 * t), 0)
         elif kind == "y":
             after = call(
-                space_kernel, [arr(16, 128)], [after, *done[g]], [ANY] * (1 + len(done[g])), name=f"hold{step[-1]}"
+                space_kernel,
+                [arr(16, 128)],
+                [after] + [x for x, _ in done[g]],
+                [ANY] * (1 + len(done[g])),
+                name=f"hold{step[-1]}",
             )[0]
         elif kind == "x":
-            first = [x for part in (swaps[:-2] if XS else []) for x in part]
+            first = [x for part in swaps[:-2] for x in part]
             after = call(
                 space_kernel, [arr(16, 128)], [after, *first], [ANY] * (1 + len(first)), name="space"
             )[0]
-        elif kind in "qut":
+        elif kind in "qu":
             pairs = inner // 2
-            begin = early if kind == "t" else 0
+            begin = 0
             end = early if kind == "u" else pairs
             if begin < end:
                 turns = list(range(end - begin))
-                if TURN:
-                    turns = turns[early:] + turns[:early]
-                group = [done[g][begin + t] for t in turns]
+                group = [done[g][begin + t][0] for t in turns]
+                bases = [done[g][begin + t][1] for t in turns]
                 after = call(
-                    functools.partial(pack_kernel, turns),
+                    functools.partial(pack_kernel, turns, bases),
                     [arr(len(group), spans[g][1], piece)],
                     group + [after],
                     [VMEM] * len(group) + [ANY],
@@ -436,10 +460,12 @@
                 swaps[g].append(swapped(after, "inner", 1))
         elif kind == "z":
             counts = [len(a) + len(b) for a, b in zip(done[:-1], swaps)] + [early + 1]
-            flat = [x for d, w in zip(done[:-1], swaps) for x in d + w]
-            flat += done[-1][:early] + swaps[-1][:1]
+            turns = list(range(inner // 2))
+            flat = [x for d, w in zip(done[:-1], swaps) for x in [d[t][0] for t in turns] + w]
+            bases = [[x[1] for x in d] for d in done[:-1]] + [[0] * early]
+            flat += [x for x, _ in done[-1][:early]] + swaps[-1][:1]
             placed, rest = call(
-                functools.partial(place_kernel, spans, counts, early),
+                functools.partial(place_kernel, spans, counts, early, turns, bases),
                 [arr(*vectors.shape), arr(inner - 2 * early, piece, columns)],
                 flat + [after],
                 [VMEM] * len(flat) + [ANY],
@@ -451,7 +477,7 @@
                 out_specs=[HBM, VMEM],
             )
             after = rest
-    flat = done[-1][early:] + swaps[-1][1:]
+    flat = [x for x, _ in done[-1][early:]] + swaps[-1][1:]
     return call(
         functools.partial(finish_kernel, spans[-1]),
         [arr(*vectors.shape)],

time: 51.5 us -> 51.2 us (level)
  starting transfers between devices: 28.4 us -> 27.7 us
    ppermute x24, starting transfers between devices: 28.4 us -> 27.7 us  [swapped(): lax.ppermute(array, axis, [(i, i ^ step) for i in range(lax.axis_size(axi...]
    pallas_call x25 -> x27, Pallas kernels: 14.3 us -> 14.5 us  [call(): return list(run(*ins))]
  transfers between devices with their start and end apart: 24 -> 24, of which waited for: 6 -> 6; matrix products, arithmetic and copies ran while one was open for 0% -> 0% of each run, Pallas kernels for 22% -> 23%
where the time goes in v6:
time: 51.2 us; the launch traced here: 51 us
  starting transfers between devices  27.7 us (54%)
  Pallas kernels  14.5 us (28%)
  waiting for transfers between devices  6.85 us (13%)
  local copies, waits for them, and re-layouts  1.59 us (3%)
    ppermute x24, starting transfers between devices, swapped(): lax.ppermute(array, axis, [(i, i ^ step) for i in range(lax.axis_size(axi...  27.7 us
    pallas_call x27, Pallas kernels, call(): return list(run(*ins))  14.5 us
    ppermute x24, waiting for transfers between devices, swapped(): lax.ppermute(array, axis, [(i, i ^ step) for i in range(lax.axis_size(axi...  6.85 us
    unnamed x10, local copies, waits for them, and re-layouts  1.59 us
  transfers between devices with their start and end apart: 24, of which 6 were waited for; matrix products, arithmetic and copies ran while one was open for 0% of the time, Pallas kernels for 23%

profile of v6, /device:TPU:0, one launch (start us, length us, event | category | flops | bytes accessed | tf_op | source)
XLA Modules:
  0.0 51.0 jit_solution(6551244384511049604)
XLA Ops:
  0.0 1.9 %leaves.1 = (bf16[4,64,256]{2,1,0:T(8,128)(2,1)S(1)}, bf16[4,64,256]{2,1,0:T(8,128)(2,1)S(1)}, bf16[4,192,256]{2,1,0:T(8,128)(2,1)S(1)}, bf16[4,192,256]{2,1,0:T(8,128)(2,1)S(1)}) custom-call(bf16[2048,256]{1,0:T(8,128)(2,1)} %x_hbm.1, bf16[2048,256]{1,0:T(8,128)(2,1)} %v_hbm.1), custom_call_target="tpu_custom_call" | custom-call | flops 2000000000 | tf_op jit(solution)/shard_map/leaves/pallas_call | solution.py:111
  1.9 0.5 %collective-permute-start.1 = (bf16[4,64,256]{2,1,0:T(8,128)(2,1)S(1)}, bf16[4,64,256]{2,1,0:T(8,128)(2,1)S(1)}, u32[]{:S(2)}, u32[]{:S(2)}) collective-permute-start(bf16[4,64,256]{2,1,0:T(8,128)(2,1)S(1)} %get-tuple-element.44), channel_id=1, source_target_pairs={{0,1},{1,0},{2,3},{3,2},{4,5},{5,4},{6,7},{7,6},{8,9},{9,8},{10,11... | collective-permute-start | bytes 393224 | tf_op jit(solution)/shard_map/ppermute | solution.py:77
  2.5 1.6 %weights.1.w_ref.after_ref = bf16[8,512,256]{2,1,0:T(8,128)(2,1)S(1)} custom-call(bf16[4,1,1,8,512,256]{5,4,3,2,1,0:T(8,128)(2,1)} %w_ref.15, bf16[4,192,256]{2,1,0:T(8,128)(2,1)S(1)} %get-tuple-element.41.after_ref.kept_ref), custom_call_target="tpu_custom_call" | custom-call | flops 1000000000 | tf_op jit(solution)/shard_map/weights/pallas_call | solution.py:111
  4.1 0.3 sent0a.1.after_ref
  4.4 3.1 %collective-permute-start.2 = (bf16[4,64,256]{2,1,0:T(8,128)(2,1)S(1)}, bf16[4,64,256]{2,1,0:T(8,128)(2,1)S(1)}, u32[]{:S(2)}, u32[]{:S(2)}) collective-permute-start(bf16[4,64,256]{2,1,0:T(8,128)(2,1)S(1)} %sent0a.1.after_ref), channel_id=1, source_target_pairs={{0,2},{1,3},{2,0},{3,1},{4,6},{5,7},{6,4},{7,5},{8,10},{9,11},{10,... | collective-permute-start | bytes 393224 | tf_op jit(solution)/shard_map/ppermute | solution.py:77
  7.5 0.3 kept0a.1.after_ref.kept_ref
  7.8 0.5 merge0b.1
  8.3 0.1 collective-permute-start.4
  8.4 0.5 merge0c.1
  8.9 1.0 %copy-done = bf16[1,1,8,256,256]{4,3,2,1,0:T(8,128)(2,1)S(1)} copy-done((bf16[1,1,8,256,256]{4,3,2,1,0:T(8,128)(2,1)S(1)}, bf16[1,1,8,256,256]{4,3,2,1,0:T(8,128)(2,1)}, u32[]{:S(2)}) %copy-start) | copy-done | bytes 1048600
  9.9 0.3 copy-done.1
  10.2 0.5 inside.1.after_ref.inside_ref
  10.7 0.9 %collective-permute-done.2.got_ref = bf16[4,64,256]{2,1,0:T(8,128)(2,1)S(1)} collective-permute-done((bf16[4,64,256]{2,1,0:T(8,128)(2,1)S(1)}, bf16[4,64,256]{2,1,0:T(8,128)(2,1)S(1)}, u32[]{:S(2)}, u32[]{:S(2)}) %collective-permute-start.2) | collective-permute-done | bytes 131104 | tf_op jit(solution)/shard_map/ppermute | solution.py:77
  11.6 0.3 slice-done.1
  11.9 0.3 sent1a.1.after_ref
  12.2 1.8 %collective-permute-start.3 = (bf16[4,64,256]{2,1,0:T(8,128)(2,1)S(1)}, bf16[4,64,256]{2,1,0:T(8,128)(2,1)S(1)}, u32[]{:S(2)}, u32[]{:S(2)}) collective-permute-start(bf16[4,64,256]{2,1,0:T(8,128)(2,1)S(1)} %sent1a.1.after_ref), channel_id=1, source_target_pairs={{0,8},{8,0},{16,24},{24,16},{1,9},{9,1},{17,25},{25,17},{2,10},{10... | collective-permute-start | bytes 393224 | tf_op jit(solution)/shard_map/ppermute | solution.py:77
  14.0 1.7 %collective-permute-start.6 = (bf16[4,96,256]{2,1,0:T(8,128)(2,1)S(1)}, bf16[4,96,256]{2,1,0:T(8,128)(2,1)S(1)}, u32[]{:S(2)}, u32[]{:S(2)}) collective-permute-start(bf16[4,96,256]{2,1,0:T(8,128)(2,1)S(1)} %get-tuple-element.53), channel_id=1, source_target_pairs={{0,2},{1,3},{2,0},{3,1},{4,6},{5,7},{6,4},{7,5},{8,10},{9,11},{10,... | collective-permute-start | bytes 589832 | tf_op jit(solution)/shard_map/ppermute | solution.py:77
  15.7 0.3 kept1a.1.after_ref.kept_ref
  16.0 0.5 merge1b.1
  16.6 1.7 %collective-permute-start.5 = (bf16[4,96,256]{2,1,0:T(8,128)(2,1)S(1)}, bf16[4,96,256]{2,1,0:T(8,128)(2,1)S(1)}, u32[]{:S(2)}, u32[]{:S(2)}) collective-permute-start(bf16[4,96,256]{2,1,0:T(8,128)(2,1)S(1)} %get-tuple-element.52), channel_id=1, source_target_pairs={{0,8},{8,0},{16,24},{24,16},{1,9},{9,1},{17,25},{25,17},{2,10},{10... | collective-permute-start | bytes 589832 | tf_op jit(solution)/shard_map/ppermute | solution.py:77
  18.3 0.5 merge2a.1
  18.8 1.6 %collective-permute-start.7 = (bf16[4,64,256]{2,1,0:T(8,128)(2,1)S(1)}, bf16[4,64,256]{2,1,0:T(8,128)(2,1)S(1)}, u32[]{:S(2)}, u32[]{:S(2)}) collective-permute-start(bf16[4,64,256]{2,1,0:T(8,128)(2,1)S(1)} %get-tuple-element.56), channel_id=1, source_target_pairs={{0,16},{8,24},{16,0},{24,8},{1,17},{9,25},{17,1},{25,9},{2,18},{10... | collective-permute-start | bytes 393224 | tf_op jit(solution)/shard_map/ppermute | solution.py:77
  20.3 1.3 %join.1 = (bf16[8,512,256]{2,1,0:T(8,128)(2,1)S(1)}, s32[8,8,128]{2,1,0:T(8,128)S(1)}) custom-call(s32[1,1,8]{2,1,0:T(1,128)S(1)} %copy-done.2, bf16[4,1,1,8,512,256]{5,4,3,2,1,0:T(8,128)(2,1)S(1)} %bitcast.1, bf16[8,256,256]{2,1,0:T(8,128)(2,1)S(1)} %inside.1.after_ref.inside_ref, bf16[4,64,256]{2,1,0:T(8,128)(2,1)S(1)} %get-tuple-element.49.after_ref.refs_0_), custom_call_target="tpu_custom_call" | custom-call | flops 300000000 | tf_op jit(solution)/shard_map/join/pallas_call | solution.py:111
  21.6 0.5 merge1c.1
  22.1 0.8 %collective-permute-start.11 = (bf16[4,96,256]{2,1,0:T(8,128)(2,1)S(1)}, bf16[4,96,256]{2,1,0:T(8,128)(2,1)S(1)}, u32[]{:S(2)}, u32[]{:S(2)}) collective-permute-start(bf16[4,96,256]{2,1,0:T(8,128)(2,1)S(1)} %get-tuple-element.61), channel_id=1, source_target_pairs={{0,8},{8,0},{16,24},{24,16},{1,9},{9,1},{17,25},{25,17},{2,10},{10... | collective-permute-start | bytes 589832 | tf_op jit(solution)/shard_map/ppermute | solution.py:77
  22.9 0.5 merge2b.1
  23.4 1.4 %collective-permute-start.12 = (bf16[4,96,256]{2,1,0:T(8,128)(2,1)S(1)}, bf16[4,96,256]{2,1,0:T(8,128)(2,1)S(1)}, u32[]{:S(2)}, u32[]{:S(2)}) collective-permute-start(bf16[4,96,256]{2,1,0:T(8,128)(2,1)S(1)} %get-tuple-element.63), channel_id=1, source_target_pairs={{0,16},{8,24},{16,0},{24,8},{1,17},{9,25},{17,1},{25,9},{2,18},{10... | collective-permute-start | bytes 589832 | tf_op jit(solution)/shard_map/ppermute | solution.py:77
  24.9 0.7 %lasta.1 = (bf16[2,64,256]{2,1,0:T(8,128)(2,1)S(1)}, bf16[2,64,256]{2,1,0:T(8,128)(2,1)S(1)}, bf16[2,64,256]{2,1,0:T(8,128)(2,1)S(1)}, bf16[2,64,256]{2,1,0:T(8,128)(2,1)S(1)}) custom-call(s32[8,8,128]{2,1,0:T(8,128)S(1)} %get-tuple-element.50.slots_ref, bf16[8,512,256]{2,1,0:T(8,128)(2,1)S(1)} %get-tuple-element.51.after_ref.joint_ref, ...), custom_call_target="tpu_custom_call" | custom-call | flops 1000000000 | tf_op jit(solution)/shard_map/lasta/pallas_call | solution.py:111
  25.5 1.4 %collective-permute-start.8 = (bf16[2,64,256]{2,1,0:T(8,128)(2,1)S(1)}, bf16[2,64,256]{2,1,0:T(8,128)(2,1)S(1)}, u32[]{:S(2)}, u32[]{:S(2)}) collective-permute-start(bf16[2,64,256]{2,1,0:T(8,128)(2,1)S(1)} %get-tuple-element.58), channel_id=1, source_target_pairs={{0,2},{1,3},{2,0},{3,1},{4,6},{5,7},{6,4},{7,5},{8,10},{9,11},{10,... | collective-permute-start | bytes 196616 | tf_op jit(solution)/shard_map/ppermute | solution.py:77
  26.9 2.6 %collective-permute-start.9 = (bf16[2,64,256]{2,1,0:T(8,128)(2,1)S(1)}, bf16[2,64,256]{2,1,0:T(8,128)(2,1)S(1)}, u32[]{:S(2)}, u32[]{:S(2)}) collective-permute-start(bf16[2,64,256]{2,1,0:T(8,128)(2,1)S(1)} %get-tuple-element.59), channel_id=1, source_target_pairs={{0,4},{1,5},{2,6},{3,7},{4,0},{5,1},{6,2},{7,3},{8,12},{9,13},{10,... | collective-permute-start | bytes 196616 | tf_op jit(solution)/shard_map/ppermute | solution.py:77
  29.5 0.5 collective-permute-start.10
  30.0 0.5 merge2c.1
  30.5 1.0 %collective-permute-start.13 = (bf16[4,96,256]{2,1,0:T(8,128)(2,1)S(1)}, bf16[4,96,256]{2,1,0:T(8,128)(2,1)S(1)}, u32[]{:S(2)}, u32[]{:S(2)}) collective-permute-start(bf16[4,96,256]{2,1,0:T(8,128)(2,1)S(1)} %get-tuple-element.65), channel_id=1, source_target_pairs={{0,16},{8,24},{16,0},{24,8},{1,17},{9,25},{17,1},{25,9},{2,18},{10... | collective-permute-start | bytes 589832 | tf_op jit(solution)/shard_map/ppermute | solution.py:77
  31.5 0.7 %lastb.1 = (bf16[2,96,256]{2,1,0:T(8,128)(2,1)S(1)}, bf16[2,96,256]{2,1,0:T(8,128)(2,1)S(1)}, bf16[2,96,256]{2,1,0:T(8,128)(2,1)S(1)}, bf16[2,96,256]{2,1,0:T(8,128)(2,1)S(1)}) custom-call(s32[8,8,128]{2,1,0:T(8,128)S(1)} %get-tuple-element.50.slots_ref, bf16[8,512,256]{2,1,0:T(8,128)(2,1)S(1)} %get-tuple-element.51.after_ref.joint_ref, ...), custom_call_target="tpu_custom_call" | custom-call | flops 100000000 | tf_op jit(solution)/shard_map/lastb/pallas_call | solution.py:111
  32.1 1.0 %collective-permute-start.16 = (bf16[2,96,256]{2,1,0:T(8,128)(2,1)S(1)}, bf16[2,96,256]{2,1,0:T(8,128)(2,1)S(1)}, u32[]{:S(2)}, u32[]{:S(2)}) collective-permute-start(bf16[2,96,256]{2,1,0:T(8,128)(2,1)S(1)} %get-tuple-element.70), channel_id=1, source_target_pairs={{0,2},{1,3},{2,0},{3,1},{4,6},{5,7},{6,4},{7,5},{8,10},{9,11},{10,... | collective-permute-start | bytes 294920 | tf_op jit(solution)/shard_map/ppermute | solution.py:77
  33.1 3.5 %collective-permute-start.17 = (bf16[2,96,256]{2,1,0:T(8,128)(2,1)S(1)}, bf16[2,96,256]{2,1,0:T(8,128)(2,1)S(1)}, u32[]{:S(2)}, u32[]{:S(2)}) collective-permute-start(bf16[2,96,256]{2,1,0:T(8,128)(2,1)S(1)} %get-tuple-element.71), channel_id=1, source_target_pairs={{0,4},{1,5},{2,6},{3,7},{4,0},{5,1},{6,2},{7,3},{8,12},{9,13},{10,... | collective-permute-start | bytes 294920 | tf_op jit(solution)/shard_map/ppermute | solution.py:77
  36.6 0.5 farc.1
  37.2 0.5 nearc.1
  37.7 1.6 %collective-permute-start.20 = (bf16[2,96,256]{2,1,0:T(8,128)(2,1)S(1)}, bf16[2,96,256]{2,1,0:T(8,128)(2,1)S(1)}, u32[]{:S(2)}, u32[]{:S(2)}) collective-permute-start(bf16[2,96,256]{2,1,0:T(8,128)(2,1)S(1)} %get-tuple-element.73), channel_id=1, source_target_pairs={{0,2},{1,3},{2,0},{3,1},{4,6},{5,7},{6,4},{7,5},{8,10},{9,11},{10,... | collective-permute-start | bytes 294920 | tf_op jit(solution)/shard_map/ppermute | solution.py:77
  39.3 2.9 %collective-permute-start.22 = (bf16[2,96,256]{2,1,0:T(8,128)(2,1)S(1)}, bf16[2,96,256]{2,1,0:T(8,128)(2,1)S(1)}, u32[]{:S(2)}, u32[]{:S(2)}) collective-permute-start(bf16[2,96,256]{2,1,0:T(8,128)(2,1)S(1)} %get-tuple-element.69.refs_4_), channel_id=1, source_target_pairs={{0,4},{1,5},{2,6},{3,7},{4,0},{5,1},{6,2},{7,3},{8,12},{9,13},{10,... | collective-permute-start | bytes 294920 | tf_op jit(solution)/shard_map/ppermute | solution.py:77
  42.2 0.3 collective-permute-start.23
  42.5 0.6 %collective-permute-done.18.refs_3_.refs_8_ = bf16[2,96,256]{2,1,0:T(8,128)(2,1)S(1)} collective-permute-done((bf16[2,96,256]{2,1,0:T(8,128)(2,1)S(1)}, bf16[2,96,256]{2,1,0:T(8,128)(2,1)S(1)}, u32[]{:S(2)}, u32[]{:S(2)}) %collective-permute-start.18) | collective-permute-done | bytes 98336 | tf_op jit(solution)/shard_map/ppermute | solution.py:77
  43.3 2.7 %collective-permute-done.20.refs_1_.refs_11_ = bf16[2,96,256]{2,1,0:T(8,128)(2,1)S(1)} collective-permute-done((bf16[2,96,256]{2,1,0:T(8,128)(2,1)S(1)}, bf16[2,96,256]{2,1,0:T(8,128)(2,1)S(1)}, u32[]{:S(2)}, u32[]{:S(2)}) %collective-permute-start.20) | collective-permute-done | bytes 98336 | tf_op jit(solution)/shard_map/ppermute | solution.py:77
  46.1 1.3 %collective-permute-done.21.refs_12_ = bf16[2,96,256]{2,1,0:T(8,128)(2,1)S(1)} collective-permute-done((bf16[2,96,256]{2,1,0:T(8,128)(2,1)S(1)}, bf16[2,96,256]{2,1,0:T(8,128)(2,1)S(1)}, u32[]{:S(2)}, u32[]{:S(2)}) %collective-permute-start.21) | collective-permute-done | bytes 98336 | tf_op jit(solution)/shard_map/ppermute | solution.py:77
  47.3 1.4 %place.1 = (bf16[2048,256]{1,0:T(8,128)(2,1)}, bf16[4,256,256]{2,1,0:T(8,128)(2,1)S(1)}) custom-call(bf16[2,64,256]{2,1,0:T(8,128)(2,1)S(1)} %get-tuple-element.57.after_ref.refs_1_.refs_0_, bf16[2,64,256]{2,1,0:T(8,128)(2,1)S(1)} %collective-permute-done.8.refs_2_.refs_1_, bf16[2,64,256]{2,1,0:T(8,128)(2,1)S(1)} %collective-permute-done.9.refs_3_.refs_2_, ...), custom_call_target="tpu_custom_call" | custom-call | flops 10000000000 | tf_op jit(solution)/shard_map/place/pallas_call | solution.py:111
  48.7 0.7 %collective-permute-done.23.refs_1_ = bf16[2,96,256]{2,1,0:T(8,128)(2,1)S(1)} collective-permute-done((bf16[2,96,256]{2,1,0:T(8,128)(2,1)S(1)}, bf16[2,96,256]{2,1,0:T(8,128)(2,1)S(1)}, u32[]{:S(2)}, u32[]{:S(2)}) %collective-permute-start.23) | collective-permute-done | bytes 98336 | tf_op jit(solution)/shard_map/ppermute | solution.py:77
  49.4 0.6 %collective-permute-done.22.refs_0_ = bf16[2,96,256]{2,1,0:T(8,128)(2,1)S(1)} collective-permute-done((bf16[2,96,256]{2,1,0:T(8,128)(2,1)S(1)}, bf16[2,96,256]{2,1,0:T(8,128)(2,1)S(1)}, u32[]{:S(2)}, u32[]{:S(2)}) %collective-permute-start.22) | collective-permute-done | bytes 98336 | tf_op jit(solution)/shard_map/ppermute | solution.py:77
  50.0 1.0 %finish.1 = bf16[2048,256]{1,0:T(8,128)(2,1)} custom-call(bf16[2048,256]{1,0:T(8,128)(2,1)} %get-tuple-element.74.first_ref, bf16[4,256,256]{2,1,0:T(8,128)(2,1)S(1)} %get-tuple-element.75.held_ref, bf16[2,96,256]{2,1,0:T(8,128)(2,1)S(1)} %collective-permute-done.22.refs_0_, ...), custom_call_target="tpu_custom_call", output_to_operand_aliasing={{}: (0, {})} | custom-call | flops 2000000000 | tf_op jit(solution)/shard_map/finish/pallas_call | solution.py:111
  (38 shorter events, 0.4 us)
Async XLA Ops:
  1.9 2.2 %collective-permute-start.1 = (bf16[4,64,256]{2,1,0:T(8,128)(2,1)S(1)}, bf16[4,64,256]{2,1,0:T(8,128)(2,1)S(1)}, u32[]{:S(2)}, u32[]{:S(2)}) collective-permute-start(bf16[4,64,256]{2,1,0:T(8,128)(2,1)S(1)} %get-tuple-element.44), channel_id=1, source_target_pairs={{0,1},{1,0},{2,3},{3,2},{4,5},{5,4},{6,7},{7,6},{8,9},{9,8},{10,11... | collective-permute-start | bytes 393224 | tf_op jit(solution)/shard_map/ppermute | solution.py:77
  2.5 5.3 %collective-permute-start = (bf16[4,192,256]{2,1,0:T(8,128)(2,1)S(1)}, bf16[4,192,256]{2,1,0:T(8,128)(2,1)S(1)}, u32[]{:S(2)}, u32[]{:S(2)}) collective-permute-start(bf16[4,192,256]{2,1,0:T(8,128)(2,1)S(1)} %get-tuple-element.42), channel_id=1, source_target_pairs={{0,1},{1,0},{2,3},{3,2},{4,5},{5,4},{6,7},{7,6},{8,9},{9,8},{10,11... | collective-permute-start | bytes 1179656 | tf_op jit(solution)/shard_map/ppermute | solution.py:77
  4.4 7.2 %collective-permute-start.2 = (bf16[4,64,256]{2,1,0:T(8,128)(2,1)S(1)}, bf16[4,64,256]{2,1,0:T(8,128)(2,1)S(1)}, u32[]{:S(2)}, u32[]{:S(2)}) collective-permute-start(bf16[4,64,256]{2,1,0:T(8,128)(2,1)S(1)} %sent0a.1.after_ref), channel_id=1, source_target_pairs={{0,2},{1,3},{2,0},{3,1},{4,6},{5,7},{6,4},{7,5},{8,10},{9,11},{10,... | collective-permute-start | bytes 393224 | tf_op jit(solution)/shard_map/ppermute | solution.py:77
  7.8 3.8 %slice-start = ((s8[8388608]{0:T(1024)(128)(4,1)}), s8[4194304]{0:T(1024)(128)(4,1)S(1)}, s32[]{:S(2)}) async-start(s8[8388608]{0:T(1024)(128)(4,1)} %bitcast), calls=%async_computation | async-start | bytes 8388608
  8.3 7.7 %collective-permute-start.4 = (bf16[4,96,256]{2,1,0:T(8,128)(2,1)S(1)}, bf16[4,96,256]{2,1,0:T(8,128)(2,1)S(1)}, u32[]{:S(2)}, u32[]{:S(2)}) collective-permute-start(bf16[4,96,256]{2,1,0:T(8,128)(2,1)S(1)} %get-tuple-element.47), channel_id=1, source_target_pairs={{0,2},{1,3},{2,0},{3,1},{4,6},{5,7},{6,4},{7,5},{8,10},{9,11},{10,... | collective-permute-start | bytes 589832 | tf_op jit(solution)/shard_map/ppermute | solution.py:77
  8.4 1.5 %copy-start = (bf16[1,1,8,256,256]{4,3,2,1,0:T(8,128)(2,1)S(1)}, bf16[1,1,8,256,256]{4,3,2,1,0:T(8,128)(2,1)}, u32[]{:S(2)}) copy-start(bf16[1,1,8,256,256]{4,3,2,1,0:T(8,128)(2,1)} %core_ref.1) | copy-start | bytes 3145732
  8.4 1.8 %copy-start.1 = (bf16[2048,256]{1,0:T(8,128)(2,1)S(1)}, bf16[2048,256]{1,0:T(8,128)(2,1)}, u32[]{:S(2)}) copy-start(bf16[2048,256]{1,0:T(8,128)(2,1)} %u_ref.1) | copy-start | bytes 3145732
  8.4 3.5 %slice-start.1 = ((s8[8388608]{0:T(1024)(128)(4,1)}), s8[4194304]{0:T(1024)(128)(4,1)S(1)}, s32[]{:S(2)}) async-start(s8[8388608]{0:T(1024)(128)(4,1)} %bitcast), calls=%async_computation.1 | async-start | bytes 8388608
  12.2 6.0 %collective-permute-start.3 = (bf16[4,64,256]{2,1,0:T(8,128)(2,1)S(1)}, bf16[4,64,256]{2,1,0:T(8,128)(2,1)S(1)}, u32[]{:S(2)}, u32[]{:S(2)}) collective-permute-start(bf16[4,64,256]{2,1,0:T(8,128)(2,1)S(1)} %sent1a.1.after_ref), channel_id=1, source_target_pairs={{0,8},{8,0},{16,24},{24,16},{1,9},{9,1},{17,25},{25,17},{2,10},{10... | collective-permute-start | bytes 393224 | tf_op jit(solution)/shard_map/ppermute | solution.py:77
  14.0 7.6 %collective-permute-start.6 = (bf16[4,96,256]{2,1,0:T(8,128)(2,1)S(1)}, bf16[4,96,256]{2,1,0:T(8,128)(2,1)S(1)}, u32[]{:S(2)}, u32[]{:S(2)}) collective-permute-start(bf16[4,96,256]{2,1,0:T(8,128)(2,1)S(1)} %get-tuple-element.53), channel_id=1, source_target_pairs={{0,2},{1,3},{2,0},{3,1},{4,6},{5,7},{6,4},{7,5},{8,10},{9,11},{10,... | collective-permute-start | bytes 589832 | tf_op jit(solution)/shard_map/ppermute | solution.py:77
  16.6 6.4 %collective-permute-start.5 = (bf16[4,96,256]{2,1,0:T(8,128)(2,1)S(1)}, bf16[4,96,256]{2,1,0:T(8,128)(2,1)S(1)}, u32[]{:S(2)}, u32[]{:S(2)}) collective-permute-start(bf16[4,96,256]{2,1,0:T(8,128)(2,1)S(1)} %get-tuple-element.52), channel_id=1, source_target_pairs={{0,8},{8,0},{16,24},{24,16},{1,9},{9,1},{17,25},{25,17},{2,10},{10... | collective-permute-start | bytes 589832 | tf_op jit(solution)/shard_map/ppermute | solution.py:77
  18.3 2.1 %copy-start.2 = (s32[1,1,8]{2,1,0:T(1,128)S(1)}, s32[1,1,8]{2,1,0:T(1,128)}, u32[]{:S(2)}) copy-start(s32[1,1,8]{2,1,0:T(1,128)} %order_ref.1) | copy-start | bytes 100
  18.8 6.1 %collective-permute-start.7 = (bf16[4,64,256]{2,1,0:T(8,128)(2,1)S(1)}, bf16[4,64,256]{2,1,0:T(8,128)(2,1)S(1)}, u32[]{:S(2)}, u32[]{:S(2)}) collective-permute-start(bf16[4,64,256]{2,1,0:T(8,128)(2,1)S(1)} %get-tuple-element.56), channel_id=1, source_target_pairs={{0,16},{8,24},{16,0},{24,8},{1,17},{9,25},{17,1},{25,9},{2,18},{10... | collective-permute-start | bytes 393224 | tf_op jit(solution)/shard_map/ppermute | solution.py:77
  22.1 7.9 %collective-permute-start.11 = (bf16[4,96,256]{2,1,0:T(8,128)(2,1)S(1)}, bf16[4,96,256]{2,1,0:T(8,128)(2,1)S(1)}, u32[]{:S(2)}, u32[]{:S(2)}) collective-permute-start(bf16[4,96,256]{2,1,0:T(8,128)(2,1)S(1)} %get-tuple-element.61), channel_id=1, source_target_pairs={{0,8},{8,0},{16,24},{24,16},{1,9},{9,1},{17,25},{25,17},{2,10},{10... | collective-permute-start | bytes 589832 | tf_op jit(solution)/shard_map/ppermute | solution.py:77
  23.4 8.1 %collective-permute-start.12 = (bf16[4,96,256]{2,1,0:T(8,128)(2,1)S(1)}, bf16[4,96,256]{2,1,0:T(8,128)(2,1)S(1)}, u32[]{:S(2)}, u32[]{:S(2)}) collective-permute-start(bf16[4,96,256]{2,1,0:T(8,128)(2,1)S(1)} %get-tuple-element.63), channel_id=1, source_target_pairs={{0,16},{8,24},{16,0},{24,8},{1,17},{9,25},{17,1},{25,9},{2,18},{10... | collective-permute-start | bytes 589832 | tf_op jit(solution)/shard_map/ppermute | solution.py:77
  25.5 7.6 %collective-permute-start.8 = (bf16[2,64,256]{2,1,0:T(8,128)(2,1)S(1)}, bf16[2,64,256]{2,1,0:T(8,128)(2,1)S(1)}, u32[]{:S(2)}, u32[]{:S(2)}) collective-permute-start(bf16[2,64,256]{2,1,0:T(8,128)(2,1)S(1)} %get-tuple-element.58), channel_id=1, source_target_pairs={{0,2},{1,3},{2,0},{3,1},{4,6},{5,7},{6,4},{7,5},{8,10},{9,11},{10,... | collective-permute-start | bytes 196616 | tf_op jit(solution)/shard_map/ppermute | solution.py:77
  26.9 9.7 %collective-permute-start.9 = (bf16[2,64,256]{2,1,0:T(8,128)(2,1)S(1)}, bf16[2,64,256]{2,1,0:T(8,128)(2,1)S(1)}, u32[]{:S(2)}, u32[]{:S(2)}) collective-permute-start(bf16[2,64,256]{2,1,0:T(8,128)(2,1)S(1)} %get-tuple-element.59), channel_id=1, source_target_pairs={{0,4},{1,5},{2,6},{3,7},{4,0},{5,1},{6,2},{7,3},{8,12},{9,13},{10,... | collective-permute-start | bytes 196616 | tf_op jit(solution)/shard_map/ppermute | solution.py:77
  29.5 7.1 %collective-permute-start.10 = (bf16[2,64,256]{2,1,0:T(8,128)(2,1)S(1)}, bf16[2,64,256]{2,1,0:T(8,128)(2,1)S(1)}, u32[]{:S(2)}, u32[]{:S(2)}) collective-permute-start(bf16[2,64,256]{2,1,0:T(8,128)(2,1)S(1)} %get-tuple-element.60), channel_id=1, source_target_pairs={{0,6},{1,7},{2,4},{3,5},{4,2},{5,3},{6,0},{7,1},{8,14},{9,15},{10,... | collective-permute-start | bytes 196616 | tf_op jit(solution)/shard_map/ppermute | solution.py:77
  30.5 6.2 %collective-permute-start.13 = (bf16[4,96,256]{2,1,0:T(8,128)(2,1)S(1)}, bf16[4,96,256]{2,1,0:T(8,128)(2,1)S(1)}, u32[]{:S(2)}, u32[]{:S(2)}) collective-permute-start(bf16[4,96,256]{2,1,0:T(8,128)(2,1)S(1)} %get-tuple-element.65), channel_id=1, source_target_pairs={{0,16},{8,24},{16,0},{24,8},{1,17},{9,25},{17,1},{25,9},{2,18},{10... | collective-permute-start | bytes 589832 | tf_op jit(solution)/shard_map/ppermute | solution.py:77
  32.1 10.1 %collective-permute-start.16 = (bf16[2,96,256]{2,1,0:T(8,128)(2,1)S(1)}, bf16[2,96,256]{2,1,0:T(8,128)(2,1)S(1)}, u32[]{:S(2)}, u32[]{:S(2)}) collective-permute-start(bf16[2,96,256]{2,1,0:T(8,128)(2,1)S(1)} %get-tuple-element.70), channel_id=1, source_target_pairs={{0,2},{1,3},{2,0},{3,1},{4,6},{5,7},{6,4},{7,5},{8,10},{9,11},{10,... | collective-permute-start | bytes 294920 | tf_op jit(solution)/shard_map/ppermute | solution.py:77
  33.1 9.4 %collective-permute-start.17 = (bf16[2,96,256]{2,1,0:T(8,128)(2,1)S(1)}, bf16[2,96,256]{2,1,0:T(8,128)(2,1)S(1)}, u32[]{:S(2)}, u32[]{:S(2)}) collective-permute-start(bf16[2,96,256]{2,1,0:T(8,128)(2,1)S(1)} %get-tuple-element.71), channel_id=1, source_target_pairs={{0,4},{1,5},{2,6},{3,7},{4,0},{5,1},{6,2},{7,3},{8,12},{9,13},{10,... | collective-permute-start | bytes 294920 | tf_op jit(solution)/shard_map/ppermute | solution.py:77
  36.6 6.5 %collective-permute-start.18 = (bf16[2,96,256]{2,1,0:T(8,128)(2,1)S(1)}, bf16[2,96,256]{2,1,0:T(8,128)(2,1)S(1)}, u32[]{:S(2)}, u32[]{:S(2)}) collective-permute-start(bf16[2,96,256]{2,1,0:T(8,128)(2,1)S(1)} %get-tuple-element.72), channel_id=1, source_target_pairs={{0,6},{1,7},{2,4},{3,5},{4,2},{5,3},{6,0},{7,1},{8,14},{9,15},{10,... | collective-permute-start | bytes 294920 | tf_op jit(solution)/shard_map/ppermute | solution.py:77
  37.1 2.1 %collective-permute-start.14 = (bf16[2,96,256]{2,1,0:T(8,128)(2,1)S(1)}, bf16[2,96,256]{2,1,0:T(8,128)(2,1)S(1)}, u32[]{:S(2)}, u32[]{:S(2)}) collective-permute-start(bf16[2,96,256]{2,1,0:T(8,128)(2,1)S(1)} %get-tuple-element.67), channel_id=1, source_target_pairs={{0,1},{1,0},{2,3},{3,2},{4,5},{5,4},{6,7},{7,6},{8,9},{9,8},{10,11... | collective-permute-start | bytes 294920 | tf_op jit(solution)/shard_map/ppermute | solution.py:77
  37.7 8.3 %collective-permute-start.20 = (bf16[2,96,256]{2,1,0:T(8,128)(2,1)S(1)}, bf16[2,96,256]{2,1,0:T(8,128)(2,1)S(1)}, u32[]{:S(2)}, u32[]{:S(2)}) collective-permute-start(bf16[2,96,256]{2,1,0:T(8,128)(2,1)S(1)} %get-tuple-element.73), channel_id=1, source_target_pairs={{0,2},{1,3},{2,0},{3,1},{4,6},{5,7},{6,4},{7,5},{8,10},{9,11},{10,... | collective-permute-start | bytes 294920 | tf_op jit(solution)/shard_map/ppermute | solution.py:77
  39.3 10.7 %collective-permute-start.22 = (bf16[2,96,256]{2,1,0:T(8,128)(2,1)S(1)}, bf16[2,96,256]{2,1,0:T(8,128)(2,1)S(1)}, u32[]{:S(2)}, u32[]{:S(2)}) collective-permute-start(bf16[2,96,256]{2,1,0:T(8,128)(2,1)S(1)} %get-tuple-element.69.refs_4_), channel_id=1, source_target_pairs={{0,4},{1,5},{2,6},{3,7},{4,0},{5,1},{6,2},{7,3},{8,12},{9,13},{10,... | collective-permute-start | bytes 294920 | tf_op jit(solution)/shard_map/ppermute | solution.py:77
  42.2 7.2 %collective-permute-start.23 = (bf16[2,96,256]{2,1,0:T(8,128)(2,1)S(1)}, bf16[2,96,256]{2,1,0:T(8,128)(2,1)S(1)}, u32[]{:S(2)}, u32[]{:S(2)}) collective-permute-start(bf16[2,96,256]{2,1,0:T(8,128)(2,1)S(1)} %get-tuple-element.76), channel_id=1, source_target_pairs={{0,6},{1,7},{2,4},{3,5},{4,2},{5,3},{6,0},{7,1},{8,14},{9,15},{10,... | collective-permute-start | bytes 294920 | tf_op jit(solution)/shard_map/ppermute | solution.py:77
  42.5 3.5 %collective-permute-start.15 = (bf16[4,64,256]{2,1,0:T(8,128)(2,1)S(1)}, bf16[4,64,256]{2,1,0:T(8,128)(2,1)S(1)}, u32[]{:S(2)}, u32[]{:S(2)}) collective-permute-start(bf16[4,64,256]{2,1,0:T(8,128)(2,1)S(1)} %packa.1.refs_4_), channel_id=1, source_target_pairs={{0,1},{1,0},{2,3},{3,2},{4,5},{5,4},{6,7},{7,6},{8,9},{9,8},{10,11... | collective-permute-start | bytes 393224 | tf_op jit(solution)/shard_map/ppermute | solution.py:77
  43.2 4.2 %collective-permute-start.19 = (bf16[4,96,256]{2,1,0:T(8,128)(2,1)S(1)}, bf16[4,96,256]{2,1,0:T(8,128)(2,1)S(1)}, u32[]{:S(2)}, u32[]{:S(2)}) collective-permute-start(bf16[4,96,256]{2,1,0:T(8,128)(2,1)S(1)} %packb.1.refs_2_), channel_id=1, source_target_pairs={{0,1},{1,0},{2,3},{3,2},{4,5},{5,4},{6,7},{7,6},{8,9},{9,8},{10,11... | collective-permute-start | bytes 589832 | tf_op jit(solution)/shard_map/ppermute | solution.py:77
  46.0 1.4 %collective-permute-start.21 = (bf16[2,96,256]{2,1,0:T(8,128)(2,1)S(1)}, bf16[2,96,256]{2,1,0:T(8,128)(2,1)S(1)}, u32[]{:S(2)}, u32[]{:S(2)}) collective-permute-start(bf16[2,96,256]{2,1,0:T(8,128)(2,1)S(1)} %packc.1.refs_0_), channel_id=1, source_target_pairs={{0,1},{1,0},{2,3},{3,2},{4,5},{5,4},{6,7},{7,6},{8,9},{9,8},{10,11... | collective-permute-start | bytes 294920 | tf_op jit(solution)/shard_map/ppermute | solution.py:77

commit v7 on v6

--- a/solution.py
+++ b/solution.py
@@ -11,11 +11,10 @@
 PARTS = (4, 6, 6)
 GROUPS = ("a", "b", "c")
 COSTS = {
-    "merge2c": 1,
     "lastb": 0.1,
     "lastc": 10,
     "packc": 10,
-    "lasta": 1,
+    "lasta": 2,
     "packa": 10,
     "packb": 10,
     "merge1b": 0.4,
@@ -35,7 +34,9 @@
     "sent0a": 5,
     "kept0a": 5,
     "sent1a": 0.5,
-    "kept1a": 0.5,
+    "kept1a": 0.1,
+    "sent2c": 1,
+    "kept2c": 0.1,
 }
 ORDER = (
     "f",
@@ -53,7 +54,8 @@
     "m1c",
     "m2b",
     "oa",
-    "m2c",
+    "s2c",
+    "k2c",
     "ob",
     "ya",
     "efc",

time: 51.2 us -> 51.3 us (level)
    pallas_call x27 -> x28, Pallas kernels: 14.5 us -> 14.7 us  [call(): return list(run(*ins))]
where the time goes in v7:
time: 51.3 us; the launch traced here: 51.1 us
  starting transfers between devices  27.7 us (54%)
  Pallas kernels  14.7 us (29%)
  waiting for transfers between devices  6.88 us (13%)
  local copies, waits for them, and re-layouts  1.59 us (3%)
    ppermute x24, starting transfers between devices, swapped(): lax.ppermute(array, axis, [(i, i ^ step) for i in range(lax.axis_size(axi...  27.7 us
    pallas_call x28, Pallas kernels, call(): return list(run(*ins))  14.7 us
    ppermute x24, waiting for transfers between devices, swapped(): lax.ppermute(array, axis, [(i, i ^ step) for i in range(lax.axis_size(axi...  6.88 us
    unnamed x10, local copies, waits for them, and re-layouts  1.59 us
  transfers between devices with their start and end apart: 24, of which 6 were waited for; matrix products, arithmetic and copies ran while one was open for 0% of the time, Pallas kernels for 23%

profile of v7, /device:TPU:0, one launch (start us, length us, event | category | flops | bytes accessed | tf_op | source)
XLA Modules:
  0.0 51.1 jit_solution(17778369002198444920)
XLA Ops:
  0.0 1.9 %leaves.1 = (bf16[4,64,256]{2,1,0:T(8,128)(2,1)S(1)}, bf16[4,64,256]{2,1,0:T(8,128)(2,1)S(1)}, bf16[4,192,256]{2,1,0:T(8,128)(2,1)S(1)}, bf16[4,192,256]{2,1,0:T(8,128)(2,1)S(1)}) custom-call(bf16[2048,256]{1,0:T(8,128)(2,1)} %x_hbm.1, bf16[2048,256]{1,0:T(8,128)(2,1)} %v_hbm.1), custom_call_target="tpu_custom_call" | custom-call | flops 2000000000 | tf_op jit(solution)/shard_map/leaves/pallas_call | solution.py:113
  1.9 0.5 %collective-permute-start.1 = (bf16[4,64,256]{2,1,0:T(8,128)(2,1)S(1)}, bf16[4,64,256]{2,1,0:T(8,128)(2,1)S(1)}, u32[]{:S(2)}, u32[]{:S(2)}) collective-permute-start(bf16[4,64,256]{2,1,0:T(8,128)(2,1)S(1)} %get-tuple-element.42), channel_id=1, source_target_pairs={{0,1},{1,0},{2,3},{3,2},{4,5},{5,4},{6,7},{7,6},{8,9},{9,8},{10,11... | collective-permute-start | bytes 393224 | tf_op jit(solution)/shard_map/ppermute | solution.py:79
  2.5 1.6 %weights.1.w_ref.after_ref = bf16[8,512,256]{2,1,0:T(8,128)(2,1)S(1)} custom-call(bf16[4,1,1,8,512,256]{5,4,3,2,1,0:T(8,128)(2,1)} %w_ref.17, bf16[4,192,256]{2,1,0:T(8,128)(2,1)S(1)} %get-tuple-element.39.after_ref.kept_ref), custom_call_target="tpu_custom_call" | custom-call | flops 1000000000 | tf_op jit(solution)/shard_map/weights/pallas_call | solution.py:113
  4.1 0.3 sent0a.1.after_ref
  4.4 3.1 %collective-permute-start.2 = (bf16[4,64,256]{2,1,0:T(8,128)(2,1)S(1)}, bf16[4,64,256]{2,1,0:T(8,128)(2,1)S(1)}, u32[]{:S(2)}, u32[]{:S(2)}) collective-permute-start(bf16[4,64,256]{2,1,0:T(8,128)(2,1)S(1)} %sent0a.1.after_ref), channel_id=1, source_target_pairs={{0,2},{1,3},{2,0},{3,1},{4,6},{5,7},{6,4},{7,5},{8,10},{9,11},{10,... | collective-permute-start | bytes 393224 | tf_op jit(solution)/shard_map/ppermute | solution.py:79
  7.5 0.3 kept0a.1.after_ref.kept_ref
  7.8 0.5 merge0b.1
  8.4 0.5 merge0c.1
  8.9 1.0 %copy-done = bf16[1,1,8,256,256]{4,3,2,1,0:T(8,128)(2,1)S(1)} copy-done((bf16[1,1,8,256,256]{4,3,2,1,0:T(8,128)(2,1)S(1)}, bf16[1,1,8,256,256]{4,3,2,1,0:T(8,128)(2,1)}, u32[]{:S(2)}) %copy-start) | copy-done | bytes 1048600
  9.9 0.3 copy-done.1
  10.2 0.5 inside.1.after_ref.inside_ref
  10.7 0.9 %collective-permute-done.2.got_ref = bf16[4,64,256]{2,1,0:T(8,128)(2,1)S(1)} collective-permute-done((bf16[4,64,256]{2,1,0:T(8,128)(2,1)S(1)}, bf16[4,64,256]{2,1,0:T(8,128)(2,1)S(1)}, u32[]{:S(2)}, u32[]{:S(2)}) %collective-permute-start.2) | collective-permute-done | bytes 131104 | tf_op jit(solution)/shard_map/ppermute | solution.py:79
  11.6 0.3 slice-done.1
  11.9 0.3 sent1a.1.after_ref
  12.2 1.8 %collective-permute-start.3 = (bf16[4,64,256]{2,1,0:T(8,128)(2,1)S(1)}, bf16[4,64,256]{2,1,0:T(8,128)(2,1)S(1)}, u32[]{:S(2)}, u32[]{:S(2)}) collective-permute-start(bf16[4,64,256]{2,1,0:T(8,128)(2,1)S(1)} %sent1a.1.after_ref), channel_id=1, source_target_pairs={{0,8},{8,0},{16,24},{24,16},{1,9},{9,1},{17,25},{25,17},{2,10},{10... | collective-permute-start | bytes 393224 | tf_op jit(solution)/shard_map/ppermute | solution.py:79
  14.0 1.7 %collective-permute-start.6 = (bf16[4,96,256]{2,1,0:T(8,128)(2,1)S(1)}, bf16[4,96,256]{2,1,0:T(8,128)(2,1)S(1)}, u32[]{:S(2)}, u32[]{:S(2)}) collective-permute-start(bf16[4,96,256]{2,1,0:T(8,128)(2,1)S(1)} %get-tuple-element.51), channel_id=1, source_target_pairs={{0,2},{1,3},{2,0},{3,1},{4,6},{5,7},{6,4},{7,5},{8,10},{9,11},{10,... | collective-permute-start | bytes 589832 | tf_op jit(solution)/shard_map/ppermute | solution.py:79
  15.7 0.3 kept1a.1.after_ref.kept_ref
  16.0 0.5 merge1b.1
  16.6 1.7 %collective-permute-start.5 = (bf16[4,96,256]{2,1,0:T(8,128)(2,1)S(1)}, bf16[4,96,256]{2,1,0:T(8,128)(2,1)S(1)}, u32[]{:S(2)}, u32[]{:S(2)}) collective-permute-start(bf16[4,96,256]{2,1,0:T(8,128)(2,1)S(1)} %get-tuple-element.50), channel_id=1, source_target_pairs={{0,8},{8,0},{16,24},{24,16},{1,9},{9,1},{17,25},{25,17},{2,10},{10... | collective-permute-start | bytes 589832 | tf_op jit(solution)/shard_map/ppermute | solution.py:79
  18.3 0.5 merge2a.1
  18.8 1.6 %collective-permute-start.7 = (bf16[4,64,256]{2,1,0:T(8,128)(2,1)S(1)}, bf16[4,64,256]{2,1,0:T(8,128)(2,1)S(1)}, u32[]{:S(2)}, u32[]{:S(2)}) collective-permute-start(bf16[4,64,256]{2,1,0:T(8,128)(2,1)S(1)} %get-tuple-element.54), channel_id=1, source_target_pairs={{0,16},{8,24},{16,0},{24,8},{1,17},{9,25},{17,1},{25,9},{2,18},{10... | collective-permute-start | bytes 393224 | tf_op jit(solution)/shard_map/ppermute | solution.py:79
  20.3 1.3 %join.1 = (bf16[8,512,256]{2,1,0:T(8,128)(2,1)S(1)}, s32[8,8,128]{2,1,0:T(8,128)S(1)}) custom-call(s32[1,1,8]{2,1,0:T(1,128)S(1)} %copy-done.2, bf16[4,1,1,8,512,256]{5,4,3,2,1,0:T(8,128)(2,1)S(1)} %bitcast.1, bf16[8,256,256]{2,1,0:T(8,128)(2,1)S(1)} %inside.1.after_ref.inside_ref, bf16[4,64,256]{2,1,0:T(8,128)(2,1)S(1)} %get-tuple-element.47.after_ref.refs_0_), custom_call_target="tpu_custom_call" | custom-call | flops 300000000 | tf_op jit(solution)/shard_map/join/pallas_call | solution.py:113
  21.6 0.5 merge1c.1
  22.1 0.8 %collective-permute-start.11 = (bf16[4,96,256]{2,1,0:T(8,128)(2,1)S(1)}, bf16[4,96,256]{2,1,0:T(8,128)(2,1)S(1)}, u32[]{:S(2)}, u32[]{:S(2)}) collective-permute-start(bf16[4,96,256]{2,1,0:T(8,128)(2,1)S(1)} %get-tuple-element.59), channel_id=1, source_target_pairs={{0,8},{8,0},{16,24},{24,16},{1,9},{9,1},{17,25},{25,17},{2,10},{10... | collective-permute-start | bytes 589832 | tf_op jit(solution)/shard_map/ppermute | solution.py:79
  22.9 0.5 merge2b.1
  23.4 1.4 %collective-permute-start.12 = (bf16[4,96,256]{2,1,0:T(8,128)(2,1)S(1)}, bf16[4,96,256]{2,1,0:T(8,128)(2,1)S(1)}, u32[]{:S(2)}, u32[]{:S(2)}) collective-permute-start(bf16[4,96,256]{2,1,0:T(8,128)(2,1)S(1)} %get-tuple-element.60), channel_id=1, source_target_pairs={{0,16},{8,24},{16,0},{24,8},{1,17},{9,25},{17,1},{25,9},{2,18},{10... | collective-permute-start | bytes 589832 | tf_op jit(solution)/shard_map/ppermute | solution.py:79
  24.9 0.7 %lasta.1 = (bf16[2,64,256]{2,1,0:T(8,128)(2,1)S(1)}, bf16[2,64,256]{2,1,0:T(8,128)(2,1)S(1)}, bf16[2,64,256]{2,1,0:T(8,128)(2,1)S(1)}, bf16[2,64,256]{2,1,0:T(8,128)(2,1)S(1)}) custom-call(s32[8,8,128]{2,1,0:T(8,128)S(1)} %get-tuple-element.48.slots_ref, bf16[8,512,256]{2,1,0:T(8,128)(2,1)S(1)} %get-tuple-element.49.after_ref.joint_ref, ...), custom_call_target="tpu_custom_call" | custom-call | flops 2000000000 | tf_op jit(solution)/shard_map/lasta/pallas_call | solution.py:113
  25.5 1.4 %collective-permute-start.8 = (bf16[2,64,256]{2,1,0:T(8,128)(2,1)S(1)}, bf16[2,64,256]{2,1,0:T(8,128)(2,1)S(1)}, u32[]{:S(2)}, u32[]{:S(2)}) collective-permute-start(bf16[2,64,256]{2,1,0:T(8,128)(2,1)S(1)} %get-tuple-element.56), channel_id=1, source_target_pairs={{0,2},{1,3},{2,0},{3,1},{4,6},{5,7},{6,4},{7,5},{8,10},{9,11},{10,... | collective-permute-start | bytes 196616 | tf_op jit(solution)/shard_map/ppermute | solution.py:79
  26.9 2.6 %collective-permute-start.9 = (bf16[2,64,256]{2,1,0:T(8,128)(2,1)S(1)}, bf16[2,64,256]{2,1,0:T(8,128)(2,1)S(1)}, u32[]{:S(2)}, u32[]{:S(2)}) collective-permute-start(bf16[2,64,256]{2,1,0:T(8,128)(2,1)S(1)} %get-tuple-element.57), channel_id=1, source_target_pairs={{0,4},{1,5},{2,6},{3,7},{4,0},{5,1},{6,2},{7,3},{8,12},{9,13},{10,... | collective-permute-start | bytes 196616 | tf_op jit(solution)/shard_map/ppermute | solution.py:79
  29.5 0.5 collective-permute-start.10
  30.0 0.3 sent2c.1.after_ref
  30.3 1.0 %collective-permute-start.13 = (bf16[4,96,256]{2,1,0:T(8,128)(2,1)S(1)}, bf16[4,96,256]{2,1,0:T(8,128)(2,1)S(1)}, u32[]{:S(2)}, u32[]{:S(2)}) collective-permute-start(bf16[4,96,256]{2,1,0:T(8,128)(2,1)S(1)} %sent2c.1.after_ref), channel_id=1, source_target_pairs={{0,16},{8,24},{16,0},{24,8},{1,17},{9,25},{17,1},{25,9},{2,18},{10... | collective-permute-start | bytes 589832 | tf_op jit(solution)/shard_map/ppermute | solution.py:79
  31.3 0.3 kept2c.1.after_ref.refs_0_
  31.6 0.7 %lastb.1 = (bf16[2,96,256]{2,1,0:T(8,128)(2,1)S(1)}, bf16[2,96,256]{2,1,0:T(8,128)(2,1)S(1)}, bf16[2,96,256]{2,1,0:T(8,128)(2,1)S(1)}, bf16[2,96,256]{2,1,0:T(8,128)(2,1)S(1)}) custom-call(s32[8,8,128]{2,1,0:T(8,128)S(1)} %get-tuple-element.48.slots_ref, bf16[8,512,256]{2,1,0:T(8,128)(2,1)S(1)} %get-tuple-element.49.after_ref.joint_ref, ...), custom_call_target="tpu_custom_call" | custom-call | flops 100000000 | tf_op jit(solution)/shard_map/lastb/pallas_call | solution.py:113
  32.3 1.0 %collective-permute-start.16 = (bf16[2,96,256]{2,1,0:T(8,128)(2,1)S(1)}, bf16[2,96,256]{2,1,0:T(8,128)(2,1)S(1)}, u32[]{:S(2)}, u32[]{:S(2)}) collective-permute-start(bf16[2,96,256]{2,1,0:T(8,128)(2,1)S(1)} %get-tuple-element.66), channel_id=1, source_target_pairs={{0,2},{1,3},{2,0},{3,1},{4,6},{5,7},{6,4},{7,5},{8,10},{9,11},{10,... | collective-permute-start | bytes 294920 | tf_op jit(solution)/shard_map/ppermute | solution.py:79
  33.3 3.5 %collective-permute-start.17 = (bf16[2,96,256]{2,1,0:T(8,128)(2,1)S(1)}, bf16[2,96,256]{2,1,0:T(8,128)(2,1)S(1)}, u32[]{:S(2)}, u32[]{:S(2)}) collective-permute-start(bf16[2,96,256]{2,1,0:T(8,128)(2,1)S(1)} %get-tuple-element.67), channel_id=1, source_target_pairs={{0,4},{1,5},{2,6},{3,7},{4,0},{5,1},{6,2},{7,3},{8,12},{9,13},{10,... | collective-permute-start | bytes 294920 | tf_op jit(solution)/shard_map/ppermute | solution.py:79
  36.8 0.5 farc.1
  37.4 0.5 nearc.1
  37.9 1.3 %collective-permute-start.20 = (bf16[2,96,256]{2,1,0:T(8,128)(2,1)S(1)}, bf16[2,96,256]{2,1,0:T(8,128)(2,1)S(1)}, u32[]{:S(2)}, u32[]{:S(2)}) collective-permute-start(bf16[2,96,256]{2,1,0:T(8,128)(2,1)S(1)} %get-tuple-element.69), channel_id=1, source_target_pairs={{0,2},{1,3},{2,0},{3,1},{4,6},{5,7},{6,4},{7,5},{8,10},{9,11},{10,... | collective-permute-start | bytes 294920 | tf_op jit(solution)/shard_map/ppermute | solution.py:79
  39.2 3.2 %collective-permute-start.22 = (bf16[2,96,256]{2,1,0:T(8,128)(2,1)S(1)}, bf16[2,96,256]{2,1,0:T(8,128)(2,1)S(1)}, u32[]{:S(2)}, u32[]{:S(2)}) collective-permute-start(bf16[2,96,256]{2,1,0:T(8,128)(2,1)S(1)} %get-tuple-element.65.refs_4_), channel_id=1, source_target_pairs={{0,4},{1,5},{2,6},{3,7},{4,0},{5,1},{6,2},{7,3},{8,12},{9,13},{10,... | collective-permute-start | bytes 294920 | tf_op jit(solution)/shard_map/ppermute | solution.py:79
  42.4 0.3 collective-permute-start.23
  42.7 0.7 %collective-permute-done.18.refs_3_.refs_8_ = bf16[2,96,256]{2,1,0:T(8,128)(2,1)S(1)} collective-permute-done((bf16[2,96,256]{2,1,0:T(8,128)(2,1)S(1)}, bf16[2,96,256]{2,1,0:T(8,128)(2,1)S(1)}, u32[]{:S(2)}, u32[]{:S(2)}) %collective-permute-start.18) | collective-permute-done | bytes 98336 | tf_op jit(solution)/shard_map/ppermute | solution.py:79
  43.4 2.6 %collective-permute-done.20.refs_1_.refs_11_ = bf16[2,96,256]{2,1,0:T(8,128)(2,1)S(1)} collective-permute-done((bf16[2,96,256]{2,1,0:T(8,128)(2,1)S(1)}, bf16[2,96,256]{2,1,0:T(8,128)(2,1)S(1)}, u32[]{:S(2)}, u32[]{:S(2)}) %collective-permute-start.20) | collective-permute-done | bytes 98336 | tf_op jit(solution)/shard_map/ppermute | solution.py:79
  46.1 1.3 %collective-permute-done.21.refs_12_ = bf16[2,96,256]{2,1,0:T(8,128)(2,1)S(1)} collective-permute-done((bf16[2,96,256]{2,1,0:T(8,128)(2,1)S(1)}, bf16[2,96,256]{2,1,0:T(8,128)(2,1)S(1)}, u32[]{:S(2)}, u32[]{:S(2)}) %collective-permute-start.21) | collective-permute-done | bytes 98336 | tf_op jit(solution)/shard_map/ppermute | solution.py:79
  47.4 1.4 %place.1 = (bf16[2048,256]{1,0:T(8,128)(2,1)}, bf16[4,256,256]{2,1,0:T(8,128)(2,1)S(1)}) custom-call(bf16[2,64,256]{2,1,0:T(8,128)(2,1)S(1)} %get-tuple-element.55.after_ref.refs_1_.refs_0_, bf16[2,64,256]{2,1,0:T(8,128)(2,1)S(1)} %collective-permute-done.8.refs_2_.refs_1_, bf16[2,64,256]{2,1,0:T(8,128)(2,1)S(1)} %collective-permute-done.9.refs_3_.refs_2_, ...), custom_call_target="tpu_custom_call" | custom-call | flops 10000000000 | tf_op jit(solution)/shard_map/place/pallas_call | solution.py:113
  48.8 0.8 %collective-permute-done.23.refs_1_ = bf16[2,96,256]{2,1,0:T(8,128)(2,1)S(1)} collective-permute-done((bf16[2,96,256]{2,1,0:T(8,128)(2,1)S(1)}, bf16[2,96,256]{2,1,0:T(8,128)(2,1)S(1)}, u32[]{:S(2)}, u32[]{:S(2)}) %collective-permute-start.23) | collective-permute-done | bytes 98336 | tf_op jit(solution)/shard_map/ppermute | solution.py:79
  49.6 0.5 %collective-permute-done.22.refs_0_ = bf16[2,96,256]{2,1,0:T(8,128)(2,1)S(1)} collective-permute-done((bf16[2,96,256]{2,1,0:T(8,128)(2,1)S(1)}, bf16[2,96,256]{2,1,0:T(8,128)(2,1)S(1)}, u32[]{:S(2)}, u32[]{:S(2)}) %collective-permute-start.22) | collective-permute-done | bytes 98336 | tf_op jit(solution)/shard_map/ppermute | solution.py:79
  50.2 1.0 %finish.1 = bf16[2048,256]{1,0:T(8,128)(2,1)} custom-call(bf16[2048,256]{1,0:T(8,128)(2,1)} %get-tuple-element.70.first_ref, bf16[4,256,256]{2,1,0:T(8,128)(2,1)S(1)} %get-tuple-element.71.held_ref, bf16[2,96,256]{2,1,0:T(8,128)(2,1)S(1)} %collective-permute-done.22.refs_0_, ...), custom_call_target="tpu_custom_call", output_to_operand_aliasing={{}: (0, {})} | custom-call | flops 2000000000 | tf_op jit(solution)/shard_map/finish/pallas_call | solution.py:113
  (39 shorter events, 0.5 us)
Async XLA Ops:
  1.9 2.2 %collective-permute-start.1 = (bf16[4,64,256]{2,1,0:T(8,128)(2,1)S(1)}, bf16[4,64,256]{2,1,0:T(8,128)(2,1)S(1)}, u32[]{:S(2)}, u32[]{:S(2)}) collective-permute-start(bf16[4,64,256]{2,1,0:T(8,128)(2,1)S(1)} %get-tuple-element.42), channel_id=1, source_target_pairs={{0,1},{1,0},{2,3},{3,2},{4,5},{5,4},{6,7},{7,6},{8,9},{9,8},{10,11... | collective-permute-start | bytes 393224 | tf_op jit(solution)/shard_map/ppermute | solution.py:79
  2.5 5.3 %collective-permute-start = (bf16[4,192,256]{2,1,0:T(8,128)(2,1)S(1)}, bf16[4,192,256]{2,1,0:T(8,128)(2,1)S(1)}, u32[]{:S(2)}, u32[]{:S(2)}) collective-permute-start(bf16[4,192,256]{2,1,0:T(8,128)(2,1)S(1)} %get-tuple-element.40), channel_id=1, source_target_pairs={{0,1},{1,0},{2,3},{3,2},{4,5},{5,4},{6,7},{7,6},{8,9},{9,8},{10,11... | collective-permute-start | bytes 1179656 | tf_op jit(solution)/shard_map/ppermute | solution.py:79
  4.4 7.2 %collective-permute-start.2 = (bf16[4,64,256]{2,1,0:T(8,128)(2,1)S(1)}, bf16[4,64,256]{2,1,0:T(8,128)(2,1)S(1)}, u32[]{:S(2)}, u32[]{:S(2)}) collective-permute-start(bf16[4,64,256]{2,1,0:T(8,128)(2,1)S(1)} %sent0a.1.after_ref), channel_id=1, source_target_pairs={{0,2},{1,3},{2,0},{3,1},{4,6},{5,7},{6,4},{7,5},{8,10},{9,11},{10,... | collective-permute-start | bytes 393224 | tf_op jit(solution)/shard_map/ppermute | solution.py:79
  7.8 3.8 %slice-start = ((s8[8388608]{0:T(1024)(128)(4,1)}), s8[4194304]{0:T(1024)(128)(4,1)S(1)}, s32[]{:S(2)}) async-start(s8[8388608]{0:T(1024)(128)(4,1)} %bitcast), calls=%async_computation | async-start | bytes 8388608
  8.3 7.7 %collective-permute-start.4 = (bf16[4,96,256]{2,1,0:T(8,128)(2,1)S(1)}, bf16[4,96,256]{2,1,0:T(8,128)(2,1)S(1)}, u32[]{:S(2)}, u32[]{:S(2)}) collective-permute-start(bf16[4,96,256]{2,1,0:T(8,128)(2,1)S(1)} %get-tuple-element.45), channel_id=1, source_target_pairs={{0,2},{1,3},{2,0},{3,1},{4,6},{5,7},{6,4},{7,5},{8,10},{9,11},{10,... | collective-permute-start | bytes 589832 | tf_op jit(solution)/shard_map/ppermute | solution.py:79
  8.4 1.5 %copy-start = (bf16[1,1,8,256,256]{4,3,2,1,0:T(8,128)(2,1)S(1)}, bf16[1,1,8,256,256]{4,3,2,1,0:T(8,128)(2,1)}, u32[]{:S(2)}) copy-start(bf16[1,1,8,256,256]{4,3,2,1,0:T(8,128)(2,1)} %core_ref.1) | copy-start | bytes 3145732
  8.4 1.8 %copy-start.1 = (bf16[2048,256]{1,0:T(8,128)(2,1)S(1)}, bf16[2048,256]{1,0:T(8,128)(2,1)}, u32[]{:S(2)}) copy-start(bf16[2048,256]{1,0:T(8,128)(2,1)} %u_ref.1) | copy-start | bytes 3145732
  8.4 3.5 %slice-start.1 = ((s8[8388608]{0:T(1024)(128)(4,1)}), s8[4194304]{0:T(1024)(128)(4,1)S(1)}, s32[]{:S(2)}) async-start(s8[8388608]{0:T(1024)(128)(4,1)} %bitcast), calls=%async_computation.1 | async-start | bytes 8388608
  12.2 6.0 %collective-permute-start.3 = (bf16[4,64,256]{2,1,0:T(8,128)(2,1)S(1)}, bf16[4,64,256]{2,1,0:T(8,128)(2,1)S(1)}, u32[]{:S(2)}, u32[]{:S(2)}) collective-permute-start(bf16[4,64,256]{2,1,0:T(8,128)(2,1)S(1)} %sent1a.1.after_ref), channel_id=1, source_target_pairs={{0,8},{8,0},{16,24},{24,16},{1,9},{9,1},{17,25},{25,17},{2,10},{10... | collective-permute-start | bytes 393224 | tf_op jit(solution)/shard_map/ppermute | solution.py:79
  14.0 7.6 %collective-permute-start.6 = (bf16[4,96,256]{2,1,0:T(8,128)(2,1)S(1)}, bf16[4,96,256]{2,1,0:T(8,128)(2,1)S(1)}, u32[]{:S(2)}, u32[]{:S(2)}) collective-permute-start(bf16[4,96,256]{2,1,0:T(8,128)(2,1)S(1)} %get-tuple-element.51), channel_id=1, source_target_pairs={{0,2},{1,3},{2,0},{3,1},{4,6},{5,7},{6,4},{7,5},{8,10},{9,11},{10,... | collective-permute-start | bytes 589832 | tf_op jit(solution)/shard_map/ppermute | solution.py:79
  16.6 6.4 %collective-permute-start.5 = (bf16[4,96,256]{2,1,0:T(8,128)(2,1)S(1)}, bf16[4,96,256]{2,1,0:T(8,128)(2,1)S(1)}, u32[]{:S(2)}, u32[]{:S(2)}) collective-permute-start(bf16[4,96,256]{2,1,0:T(8,128)(2,1)S(1)} %get-tuple-element.50), channel_id=1, source_target_pairs={{0,8},{8,0},{16,24},{24,16},{1,9},{9,1},{17,25},{25,17},{2,10},{10... | collective-permute-start | bytes 589832 | tf_op jit(solution)/shard_map/ppermute | solution.py:79
  18.3 2.1 %copy-start.2 = (s32[1,1,8]{2,1,0:T(1,128)S(1)}, s32[1,1,8]{2,1,0:T(1,128)}, u32[]{:S(2)}) copy-start(s32[1,1,8]{2,1,0:T(1,128)} %order_ref.1) | copy-start | bytes 100
  18.8 6.1 %collective-permute-start.7 = (bf16[4,64,256]{2,1,0:T(8,128)(2,1)S(1)}, bf16[4,64,256]{2,1,0:T(8,128)(2,1)S(1)}, u32[]{:S(2)}, u32[]{:S(2)}) collective-permute-start(bf16[4,64,256]{2,1,0:T(8,128)(2,1)S(1)} %get-tuple-element.54), channel_id=1, source_target_pairs={{0,16},{8,24},{16,0},{24,8},{1,17},{9,25},{17,1},{25,9},{2,18},{10... | collective-permute-start | bytes 393224 | tf_op jit(solution)/shard_map/ppermute | solution.py:79
  22.1 7.8 %collective-permute-start.11 = (bf16[4,96,256]{2,1,0:T(8,128)(2,1)S(1)}, bf16[4,96,256]{2,1,0:T(8,128)(2,1)S(1)}, u32[]{:S(2)}, u32[]{:S(2)}) collective-permute-start(bf16[4,96,256]{2,1,0:T(8,128)(2,1)S(1)} %get-tuple-element.59), channel_id=1, source_target_pairs={{0,8},{8,0},{16,24},{24,16},{1,9},{9,1},{17,25},{25,17},{2,10},{10... | collective-permute-start | bytes 589832 | tf_op jit(solution)/shard_map/ppermute | solution.py:79
  23.4 8.2 %collective-permute-start.12 = (bf16[4,96,256]{2,1,0:T(8,128)(2,1)S(1)}, bf16[4,96,256]{2,1,0:T(8,128)(2,1)S(1)}, u32[]{:S(2)}, u32[]{:S(2)}) collective-permute-start(bf16[4,96,256]{2,1,0:T(8,128)(2,1)S(1)} %get-tuple-element.60), channel_id=1, source_target_pairs={{0,16},{8,24},{16,0},{24,8},{1,17},{9,25},{17,1},{25,9},{2,18},{10... | collective-permute-start | bytes 589832 | tf_op jit(solution)/shard_map/ppermute | solution.py:79
  25.5 7.8 %collective-permute-start.8 = (bf16[2,64,256]{2,1,0:T(8,128)(2,1)S(1)}, bf16[2,64,256]{2,1,0:T(8,128)(2,1)S(1)}, u32[]{:S(2)}, u32[]{:S(2)}) collective-permute-start(bf16[2,64,256]{2,1,0:T(8,128)(2,1)S(1)} %get-tuple-element.56), channel_id=1, source_target_pairs={{0,2},{1,3},{2,0},{3,1},{4,6},{5,7},{6,4},{7,5},{8,10},{9,11},{10,... | collective-permute-start | bytes 196616 | tf_op jit(solution)/shard_map/ppermute | solution.py:79
  26.9 9.9 %collective-permute-start.9 = (bf16[2,64,256]{2,1,0:T(8,128)(2,1)S(1)}, bf16[2,64,256]{2,1,0:T(8,128)(2,1)S(1)}, u32[]{:S(2)}, u32[]{:S(2)}) collective-permute-start(bf16[2,64,256]{2,1,0:T(8,128)(2,1)S(1)} %get-tuple-element.57), channel_id=1, source_target_pairs={{0,4},{1,5},{2,6},{3,7},{4,0},{5,1},{6,2},{7,3},{8,12},{9,13},{10,... | collective-permute-start | bytes 196616 | tf_op jit(solution)/shard_map/ppermute | solution.py:79
  29.5 7.3 %collective-permute-start.10 = (bf16[2,64,256]{2,1,0:T(8,128)(2,1)S(1)}, bf16[2,64,256]{2,1,0:T(8,128)(2,1)S(1)}, u32[]{:S(2)}, u32[]{:S(2)}) collective-permute-start(bf16[2,64,256]{2,1,0:T(8,128)(2,1)S(1)} %get-tuple-element.58), channel_id=1, source_target_pairs={{0,6},{1,7},{2,4},{3,5},{4,2},{5,3},{6,0},{7,1},{8,14},{9,15},{10,... | collective-permute-start | bytes 196616 | tf_op jit(solution)/shard_map/ppermute | solution.py:79
  30.3 6.5 %collective-permute-start.13 = (bf16[4,96,256]{2,1,0:T(8,128)(2,1)S(1)}, bf16[4,96,256]{2,1,0:T(8,128)(2,1)S(1)}, u32[]{:S(2)}, u32[]{:S(2)}) collective-permute-start(bf16[4,96,256]{2,1,0:T(8,128)(2,1)S(1)} %sent2c.1.after_ref), channel_id=1, source_target_pairs={{0,16},{8,24},{16,0},{24,8},{1,17},{9,25},{17,1},{25,9},{2,18},{10... | collective-permute-start | bytes 589832 | tf_op jit(solution)/shard_map/ppermute | solution.py:79
  32.3 10.1 %collective-permute-start.16 = (bf16[2,96,256]{2,1,0:T(8,128)(2,1)S(1)}, bf16[2,96,256]{2,1,0:T(8,128)(2,1)S(1)}, u32[]{:S(2)}, u32[]{:S(2)}) collective-permute-start(bf16[2,96,256]{2,1,0:T(8,128)(2,1)S(1)} %get-tuple-element.66), channel_id=1, source_target_pairs={{0,2},{1,3},{2,0},{3,1},{4,6},{5,7},{6,4},{7,5},{8,10},{9,11},{10,... | collective-permute-start | bytes 294920 | tf_op jit(solution)/shard_map/ppermute | solution.py:79
  33.3 9.4 %collective-permute-start.17 = (bf16[2,96,256]{2,1,0:T(8,128)(2,1)S(1)}, bf16[2,96,256]{2,1,0:T(8,128)(2,1)S(1)}, u32[]{:S(2)}, u32[]{:S(2)}) collective-permute-start(bf16[2,96,256]{2,1,0:T(8,128)(2,1)S(1)} %get-tuple-element.67), channel_id=1, source_target_pairs={{0,4},{1,5},{2,6},{3,7},{4,0},{5,1},{6,2},{7,3},{8,12},{9,13},{10,... | collective-permute-start | bytes 294920 | tf_op jit(solution)/shard_map/ppermute | solution.py:79
  36.8 6.6 %collective-permute-start.18 = (bf16[2,96,256]{2,1,0:T(8,128)(2,1)S(1)}, bf16[2,96,256]{2,1,0:T(8,128)(2,1)S(1)}, u32[]{:S(2)}, u32[]{:S(2)}) collective-permute-start(bf16[2,96,256]{2,1,0:T(8,128)(2,1)S(1)} %get-tuple-element.68), channel_id=1, source_target_pairs={{0,6},{1,7},{2,4},{3,5},{4,2},{5,3},{6,0},{7,1},{8,14},{9,15},{10,... | collective-permute-start | bytes 294920 | tf_op jit(solution)/shard_map/ppermute | solution.py:79
  37.3 1.9 %collective-permute-start.14 = (bf16[2,96,256]{2,1,0:T(8,128)(2,1)S(1)}, bf16[2,96,256]{2,1,0:T(8,128)(2,1)S(1)}, u32[]{:S(2)}, u32[]{:S(2)}) collective-permute-start(bf16[2,96,256]{2,1,0:T(8,128)(2,1)S(1)} %get-tuple-element.63), channel_id=1, source_target_pairs={{0,1},{1,0},{2,3},{3,2},{4,5},{5,4},{6,7},{7,6},{8,9},{9,8},{10,11... | collective-permute-start | bytes 294920 | tf_op jit(solution)/shard_map/ppermute | solution.py:79
  37.9 8.1 %collective-permute-start.20 = (bf16[2,96,256]{2,1,0:T(8,128)(2,1)S(1)}, bf16[2,96,256]{2,1,0:T(8,128)(2,1)S(1)}, u32[]{:S(2)}, u32[]{:S(2)}) collective-permute-start(bf16[2,96,256]{2,1,0:T(8,128)(2,1)S(1)} %get-tuple-element.69), channel_id=1, source_target_pairs={{0,2},{1,3},{2,0},{3,1},{4,6},{5,7},{6,4},{7,5},{8,10},{9,11},{10,... | collective-permute-start | bytes 294920 | tf_op jit(solution)/shard_map/ppermute | solution.py:79
  39.2 11.0 %collective-permute-start.22 = (bf16[2,96,256]{2,1,0:T(8,128)(2,1)S(1)}, bf16[2,96,256]{2,1,0:T(8,128)(2,1)S(1)}, u32[]{:S(2)}, u32[]{:S(2)}) collective-permute-start(bf16[2,96,256]{2,1,0:T(8,128)(2,1)S(1)} %get-tuple-element.65.refs_4_), channel_id=1, source_target_pairs={{0,4},{1,5},{2,6},{3,7},{4,0},{5,1},{6,2},{7,3},{8,12},{9,13},{10,... | collective-permute-start | bytes 294920 | tf_op jit(solution)/shard_map/ppermute | solution.py:79
  42.4 7.2 %collective-permute-start.23 = (bf16[2,96,256]{2,1,0:T(8,128)(2,1)S(1)}, bf16[2,96,256]{2,1,0:T(8,128)(2,1)S(1)}, u32[]{:S(2)}, u32[]{:S(2)}) collective-permute-start(bf16[2,96,256]{2,1,0:T(8,128)(2,1)S(1)} %get-tuple-element.72), channel_id=1, source_target_pairs={{0,6},{1,7},{2,4},{3,5},{4,2},{5,3},{6,0},{7,1},{8,14},{9,15},{10,... | collective-permute-start | bytes 294920 | tf_op jit(solution)/shard_map/ppermute | solution.py:79
  42.7 3.4 %collective-permute-start.15 = (bf16[4,64,256]{2,1,0:T(8,128)(2,1)S(1)}, bf16[4,64,256]{2,1,0:T(8,128)(2,1)S(1)}, u32[]{:S(2)}, u32[]{:S(2)}) collective-permute-start(bf16[4,64,256]{2,1,0:T(8,128)(2,1)S(1)} %packa.1.refs_4_), channel_id=1, source_target_pairs={{0,1},{1,0},{2,3},{3,2},{4,5},{5,4},{6,7},{7,6},{8,9},{9,8},{10,11... | collective-permute-start | bytes 393224 | tf_op jit(solution)/shard_map/ppermute | solution.py:79
  43.3 4.0 %collective-permute-start.19 = (bf16[4,96,256]{2,1,0:T(8,128)(2,1)S(1)}, bf16[4,96,256]{2,1,0:T(8,128)(2,1)S(1)}, u32[]{:S(2)}, u32[]{:S(2)}) collective-permute-start(bf16[4,96,256]{2,1,0:T(8,128)(2,1)S(1)} %packb.1.refs_2_), channel_id=1, source_target_pairs={{0,1},{1,0},{2,3},{3,2},{4,5},{5,4},{6,7},{7,6},{8,9},{9,8},{10,11... | collective-permute-start | bytes 589832 | tf_op jit(solution)/shard_map/ppermute | solution.py:79
  46.0 1.4 %collective-permute-start.21 = (bf16[2,96,256]{2,1,0:T(8,128)(2,1)S(1)}, bf16[2,96,256]{2,1,0:T(8,128)(2,1)S(1)}, u32[]{:S(2)}, u32[]{:S(2)}) collective-permute-start(bf16[2,96,256]{2,1,0:T(8,128)(2,1)S(1)} %packc.1.refs_0_), channel_id=1, source_target_pairs={{0,1},{1,0},{2,3},{3,2},{4,5},{5,4},{6,7},{7,6},{8,9},{9,8},{10,11... | collective-permute-start | bytes 294920 | tf_op jit(solution)/shard_map/ppermute | solution.py:79
